TPU v7x, 256 devices: a whole 4x4x8 slice. The times are simulated.
256 devices in a mesh: pi: 16 (over x, z_hi, core), pj: 16 (over y, z_lo).
Axes of the slice: x: 4, y: 4, z: 8 (z_hi: 2, z_lo: 4; z = z_hi * 4 + z_lo), core: 2. Of those that a mesh axis runs over, the one named last changes fastest.
Arguments:
- amplitudes: bfloat16 [32, 48, 8, 4096], P('pi', 'pj'), may hold values from -6 to 6
- coulomb: bfloat16 [48, 48, 8, 4096], P('pi', 'pj'), may hold values from -0.046875 to 0.046875
- exchange: bfloat16 [48, 48, 8, 4096], P('pi', 'pj'), may hold values from -0.046875 to 0.046875
- occ_irrep: int32 [48], replicated, may hold values from 0 to 7
Outputs:
- residual: bfloat16 [32, 48, 8, 4096], P('pi', 'pj')
Inputs may be any that keep to these rules, and one draw needn't show every extreme that they name: `occ_irrep`: the virtual orbitals hold 64 of each of the 8 irreps and are stored irrep by irrep.
All inputs are finite; a program needn't handle non-finite values.
Results may differ from a plain program's by a relative error of at most 0.0058.
Values may be sent and summed in bfloat16 or wider, within the bound.
No kernel may reach another device: no remote copies, remote signals or barrier semaphores. Data moves between devices by JAX's collectives and lax.ppermute only.
A program may use at most 384 MiB of HBM per device.

v0:
```python
import jax
import jax.numpy as jnp
from jax import lax
from jax.sharding import PartitionSpec as P

NVI = 64


def on_device(amplitudes, coulomb, exchange, occ_irrep):
    rows_here = amplitudes.shape[0]
    cols_here = coulomb.shape[1]
    blocks = jnp.arange(8, dtype=jnp.int32)
    gathered = lax.all_gather(amplitudes, "pj", axis=1, tiled=True)
    occupied = gathered.shape[1]
    label_i = lax.dynamic_slice_in_dim(occ_irrep, lax.axis_index("pi") * rows_here, rows_here)
    label_j = lax.dynamic_slice_in_dim(occ_irrep, lax.axis_index("pj") * cols_here, cols_here)
    pair_ik = jnp.bitwise_xor(label_i[:, None], occ_irrep[None, :])
    target_ik = jnp.bitwise_xor(blocks[None, None, :], pair_ik[:, :, None])
    picker_ik = (target_ik[:, :, :, None] == blocks[None, None, None, :]).astype(jnp.bfloat16)
    swapped = jnp.einsum(
        "ikhg,ikgx->ikhx", picker_ik, gathered, preferred_element_type=jnp.bfloat16
    )
    swapped = swapped.reshape(rows_here, occupied, 8, NVI, NVI)
    amp_blocks = gathered.reshape(rows_here, occupied, 8, NVI, NVI)
    doubled = (
        2.0 * amp_blocks.astype(jnp.float32) - jnp.swapaxes(swapped, 3, 4).astype(jnp.float32)
    ).astype(jnp.bfloat16)
    ladder_rows = (
        2.0 * lax.all_gather(coulomb, "pi", axis=0, tiled=True).astype(jnp.float32)
        - lax.all_gather(exchange, "pi", axis=0, tiled=True).astype(jnp.float32)
    ).astype(jnp.bfloat16)
    span = ladder_rows.shape[0]
    pair_kj = jnp.bitwise_xor(occ_irrep[:, None], label_j[None, :])
    target_kj = jnp.bitwise_xor(blocks[None, None, :], pair_kj[:, :, None])
    picker_kj = (target_kj[:, :, :, None] == blocks[None, None, None, :]).astype(jnp.bfloat16)
    direct_ladder = jnp.einsum(
        "ikhg,kjgx->ikjhx", picker_ik, ladder_rows, preferred_element_type=jnp.bfloat16
    )
    direct_ladder = direct_ladder.reshape(rows_here, span, cols_here, 8, NVI, NVI)
    cross_ladder = jnp.einsum(
        "kjhg,kjgx->kjhx", picker_kj, ladder_rows, preferred_element_type=jnp.bfloat16
    )
    cross_ladder = cross_ladder.reshape(span, cols_here, 8, NVI, NVI)
    cross_amp = jnp.einsum(
        "kjhg,ikgx->ikjhx", picker_kj, gathered, preferred_element_type=jnp.bfloat16
    )
    cross_amp = cross_amp.reshape(rows_here, span, cols_here, 8, NVI, NVI)
    direct = jnp.einsum(
        "ikhac,ikjhcb->ijhab", doubled, direct_ladder, preferred_element_type=jnp.float32
    )
    crossed = jnp.einsum(
        "kjhca,ikjhcb->ijhab", cross_ladder, cross_amp, preferred_element_type=jnp.float32
    )
    direct, crossed = (direct, crossed)
    result = (direct - crossed).astype(jnp.bfloat16)
    return result.reshape(rows_here, cols_here, 8, NVI * NVI)


def solution(mesh):
    placed = (P("pi", "pj", None, None), P("pi", "pj", None, None), P("pi", "pj", None, None), P())
    return jax.shard_map(
        on_device, mesh=mesh, in_specs=placed, out_specs=P("pi", "pj", None, None), check_vma=False
    )
```

profile of v0, /device:TPU:1, one launch (start us, length us, event | category | flops | bytes accessed | tf_op | source)
XLA Modules:
  0.0 551.1 jit_solution(6891773277035070051)
XLA Ops:
  6.5 0.0 all-gather.8.cloned.1.call-start
  6.5 0.7 all-gather.8.cloned.1.call-update
  7.3 0.0 all-gather.6.cloned.1.call-start
  7.3 0.7 all-gather.6.cloned.1.call-update
  8.0 0.0 all-gather.4.cloned.1.call-start
  8.1 0.7 all-gather.4.cloned.1.call-update
  8.7 0.7 dynamic_slice.7
  9.5 0.7 dynamic_slice.6
  10.2 0.7 broadcast_xor_fusion.1
  10.9 0.7 broadcast_xor_fusion
  11.7 0.1 iota_xor_fusion.1
  11.7 0.1 iota_xor_fusion
  11.9 144.7 %all-gather.8.cloned.1.call-done = bf16[2,48,8,4096]{3,2,1,0:T(8,128)(2,1)} async-done(((bf16[2,3,8,4096]{3,2,1,0:T(8,128)(2,1)}), bf16[2,48,8,4096]{3,2,1,0:T(8,128)(2,1)}) %all-gather.8.cloned.1.call-update) | async-done | bytes 6291472 | tf_op jit(solution)/shard_map/all_gather | solution.py:13
  156.5 11.8 %convolution_bitcast_fusion = bf16[2,48,3,8,4096]{4,3,0,2,1:T(8,128)(2,1)} fusion(s32[48,3,8]{2,1,0:T(4,128)S(1)} %iota_xor_fusion, bf16[2,48,8,4096]{3,2,1,0:T(8,128)(2,1)} %all-gather.8.cloned.1.call-done), kind=kOutput, calls=%fused_computation.11 | convolution fusion | flops 151004160 | bytes 25170432 | tf_op jit(solution)/shard_map/kjhg,ikgx->ikjhx/dot_general | solution.py:44
  168.3 50.9 %reshape.80 = bf16[2,48,3,8,64,64]{5,4,3,0,2,1:T(8,128)(2,1)} reshape(bf16[2,48,3,8,4096]{4,3,0,2,1:T(8,128)(2,1)} %convolution_bitcast_fusion) | data formatting | bytes 37748736 | tf_op jit(solution)/shard_map/reshape | solution.py:47
  219.2 9.1 %convolution_convert_fusion = f32[2,48,8,4096]{3,2,1,0:T(8,128)} fusion(bf16[2,48,8,4096]{3,2,1,0:T(8,128)(2,1)} %all-gather.8.cloned.1.call-done, s32[2,48,8]{2,1,0:T(8,128)S(1)} %iota_xor_fusion.1), kind=kOutput, calls=%fused_computation.13 | convolution fusion | flops 53483520 | bytes 18877440 | tf_op jit(solution)/shard_map/ikhg,ikgx->ikhx/dot_general | solution.py:20
  228.3 20.5 %reshape.83 = f32[2,48,8,64,64]{4,3,2,1,0:T(8,128)} reshape(f32[2,48,8,4096]{3,2,1,0:T(8,128)} %convolution_convert_fusion) | data formatting | bytes 25165824 | tf_op jit(solution)/shard_map/convert_element_type | solution.py:26
  248.8 24.8 %copy.23 = f32[2,48,8,64,64]{3,4,0,2,1:T(8,128)} copy(f32[2,48,8,64,64]{4,3,2,1,0:T(8,128)} %reshape.83) | data formatting | bytes 25165824 | tf_op jit(solution)/shard_map/convert_element_type | solution.py:26
  273.5 8.9 %convert_multiply_fusion = f32[2,48,8,4096]{3,2,1,0:T(8,128)} fusion(bf16[2,48,8,4096]{3,2,1,0:T(8,128)(2,1)} %all-gather.8.cloned.1.call-done), kind=kLoop, calls=%fused_computation.8 | loop fusion | flops 6291456 | bytes 18874368 | tf_op jit(solution)/shard_map/mul | solution.py:26
  282.5 20.5 %mul.26 = f32[2,48,8,64,64]{4,3,2,1,0:T(8,128)} reshape(f32[2,48,8,4096]{3,2,1,0:T(8,128)} %convert_multiply_fusion) | data formatting | bytes 25165824 | tf_op jit(solution)/shard_map/mul | solution.py:26
  303.0 0.0 all-gather.6.cloned.1.call-done
  303.0 84.0 %all-gather.4.cloned.1.call-done = bf16[48,3,8,4096]{3,2,1,0:T(8,128)(2,1)} async-done(((bf16[3,3,8,4096]{3,2,1,0:T(8,128)(2,1)}), bf16[48,3,8,4096]{3,2,1,0:T(8,128)(2,1)}) %all-gather.4.cloned.1.call-update) | async-done | bytes 9437200 | tf_op jit(solution)/shard_map/all_gather | solution.py:29
  387.0 10.4 %fusion.12 = bf16[48,3,8,4096]{3,2,1,0:T(8,128)(2,1)} fusion(bf16[48,3,8,4096]{3,2,1,0:T(8,128)(2,1)} %all-gather.6.cloned.1.call-done, bf16[48,3,8,4096]{3,2,1,0:T(8,128)(2,1)} %all-gather.4.cloned.1.call-done, s32[48,3,8]{2,1,0:T(4,128)S(1)} %iota_xor_fusion), kind=kOutput, calls=%fused_computation.15 | convolution fusion | flops 99099648 | bytes 28316160 | tf_op jit(solution)/shard_map/kjhg,kjgx->kjhx/dot_general | solution.py:40
  397.4 26.1 %reshape.81 = bf16[48,3,8,64,64]{4,3,2,1,0:T(8,128)(2,1)} reshape(bf16[48,3,8,4096]{3,2,1,0:T(8,128)(2,1)} %fusion.12) | data formatting | bytes 18874368 | tf_op jit(solution)/shard_map/reshape | solution.py:43
  423.5 16.4 %fusion.8 = bf16[2,48,3,8,4096]{4,3,0,2,1:T(8,128)(2,1)} fusion(bf16[48,3,8,4096]{3,2,1,0:T(8,128)(2,1)} %all-gather.6.cloned.1.call-done, bf16[48,3,8,4096]{3,2,1,0:T(8,128)(2,1)} %all-gather.4.cloned.1.call-done, s32[2,48,8]{2,1,0:T(8,128)S(1)} %iota_xor_fusion.1), kind=kOutput, calls=%fused_computation.12 | convolution fusion | flops 174594048 | bytes 37751808 | tf_op jit(solution)/shard_map/ikhg,kjgx->ikjhx/dot_general | solution.py:36
  439.9 50.8 %reshape.79 = bf16[2,48,3,8,64,64]{5,4,3,0,2,1:T(8,128)(2,1)} reshape(bf16[2,48,3,8,4096]{4,3,0,2,1:T(8,128)(2,1)} %fusion.8) | data formatting | bytes 37748736 | tf_op jit(solution)/shard_map/reshape | solution.py:39
  490.7 21.3 %fusion.1 = f32[3,8,2,64,64,1]{4,3,1,2,0,5:T(8,128)} fusion(bf16[2,48,3,8,64,64]{5,4,3,0,2,1:T(8,128)(2,1)} %reshape.80, bf16[48,3,8,64,64]{4,3,2,1,0:T(8,128)(2,1)} %reshape.81), kind=kOutput, calls=%fused_computation.2 | convolution fusion | flops 1207959552 | bytes 29097984 | tf_op jit(solution)/shard_map/kjhca,ikjhcb->ijhab/dot_general | solution.py:51
  512.0 29.2 %fusion.4 = f32[2,8,3,64,64,1]{4,3,1,0,2,5:T(8,128)S(1)} fusion(bf16[2,48,3,8,64,64]{5,4,3,0,2,1:T(8,128)(2,1)} %reshape.79, f32[2,48,8,64,64]{3,4,0,2,1:T(8,128)} %copy.23, f32[2,48,8,64,64]{4,3,2,1,0:T(8,128)} %mul.26), kind=kOutput, calls=%fused_computation.6 | convolution fusion | flops 1214251008 | bytes 44826624 | tf_op jit(solution)/shard_map/ikhac,ikjhcb->ijhab/dot_general | solution.py:48
  541.1 1.7 fusion.13
  542.8 0.4 copy.29
  543.2 1.4 reshape.82
Async XLA Ops:
  6.5 150.0 %all-gather.8.cloned.1.call-start = ((), (), s32[]{:S(2)}) async-start(), calls=%async_computation.2 | async-start | bytes 6684672 | tf_op jit(solution)/shard_map/all_gather | solution.py:13
  7.3 295.8 %all-gather.6.cloned.1.call-start = ((), (), s32[]{:S(2)}) async-start(), calls=%async_computation.1 | async-start | bytes 10027008 | tf_op jit(solution)/shard_map/all_gather | solution.py:30
  8.0 379.0 %all-gather.4.cloned.1.call-start = ((), (), s32[]{:S(2)}) async-start(), calls=%async_computation | async-start | bytes 10027008 | tf_op jit(solution)/shard_map/all_gather | solution.py:29
Sparse Core Ops, SparseCore 0:
  9.1 147.3 all-gather.7
  159.2 114.3 all-gather.5
  276.3 110.6 all-gather.3
where the time goes:
time: 556 us; the launch traced here: 551 us
  waiting for transfers between devices  231 us (42%)
  local copies, waits for them, and re-layouts  197 us (35%)
  matrix products  98.1 us (18%)
  between operations  13.1 us (2%)
  other arithmetic  12.3 us (2%)
    all_gather x1, waiting for transfers between devices, on_device(): gathered = lax.all_gather(amplitudes, 'pj', axis=1, tiled=True)  145 us
    all_gather x1, waiting for transfers between devices, on_device(): lax.all_gather(coulomb, 'pi', axis=0, tiled=True).astype(jnp.float32)  84 us
    reshape x1, local copies, waits for them, and re-layouts, on_device(): cross_amp = cross_amp.reshape(rows_here, span, cols_here, 8, NVI, NVI)  50.9 us
    reshape x1, local copies, waits for them, and re-layouts, on_device(): direct_ladder.reshape(rows_here, span, cols_here, 8, NVI, NVI)  50.8 us
    convert_element_type x2, local copies, waits for them, and re-layouts, on_device(): jnp.swapaxes(swapped, 3, 4).astype(jnp.float32)  45.2 us
    dot_general x1, matrix products, on_device(): jnp.einsum('ikhac,ikjhcb->ijhab', doubled, direct_ladder, preferred_eleme...  29.2 us
    reshape x1, local copies, waits for them, and re-layouts, on_device(): cross_ladder = cross_ladder.reshape(span, cols_here, 8, NVI, NVI)  26.1 us
    dot_general x1, matrix products, on_device(): jnp.einsum('kjhca,ikjhcb->ijhab', cross_ladder, cross_amp, preferred_elem...  21.3 us
  transfers between devices with their start and end apart: 3, of which 2 were waited for; matrix products, arithmetic and copies ran while one was open for 27% of the time, Pallas kernels for 0%

commit v1 on v0

v1 whole, which is shorter than its diff:
```python
import jax
import jax.numpy as jnp
from jax import lax
from jax.experimental import pallas as pl
from jax.experimental.pallas import tpu as pltpu
from jax.sharding import PartitionSpec as P

NVI = 64
MESH_X, MESH_Y, MESH_ZH, MESH_ZL = 4, 4, 2, 4
CHUNKS = 16


def perm_pi(move):
    pairs = []
    for x in range(MESH_X):
        for zh in range(MESH_ZH):
            for c in range(2):
                x2, zh2, c2 = move(x, zh, c)
                pairs.append((x * 4 + zh * 2 + c, (x2 % 4) * 4 + zh2 * 2 + c2))
    return pairs


def perm_pj(move):
    pairs = []
    for y in range(MESH_Y):
        for zl in range(MESH_ZL):
            y2, zl2 = move(y, zl)
            pairs.append((y * 4 + zl, (y2 % 4) * 4 + zl2))
    return pairs


def shift_y(d):
    return perm_pj(lambda y, zl: (y + d, zl))


def shift_x(d):
    return perm_pi(lambda x, zh, c: (x + d, zh, c))


def swap_zl(d):
    return perm_pj(lambda y, zl: (y, zl ^ d))


SWAP_ZH = perm_pi(lambda x, zh, c: (x, zh ^ 1, c))
SWAP_CORE = perm_pi(lambda x, zh, c: (x, zh, c ^ 1))


def spread(half):
    row = lax.broadcasted_iota(jnp.int32, (512, 256), 0)
    col = lax.broadcasted_iota(jnp.int32, (512, 256), 1)
    want = ((row & 63) >> 1) * 8 + (row >> 6)
    return jnp.where((col == want) & ((row & 1) == half), 1.0, 0.0).astype(jnp.bfloat16)


def gather_back(half):
    row = lax.broadcasted_iota(jnp.int32, (256, 512), 0)
    col = lax.broadcasted_iota(jnp.int32, (256, 512), 1)
    want = ((col & 63) >> 1) * 8 + (col >> 6)
    return jnp.where((row == want) & ((col & 1) == half), 1.0, 0.0).astype(jnp.bfloat16)


def stacked(flat):
    return jnp.concatenate([flat[:, v * 128 : (v + 1) * 128] for v in range(32)], axis=0)


def amp_prep(labels, amp_ref, out_ref):
    base = lax.axis_index("pj") * 3
    picks = [spread(0), spread(1)]
    for k in range(3):
        label = labels[base + k]
        rows = [stacked(amp_ref[i, k].astype(jnp.float32)).astype(jnp.bfloat16) for i in range(2)]
        block = jnp.zeros((512, 128), jnp.float32)
        for p in range(2):
            side = jnp.concatenate([r[:, p * 64 : p * 64 + 64] for r in rows], axis=1)
            block += jnp.dot(picks[p], side, preferred_element_type=jnp.float32)
        block = block.astype(jnp.bfloat16)
        for h in range(8):
            out_ref[h ^ label, k] = block[h * 64 : h * 64 + 64]


def ladder_prep(labels, coul_ref, exch_ref, out_ref):
    base = lax.axis_index("pi") * 3
    picks = [spread(0), spread(1)]
    for k in range(3):
        label = labels[base + k]
        rows = []
        for j in range(3):
            ladder = 2.0 * coul_ref[k, j].astype(jnp.float32) - exch_ref[k, j].astype(jnp.float32)
            rows.append(stacked(ladder).astype(jnp.bfloat16))
        block = jnp.zeros((512, 192), jnp.float32)
        for p in range(2):
            side = jnp.concatenate([r[:, p * 64 : p * 64 + 64] for r in rows], axis=1)
            block += jnp.dot(picks[p], side, preferred_element_type=jnp.float32)
        for h in range(8):
            part = block[h * 64 : h * 64 + 64]
            out_ref[h ^ label, k, 0:64] = part[:, 0:128].astype(jnp.bfloat16)
            third = jnp.concatenate([part[0:32, 128:192], part[32:64, 128:192]], axis=1)
            out_ref[h ^ label, k, 64:96] = third.astype(jnp.bfloat16)


def contract(labels, *refs):
    amp_in, lad_in = refs[:CHUNKS], refs[CHUNKS : 2 * CHUNKS]
    out_ref, amp, lad, diff, cross, sems = refs[2 * CHUNKS :]
    pi, pj = lax.axis_index("pi"), lax.axis_index("pj")
    x, zh, core = pi // 4, (pi // 2) % 2, pi % 2
    y, zl = pj // 4, pj % 4
    copies = []
    for n, (s, d) in enumerate(AMP_KEYS):
        slot = ((y + 4 - s) % 4) * 4 + (zl ^ d)
        copies.append(pltpu.make_async_copy(amp_in[n], amp.at[slot], sems.at[n]))
    for n, (s, d, c) in enumerate(LAD_KEYS):
        slot = ((x + 4 - s) % 4) * 4 + (zh ^ d) * 2 + (core ^ c)
        copies.append(pltpu.make_async_copy(lad_in[n], lad.at[slot], sems.at[CHUNKS + n]))
    for copy in copies:
        copy.start()
    for copy in copies:
        copy.wait()
    label_i = [labels[pi * 2 + i] for i in range(2)]

    def one_block(hb, carry):
        first = jnp.zeros((128, 256), jnp.float32)
        second = jnp.zeros((128, 256), jnp.float32)
        for g in range(4):
            weights, left, right = [], [], []
            for k in range(12):
                m, kk = g * 4 + k // 3, k % 3
                part = lad[m, hb, kk]
                low = part[64:96]
                third = jnp.concatenate([low, pltpu.roll(low.astype(jnp.float32), 64, 1).astype(jnp.bfloat16)], axis=0)
                weights.append(jnp.concatenate([part[0:64], third], axis=1))
                right.append(amp[m, hb, kk])
            for q in range(6):
                tops = []
                for i in range(2):
                    pair = []
                    for k in (2 * q, 2 * q + 1):
                        m, kk = g * 4 + k // 3, k % 3
                        at = hb ^ label_i[i] ^ labels[m * 3 + kk]
                        pair.append(amp[m, at, kk][:, i * 64 : i * 64 + 64])
                    tops.append(jnp.concatenate(pair, axis=1))
                left.append(jnp.concatenate(tops, axis=0))
            weight = jnp.concatenate(weights, axis=0)
            first += jnp.dot(jnp.concatenate(left, axis=1), weight, preferred_element_type=jnp.float32)
            second += lax.dot_general(
                jnp.concatenate(right, axis=0), weight, (((0,), (0,)), ((), ())),
                preferred_element_type=jnp.float32,
            )
        diff[hb] = 2.0 * first - second
        cross[hb] = jnp.transpose(second)
        return carry

    lax.fori_loop(0, 8, one_block, 0)
    label_j = [labels[pj * 3 + j] for j in range(3)]
    tall = []
    for h in range(8):
        row = []
        for i in range(2):
            for j in range(3):
                direct = diff[h ^ label_i[i], i * 64 : i * 64 + 64, j * 64 : j * 64 + 64]
                crossed = cross[h ^ label_j[j], j * 64 : j * 64 + 64, i * 64 : i * 64 + 64]
                row.append(direct - crossed)
        tall.append(jnp.concatenate(row, axis=1).astype(jnp.bfloat16))
    tall = jnp.concatenate(tall, axis=0)
    sides = [jnp.dot(gather_back(p), tall, preferred_element_type=jnp.float32) for p in range(2)]
    for i in range(2):
        for j in range(3):
            at = (i * 3 + j) * 64
            both = jnp.concatenate([s[:, at : at + 64] for s in sides], axis=1)
            for v in range(32):
                out_ref[i, j, :, v * 128 : v * 128 + 128] = both[v * 8 : v * 8 + 8].astype(jnp.bfloat16)


AMP_KEYS = [(s, d) for s in range(4) for d in range(4)]
LAD_KEYS = [(s, d, c) for c in range(2) for s in range(4) for d in range(2)]


def call(kernel, shape, labels, args, spaces, scratch, flops, nbytes):
    return pl.pallas_call(
        kernel,
        out_shape=jax.ShapeDtypeStruct(shape, jnp.bfloat16),
        in_specs=[pl.BlockSpec(memory_space=pltpu.SMEM)] + [pl.BlockSpec(memory_space=s) for s in spaces],
        out_specs=pl.BlockSpec(memory_space=pltpu.VMEM),
        scratch_shapes=scratch,
        compiler_params=pltpu.CompilerParams(vmem_limit_bytes=40 * 1024 * 1024),
        cost_estimate=pl.CostEstimate(flops=flops, bytes_accessed=nbytes, transcendentals=0),
    )(labels, *args)


def prepare_amp(labels, amplitudes):
    return call(amp_prep, (8, 3, 64, 128), labels, [amplitudes], [pltpu.VMEM], [], 10**9, 10**6)


def prepare_ladder(labels, coulomb, exchange):
    return call(
        ladder_prep, (8, 3, 96, 128), labels, [coulomb, exchange], [pltpu.VMEM] * 2, [], 10**9, 2 * 10**6
    )


def finish(labels, amp, lad):
    args = [amp[key] for key in AMP_KEYS] + [lad[key] for key in LAD_KEYS]
    scratch = [
        pltpu.VMEM((CHUNKS, 8, 3, 64, 128), jnp.bfloat16),
        pltpu.VMEM((CHUNKS, 8, 3, 96, 128), jnp.bfloat16),
        pltpu.VMEM((8, 128, 256), jnp.float32),
        pltpu.VMEM((8, 256, 128), jnp.float32),
        pltpu.SemaphoreType.DMA((2 * CHUNKS,)),
    ]
    return call(
        contract, (2, 3, 8, NVI * NVI), labels, args, [pl.ANY] * (2 * CHUNKS), scratch, 5 * 10**9, 16 * 10**6
    )


def on_device(amplitudes, coulomb, exchange, occ_irrep):
    amp, lad = {}, {}
    amp[0, 0] = prepare_amp(occ_irrep, amplitudes)
    own = prepare_ladder(occ_irrep, coulomb, exchange)
    for d in (1, 2, 3):
        amp[0, d] = lax.ppermute(amp[0, 0], "pj", swap_zl(d))
    for d in range(4):
        amp[1, d] = lax.ppermute(amp[0, d], "pj", shift_y(1))
        amp[3, d] = lax.ppermute(amp[0, d], "pj", shift_y(-1))
    for d in range(4):
        if d < 2:
            amp[2, d] = lax.ppermute(amp[1, d], "pj", shift_y(1))
        else:
            amp[2, d] = lax.ppermute(amp[3, d], "pj", shift_y(-1))
    lad[0, 0, 0] = own
    lad[0, 1, 0] = lax.ppermute(own, "pi", SWAP_ZH)
    for d in range(2):
        lad[1, d, 0] = lax.ppermute(lad[0, d, 0], "pi", shift_x(1))
        lad[3, d, 0] = lax.ppermute(lad[0, d, 0], "pi", shift_x(-1))
    lad[2, 0, 0] = lax.ppermute(lad[1, 0, 0], "pi", shift_x(1))
    lad[2, 1, 0] = lax.ppermute(lad[3, 1, 0], "pi", shift_x(-1))
    for s in range(4):
        for d in range(2):
            lad[s, d, 1] = lax.ppermute(lad[s, d, 0], "pi", SWAP_CORE)
    return finish(occ_irrep, amp, lad)


def solution(mesh):
    placed = (P("pi", "pj", None, None), P("pi", "pj", None, None), P("pi", "pj", None, None), P())
    return jax.shard_map(
        on_device, mesh=mesh, in_specs=placed, out_specs=P("pi", "pj", None, None), check_vma=False
    )
```

time: 556 us -> 150 us (0.27)
  local copies, waits for them, and re-layouts: 197 us -> 1.73 us
  waiting for transfers between devices: 231 us -> 63 us
  matrix products: 98.1 us -> 0 us
  starting transfers between devices: 0.08 us -> 66.3 us
  Pallas kernels: 0 us -> 18.5 us
  between operations: 13.1 us -> 0.25 us
  other arithmetic: 12.3 us -> 0 us
    all_gather x3 -> x0, waiting for transfers between devices: 229 us -> none  [the longest x1 145 us: on_device(): gathered = lax.all_gather(amplitudes, 'pj', axis=1, tiled=True)]
    reshape x4 -> x0, local copies, waits for them, and re-layouts: 129 us -> none  [the longest x1 50.9 us: on_device(): cross_amp = cross_amp.reshape(rows_here, span, cols_here, 8, NVI, NVI)]
    dot_general x6 -> x0, matrix products: 98.1 us -> none  [the longest x1 29.2 us: on_device(): jnp.einsum('ikhac,ikjhcb->ijhab', doubled, direct_ladder, preferred_eleme...]
    ppermute x0 -> x30, starting transfers between devices: none -> 66.3 us  [the longest x8 32.9 us: on_device(): lad[s, d, 1] = lax.ppermute(lad[s, d, 0], 'pi', SWAP_CORE)]
    ppermute x0 -> x30, waiting for transfers between devices: none -> 63 us  [the longest x3 22.5 us: on_device(): amp[0, d] = lax.ppermute(amp[0, 0], 'pj', swap_zl(d))]
    convert_element_type x3 -> x0, local copies, waits for them, and re-layouts: 45.6 us -> none  [the longest x2 45.2 us: on_device(): jnp.swapaxes(swapped, 3, 4).astype(jnp.float32)]
    mul x1 -> x0, local copies, waits for them, and re-layouts: 20.5 us -> none  [on_device(): 2.0 * amp_blocks.astype(jnp.float32)]
    pallas_call x0 -> x3, Pallas kernels: none -> 18.5 us  [call(): pl.pallas_call(kernel, out_shape=jax.ShapeDtypeStruct(shape, jnp.bfloat16...]
  transfers between devices with their start and end apart: 3 -> 30, of which waited for: 2 -> 10; matrix products, arithmetic and copies ran while one was open for 27% -> 0% of each run, Pallas kernels for 0% -> 1%
where the time goes in v1:
time: 150 us
  starting transfers between devices  66.3 us (44%)
  waiting for transfers between devices  63 us (42%)
  Pallas kernels  18.5 us (12%)
  local copies, waits for them, and re-layouts  1.73 us (1%)
    ppermute x8, starting transfers between devices, on_device(): lad[s, d, 1] = lax.ppermute(lad[s, d, 0], 'pi', SWAP_CORE)  32.9 us
    ppermute x3, waiting for transfers between devices, on_device(): amp[0, d] = lax.ppermute(amp[0, 0], 'pj', swap_zl(d))  22.5 us
    ppermute x1, waiting for transfers between devices, on_device(): lad[0, 1, 0] = lax.ppermute(own, 'pi', SWAP_ZH)  18.7 us
    pallas_call x3, Pallas kernels, call(): pl.pallas_call(kernel, out_shape=jax.ShapeDtypeStruct(shape, jnp.bfloat16...  18.5 us
    ppermute x4, starting transfers between devices, on_device(): amp[3, d] = lax.ppermute(amp[0, d], 'pj', shift_y(-1))  10.7 us
    ppermute x4, waiting for transfers between devices, on_device(): amp[1, d] = lax.ppermute(amp[0, d], 'pj', shift_y(1))  10.6 us
    ppermute x1, starting transfers between devices, on_device(): lad[0, 1, 0] = lax.ppermute(own, 'pi', SWAP_ZH)  5.65 us
    ppermute x2, starting transfers between devices, on_device(): lad[3, d, 0] = lax.ppermute(lad[0, d, 0], 'pi', shift_x(-1))  4.96 us
  transfers between devices with their start and end apart: 30, of which 10 were waited for; matrix products, arithmetic and copies ran while one was open for 0% of the time, Pallas kernels for 1%

profile of v1, /device:TPU:1, one launch (start us, length us, event | category | flops | bytes accessed | tf_op | source)
XLA Modules:
  0.0 149.8 jit_solution(11705420900082949413)
XLA Ops:
  0.0 1.1 copy-done.2
  1.1 0.7 copy-done.3
  1.7 1.2 shard_map.46.refs_0_
  2.9 3.6 %collective-permute-start.13 = (bf16[8,3,64,128]{3,2,1,0:T(8,128)(2,1)S(1)}, bf16[8,3,64,128]{3,2,1,0:T(8,128)(2,1)S(1)}, u32[]{:S(2)}, u32[]{:S(2)}) collective-permute-start(bf16[8,3,64,128]{3,2,1,0:T(8,128)(2,1)S(1)} %shard_map.46.refs_0_), channel_id=1, source_target_pairs={{0,12},{1,13},{2,14},{3,15},{4,0},{5,1},{6,2},{7,3},{8,4},{9,5},{1... | collective-permute-start | bytes 1179656 | tf_op jit(solution)/shard_map/ppermute | solution.py:221
  6.6 0.0 collective-permute-start.3
  6.6 4.3 %collective-permute-start.2 = (bf16[8,3,64,128]{3,2,1,0:T(8,128)(2,1)S(1)}, bf16[8,3,64,128]{3,2,1,0:T(8,128)(2,1)S(1)}, u32[]{:S(2)}, u32[]{:S(2)}) collective-permute-start(bf16[8,3,64,128]{3,2,1,0:T(8,128)(2,1)S(1)} %shard_map.46.refs_0_), channel_id=1, source_target_pairs={{0,3},{1,2},{2,1},{3,0},{4,7},{5,6},{6,5},{7,4},{8,11},{9,10},{10,... | collective-permute-start | bytes 1179656 | tf_op jit(solution)/shard_map/ppermute | solution.py:218
  10.9 0.0 collective-permute-start.1
  10.9 0.3 collective-permute-start
  11.2 1.4 shard_map.47.refs_16_
  12.6 1.8 %collective-permute-done.13.refs_12_ = bf16[8,3,64,128]{3,2,1,0:T(8,128)(2,1)S(1)} collective-permute-done((bf16[8,3,64,128]{3,2,1,0:T(8,128)(2,1)S(1)}, bf16[8,3,64,128]{3,2,1,0:T(8,128)(2,1)S(1)}, u32[]{:S(2)}, u32[]{:S(2)}) %collective-permute-start.13) | collective-permute-done | bytes 393248 | tf_op jit(solution)/shard_map/ppermute | solution.py:221
  14.3 1.5 %collective-permute-start.22 = (bf16[8,3,96,128]{3,2,1,0:T(8,128)(2,1)S(1)}, bf16[8,3,96,128]{3,2,1,0:T(8,128)(2,1)S(1)}, u32[]{:S(2)}, u32[]{:S(2)}) collective-permute-start(bf16[8,3,96,128]{3,2,1,0:T(8,128)(2,1)S(1)} %shard_map.47.refs_16_), channel_id=1, source_target_pairs={{0,16},{16,0},{32,48},{48,32},{64,80},{80,64},{96,112},{112,96},{1... | collective-permute-start | bytes 1769480 | tf_op jit(solution)/shard_map/ppermute | solution.py:236
  15.9 1.5 %collective-permute-done.3.refs_4_ = bf16[8,3,64,128]{3,2,1,0:T(8,128)(2,1)S(1)} collective-permute-done((bf16[8,3,64,128]{3,2,1,0:T(8,128)(2,1)S(1)}, bf16[8,3,64,128]{3,2,1,0:T(8,128)(2,1)S(1)}, u32[]{:S(2)}, u32[]{:S(2)}) %collective-permute-start.3) | collective-permute-done | bytes 393248 | tf_op jit(solution)/shard_map/ppermute | solution.py:220
  17.4 2.5 %collective-permute-start.21 = (bf16[8,3,96,128]{3,2,1,0:T(8,128)(2,1)S(1)}, bf16[8,3,96,128]{3,2,1,0:T(8,128)(2,1)S(1)}, u32[]{:S(2)}, u32[]{:S(2)}) collective-permute-start(bf16[8,3,96,128]{3,2,1,0:T(8,128)(2,1)S(1)} %shard_map.47.refs_16_), channel_id=1, source_target_pairs={{0,192},{16,208},{32,224},{48,240},{64,0},{80,16},{96,32},{112,48}... | collective-permute-start | bytes 1769480 | tf_op jit(solution)/shard_map/ppermute | solution.py:231
  19.9 0.0 collective-permute-done.2.refs_3_
  19.9 0.9 collective-permute-start.16
  20.8 22.5 %collective-permute-done.1.refs_2_ = bf16[8,3,64,128]{3,2,1,0:T(8,128)(2,1)S(1)} collective-permute-done((bf16[8,3,64,128]{3,2,1,0:T(8,128)(2,1)S(1)}, bf16[8,3,64,128]{3,2,1,0:T(8,128)(2,1)S(1)}, u32[]{:S(2)}, u32[]{:S(2)}) %collective-permute-start.1) | collective-permute-done | bytes 393248 | tf_op jit(solution)/shard_map/ppermute | solution.py:218
  43.2 5.6 %collective-permute-start.15 = (bf16[8,3,96,128]{3,2,1,0:T(8,128)(2,1)S(1)}, bf16[8,3,96,128]{3,2,1,0:T(8,128)(2,1)S(1)}, u32[]{:S(2)}, u32[]{:S(2)}) collective-permute-start(bf16[8,3,96,128]{3,2,1,0:T(8,128)(2,1)S(1)} %shard_map.47.refs_16_), channel_id=1, source_target_pairs={{0,32},{16,48},{32,0},{48,16},{64,96},{80,112},{96,64},{112,80},{1... | collective-permute-start | bytes 1769480 | tf_op jit(solution)/shard_map/ppermute | solution.py:228
  48.9 0.0 collective-permute-done.refs_1_
  48.9 0.0 collective-permute-start.7
  48.9 0.0 collective-permute-done.22.refs_24_
  48.9 2.7 %collective-permute-start.11 = (bf16[8,3,64,128]{3,2,1,0:T(8,128)(2,1)S(1)}, bf16[8,3,64,128]{3,2,1,0:T(8,128)(2,1)S(1)}, u32[]{:S(2)}, u32[]{:S(2)}) collective-permute-start(bf16[8,3,64,128]{3,2,1,0:T(8,128)(2,1)S(1)} %collective-permute-done.2.refs_3_), channel_id=1, source_target_pairs={{0,12},{1,13},{2,14},{3,15},{4,0},{5,1},{6,2},{7,3},{8,4},{9,5},{1... | collective-permute-start | bytes 1179656 | tf_op jit(solution)/shard_map/ppermute | solution.py:221
  51.6 0.0 collective-permute-done.21.refs_22_
  51.6 0.0 collective-permute-start.6
  51.6 0.0 collective-permute-done.16.refs_18_
  51.6 2.7 %collective-permute-start.9 = (bf16[8,3,64,128]{3,2,1,0:T(8,128)(2,1)S(1)}, bf16[8,3,64,128]{3,2,1,0:T(8,128)(2,1)S(1)}, u32[]{:S(2)}, u32[]{:S(2)}) collective-permute-start(bf16[8,3,64,128]{3,2,1,0:T(8,128)(2,1)S(1)} %collective-permute-done.1.refs_2_), channel_id=1, source_target_pairs={{0,12},{1,13},{2,14},{3,15},{4,0},{5,1},{6,2},{7,3},{8,4},{9,5},{1... | collective-permute-start | bytes 1179656 | tf_op jit(solution)/shard_map/ppermute | solution.py:221
  54.3 18.7 %collective-permute-done.15.refs_17_ = bf16[8,3,96,128]{3,2,1,0:T(8,128)(2,1)S(1)} collective-permute-done((bf16[8,3,96,128]{3,2,1,0:T(8,128)(2,1)S(1)}, bf16[8,3,96,128]{3,2,1,0:T(8,128)(2,1)S(1)}, u32[]{:S(2)}, u32[]{:S(2)}) %collective-permute-start.15) | collective-permute-done | bytes 589856 | tf_op jit(solution)/shard_map/ppermute | solution.py:228
  73.0 0.0 collective-permute-start.5
  73.0 0.0 collective-permute-done.7.refs_8_
  73.0 1.2 collective-permute-start.4
  74.2 0.0 collective-permute-done.11.refs_15_
  74.2 2.5 %collective-permute-start.19 = (bf16[8,3,96,128]{3,2,1,0:T(8,128)(2,1)S(1)}, bf16[8,3,96,128]{3,2,1,0:T(8,128)(2,1)S(1)}, u32[]{:S(2)}, u32[]{:S(2)}) collective-permute-start(bf16[8,3,96,128]{3,2,1,0:T(8,128)(2,1)S(1)} %collective-permute-done.15.refs_17_), channel_id=1, source_target_pairs={{0,192},{16,208},{32,224},{48,240},{64,0},{80,16},{96,32},{112,48}... | collective-permute-start | bytes 1769480 | tf_op jit(solution)/shard_map/ppermute | solution.py:231
  76.7 0.0 collective-permute-done.6.refs_7_
  76.7 1.7 %collective-permute-start.14 = (bf16[8,3,64,128]{3,2,1,0:T(8,128)(2,1)S(1)}, bf16[8,3,64,128]{3,2,1,0:T(8,128)(2,1)S(1)}, u32[]{:S(2)}, u32[]{:S(2)}) collective-permute-start(bf16[8,3,64,128]{3,2,1,0:T(8,128)(2,1)S(1)} %collective-permute-done.refs_1_), channel_id=1, source_target_pairs={{0,12},{1,13},{2,14},{3,15},{4,0},{5,1},{6,2},{7,3},{8,4},{9,5},{1... | collective-permute-start | bytes 1179656 | tf_op jit(solution)/shard_map/ppermute | solution.py:221
  78.4 0.0 collective-permute-done.9.refs_14_
  78.4 1.4 collective-permute-start.12
  79.8 1.9 %collective-permute-done.5.refs_6_ = bf16[8,3,64,128]{3,2,1,0:T(8,128)(2,1)S(1)} collective-permute-done((bf16[8,3,64,128]{3,2,1,0:T(8,128)(2,1)S(1)}, bf16[8,3,64,128]{3,2,1,0:T(8,128)(2,1)S(1)}, u32[]{:S(2)}, u32[]{:S(2)}) %collective-permute-start.5) | collective-permute-done | bytes 393248 | tf_op jit(solution)/shard_map/ppermute | solution.py:220
  81.7 1.3 collective-permute-start.10
  83.0 7.1 %collective-permute-done.4.refs_5_ = bf16[8,3,64,128]{3,2,1,0:T(8,128)(2,1)S(1)} collective-permute-done((bf16[8,3,64,128]{3,2,1,0:T(8,128)(2,1)S(1)}, bf16[8,3,64,128]{3,2,1,0:T(8,128)(2,1)S(1)}, u32[]{:S(2)}, u32[]{:S(2)}) %collective-permute-start.4) | collective-permute-done | bytes 393248 | tf_op jit(solution)/shard_map/ppermute | solution.py:220
  90.1 0.0 collective-permute-start.8
  90.1 0.0 collective-permute-done.14.refs_13_
  90.1 4.0 %collective-permute-start.28 = (bf16[8,3,96,128]{3,2,1,0:T(8,128)(2,1)S(1)}, bf16[8,3,96,128]{3,2,1,0:T(8,128)(2,1)S(1)}, u32[]{:S(2)}, u32[]{:S(2)}) collective-permute-start(bf16[8,3,96,128]{3,2,1,0:T(8,128)(2,1)S(1)} %collective-permute-done.21.refs_22_), channel_id=1, source_target_pairs={{0,16},{16,0},{32,48},{48,32},{64,80},{80,64},{96,112},{112,96},{1... | collective-permute-start | bytes 1769480 | tf_op jit(solution)/shard_map/ppermute | solution.py:236
  94.1 0.0 collective-permute-done.12.refs_11_
  94.2 7.4 %collective-permute-start.24 = (bf16[8,3,96,128]{3,2,1,0:T(8,128)(2,1)S(1)}, bf16[8,3,96,128]{3,2,1,0:T(8,128)(2,1)S(1)}, u32[]{:S(2)}, u32[]{:S(2)}) collective-permute-start(bf16[8,3,96,128]{3,2,1,0:T(8,128)(2,1)S(1)} %collective-permute-done.16.refs_18_), channel_id=1, source_target_pairs={{0,16},{16,0},{32,48},{48,32},{64,80},{80,64},{96,112},{112,96},{1... | collective-permute-start | bytes 1769480 | tf_op jit(solution)/shard_map/ppermute | solution.py:236
  101.6 0.0 collective-permute-done.10.refs_10_
  101.6 0.0 collective-permute-start.18
  101.6 0.0 collective-permute-done.8.refs_9_
  101.6 0.2 collective-permute-start.17
  101.8 0.0 collective-permute-done.19.refs_23_
  101.8 2.6 %collective-permute-start.20 = (bf16[8,3,96,128]{3,2,1,0:T(8,128)(2,1)S(1)}, bf16[8,3,96,128]{3,2,1,0:T(8,128)(2,1)S(1)}, u32[]{:S(2)}, u32[]{:S(2)}) collective-permute-start(bf16[8,3,96,128]{3,2,1,0:T(8,128)(2,1)S(1)} %collective-permute-done.19.refs_23_), channel_id=1, source_target_pairs={{0,192},{16,208},{32,224},{48,240},{64,0},{80,16},{96,32},{112,48}... | collective-permute-start | bytes 1769480 | tf_op jit(solution)/shard_map/ppermute | solution.py:233
  104.4 0.0 collective-permute-done.28.refs_30_
  104.4 4.8 %collective-permute-start.23 = (bf16[8,3,96,128]{3,2,1,0:T(8,128)(2,1)S(1)}, bf16[8,3,96,128]{3,2,1,0:T(8,128)(2,1)S(1)}, u32[]{:S(2)}, u32[]{:S(2)}) collective-permute-start(bf16[8,3,96,128]{3,2,1,0:T(8,128)(2,1)S(1)} %collective-permute-done.15.refs_17_), channel_id=1, source_target_pairs={{0,16},{16,0},{32,48},{48,32},{64,80},{80,64},{96,112},{112,96},{1... | collective-permute-start | bytes 1769480 | tf_op jit(solution)/shard_map/ppermute | solution.py:236
  109.1 0.0 collective-permute-done.24.refs_26_
  109.1 0.1 collective-permute-start.29
  109.2 4.2 %collective-permute-done.18.refs_20_ = bf16[8,3,96,128]{3,2,1,0:T(8,128)(2,1)S(1)} collective-permute-done((bf16[8,3,96,128]{3,2,1,0:T(8,128)(2,1)S(1)}, bf16[8,3,96,128]{3,2,1,0:T(8,128)(2,1)S(1)}, u32[]{:S(2)}, u32[]{:S(2)}) %collective-permute-start.18) | collective-permute-done | bytes 589856 | tf_op jit(solution)/shard_map/ppermute | solution.py:232
  113.4 9.9 %collective-permute-start.26 = (bf16[8,3,96,128]{3,2,1,0:T(8,128)(2,1)S(1)}, bf16[8,3,96,128]{3,2,1,0:T(8,128)(2,1)S(1)}, u32[]{:S(2)}, u32[]{:S(2)}) collective-permute-start(bf16[8,3,96,128]{3,2,1,0:T(8,128)(2,1)S(1)} %collective-permute-done.18.refs_20_), channel_id=1, source_target_pairs={{0,16},{16,0},{32,48},{48,32},{64,80},{80,64},{96,112},{112,96},{1... | collective-permute-start | bytes 1769480 | tf_op jit(solution)/shard_map/ppermute | solution.py:236
  123.3 2.8 %collective-permute-done.17.refs_19_ = bf16[8,3,96,128]{3,2,1,0:T(8,128)(2,1)S(1)} collective-permute-done((bf16[8,3,96,128]{3,2,1,0:T(8,128)(2,1)S(1)}, bf16[8,3,96,128]{3,2,1,0:T(8,128)(2,1)S(1)}, u32[]{:S(2)}, u32[]{:S(2)}) %collective-permute-start.17) | collective-permute-done | bytes 589856 | tf_op jit(solution)/shard_map/ppermute | solution.py:230
  126.1 5.1 %collective-permute-start.25 = (bf16[8,3,96,128]{3,2,1,0:T(8,128)(2,1)S(1)}, bf16[8,3,96,128]{3,2,1,0:T(8,128)(2,1)S(1)}, u32[]{:S(2)}, u32[]{:S(2)}) collective-permute-start(bf16[8,3,96,128]{3,2,1,0:T(8,128)(2,1)S(1)} %collective-permute-done.17.refs_19_), channel_id=1, source_target_pairs={{0,16},{16,0},{32,48},{48,32},{64,80},{80,64},{96,112},{112,96},{1... | collective-permute-start | bytes 1769480 | tf_op jit(solution)/shard_map/ppermute | solution.py:236
  131.2 0.0 collective-permute-start.27
  131.2 0.0 collective-permute-done.23.refs_25_
  131.2 0.0 collective-permute-done.26.refs_28_
  131.2 0.0 collective-permute-done.29.refs_31_
  131.2 1.6 %collective-permute-done.25.refs_27_ = bf16[8,3,96,128]{3,2,1,0:T(8,128)(2,1)S(1)} collective-permute-done((bf16[8,3,96,128]{3,2,1,0:T(8,128)(2,1)S(1)}, bf16[8,3,96,128]{3,2,1,0:T(8,128)(2,1)S(1)}, u32[]{:S(2)}, u32[]{:S(2)}) %collective-permute-start.25) | collective-permute-done | bytes 589856 | tf_op jit(solution)/shard_map/ppermute | solution.py:236
  132.8 0.8 collective-permute-done.27.refs_29_
  133.7 15.9 %shard_map.48 = bf16[2,3,8,4096]{3,2,1,0:T(8,128)(2,1)} custom-call(s32[48]{0:T(128)S(1)} %copy-done.3, bf16[8,3,64,128]{3,2,1,0:T(8,128)(2,1)S(1)} %shard_map.46.refs_0_, bf16[8,3,64,128]{3,2,1,0:T(8,128)(2,1)S(1)} %collective-permute-done.refs_1_, bf16[8,3,64,128]{3,2,1,0:T(8,128)(2,1)S(1)} %collective-permute-done.1.refs_2_, ...), custom_call_target="tpu_custom_call" | custom-call | flops 5000000000 | bytes 16000000 | tf_op jit(solution)/shard_map/pallas_call | solution.py:178
  (11 shorter events, 0.0 us)
Async XLA Ops:
  0.0 11.2 %copy-start.1 = (bf16[3,3,8,4096]{3,2,1,0:T(8,128)(2,1)S(1)}, bf16[3,3,8,4096]{3,2,1,0:T(8,128)(2,1)}, u32[]{:S(2)}) copy-start(bf16[3,3,8,4096]{3,2,1,0:T(8,128)(2,1)} %exch_ref.1) | copy-start | bytes 1769476
  0.0 1.1 copy-start.2
  1.1 0.7 copy-start.3
  1.7 9.5 %copy-start = (bf16[3,3,8,4096]{3,2,1,0:T(8,128)(2,1)S(1)}, bf16[3,3,8,4096]{3,2,1,0:T(8,128)(2,1)}, u32[]{:S(2)}) copy-start(bf16[3,3,8,4096]{3,2,1,0:T(8,128)(2,1)} %coul_ref.1) | copy-start | bytes 1769476
  2.9 11.4 %collective-permute-start.13 = (bf16[8,3,64,128]{3,2,1,0:T(8,128)(2,1)S(1)}, bf16[8,3,64,128]{3,2,1,0:T(8,128)(2,1)S(1)}, u32[]{:S(2)}, u32[]{:S(2)}) collective-permute-start(bf16[8,3,64,128]{3,2,1,0:T(8,128)(2,1)S(1)} %shard_map.46.refs_0_), channel_id=1, source_target_pairs={{0,12},{1,13},{2,14},{3,15},{4,0},{5,1},{6,2},{7,3},{8,4},{9,5},{1... | collective-permute-start | bytes 1179656 | tf_op jit(solution)/shard_map/ppermute | solution.py:221
  6.6 10.9 %collective-permute-start.3 = (bf16[8,3,64,128]{3,2,1,0:T(8,128)(2,1)S(1)}, bf16[8,3,64,128]{3,2,1,0:T(8,128)(2,1)S(1)}, u32[]{:S(2)}, u32[]{:S(2)}) collective-permute-start(bf16[8,3,64,128]{3,2,1,0:T(8,128)(2,1)S(1)} %shard_map.46.refs_0_), channel_id=1, source_target_pairs={{0,4},{1,5},{2,6},{3,7},{4,8},{5,9},{6,10},{7,11},{8,12},{9,13},{1... | collective-permute-start | bytes 1179656 | tf_op jit(solution)/shard_map/ppermute | solution.py:220
  6.6 13.3 %collective-permute-start.2 = (bf16[8,3,64,128]{3,2,1,0:T(8,128)(2,1)S(1)}, bf16[8,3,64,128]{3,2,1,0:T(8,128)(2,1)S(1)}, u32[]{:S(2)}, u32[]{:S(2)}) collective-permute-start(bf16[8,3,64,128]{3,2,1,0:T(8,128)(2,1)S(1)} %shard_map.46.refs_0_), channel_id=1, source_target_pairs={{0,3},{1,2},{2,1},{3,0},{4,7},{5,6},{6,5},{7,4},{8,11},{9,10},{10,... | collective-permute-start | bytes 1179656 | tf_op jit(solution)/shard_map/ppermute | solution.py:218
  10.9 32.3 %collective-permute-start.1 = (bf16[8,3,64,128]{3,2,1,0:T(8,128)(2,1)S(1)}, bf16[8,3,64,128]{3,2,1,0:T(8,128)(2,1)S(1)}, u32[]{:S(2)}, u32[]{:S(2)}) collective-permute-start(bf16[8,3,64,128]{3,2,1,0:T(8,128)(2,1)S(1)} %shard_map.46.refs_0_), channel_id=1, source_target_pairs={{0,2},{1,3},{2,0},{3,1},{4,6},{5,7},{6,4},{7,5},{8,10},{9,11},{10,... | collective-permute-start | bytes 1179656 | tf_op jit(solution)/shard_map/ppermute | solution.py:218
  10.9 38.0 %collective-permute-start = (bf16[8,3,64,128]{3,2,1,0:T(8,128)(2,1)S(1)}, bf16[8,3,64,128]{3,2,1,0:T(8,128)(2,1)S(1)}, u32[]{:S(2)}, u32[]{:S(2)}) collective-permute-start(bf16[8,3,64,128]{3,2,1,0:T(8,128)(2,1)S(1)} %shard_map.46.refs_0_), channel_id=1, source_target_pairs={{0,1},{1,0},{2,3},{3,2},{4,5},{5,4},{6,7},{7,6},{8,9},{9,8},{10,11... | collective-permute-start | bytes 1179656 | tf_op jit(solution)/shard_map/ppermute | solution.py:218
  14.3 34.5 %collective-permute-start.22 = (bf16[8,3,96,128]{3,2,1,0:T(8,128)(2,1)S(1)}, bf16[8,3,96,128]{3,2,1,0:T(8,128)(2,1)S(1)}, u32[]{:S(2)}, u32[]{:S(2)}) collective-permute-start(bf16[8,3,96,128]{3,2,1,0:T(8,128)(2,1)S(1)} %shard_map.47.refs_16_), channel_id=1, source_target_pairs={{0,16},{16,0},{32,48},{48,32},{64,80},{80,64},{96,112},{112,96},{1... | collective-permute-start | bytes 1769480 | tf_op jit(solution)/shard_map/ppermute | solution.py:236
  17.4 34.2 %collective-permute-start.21 = (bf16[8,3,96,128]{3,2,1,0:T(8,128)(2,1)S(1)}, bf16[8,3,96,128]{3,2,1,0:T(8,128)(2,1)S(1)}, u32[]{:S(2)}, u32[]{:S(2)}) collective-permute-start(bf16[8,3,96,128]{3,2,1,0:T(8,128)(2,1)S(1)} %shard_map.47.refs_16_), channel_id=1, source_target_pairs={{0,192},{16,208},{32,224},{48,240},{64,0},{80,16},{96,32},{112,48}... | collective-permute-start | bytes 1769480 | tf_op jit(solution)/shard_map/ppermute | solution.py:231
  19.9 31.7 %collective-permute-start.16 = (bf16[8,3,96,128]{3,2,1,0:T(8,128)(2,1)S(1)}, bf16[8,3,96,128]{3,2,1,0:T(8,128)(2,1)S(1)}, u32[]{:S(2)}, u32[]{:S(2)}) collective-permute-start(bf16[8,3,96,128]{3,2,1,0:T(8,128)(2,1)S(1)} %shard_map.47.refs_16_), channel_id=1, source_target_pairs={{0,64},{16,80},{32,96},{48,112},{64,128},{80,144},{96,160},{112,17... | collective-permute-start | bytes 1769480 | tf_op jit(solution)/shard_map/ppermute | solution.py:230
  43.2 29.7 %collective-permute-start.15 = (bf16[8,3,96,128]{3,2,1,0:T(8,128)(2,1)S(1)}, bf16[8,3,96,128]{3,2,1,0:T(8,128)(2,1)S(1)}, u32[]{:S(2)}, u32[]{:S(2)}) collective-permute-start(bf16[8,3,96,128]{3,2,1,0:T(8,128)(2,1)S(1)} %shard_map.47.refs_16_), channel_id=1, source_target_pairs={{0,32},{16,48},{32,0},{48,16},{64,96},{80,112},{96,64},{112,80},{1... | collective-permute-start | bytes 1769480 | tf_op jit(solution)/shard_map/ppermute | solution.py:228
  48.9 24.1 %collective-permute-start.7 = (bf16[8,3,64,128]{3,2,1,0:T(8,128)(2,1)S(1)}, bf16[8,3,64,128]{3,2,1,0:T(8,128)(2,1)S(1)}, u32[]{:S(2)}, u32[]{:S(2)}) collective-permute-start(bf16[8,3,64,128]{3,2,1,0:T(8,128)(2,1)S(1)} %collective-permute-done.3.refs_4_), channel_id=1, source_target_pairs={{0,4},{1,5},{2,6},{3,7},{4,8},{5,9},{6,10},{7,11},{8,12},{9,13},{1... | collective-permute-start | bytes 1179656 | tf_op jit(solution)/shard_map/ppermute | solution.py:224
  48.9 25.3 %collective-permute-start.11 = (bf16[8,3,64,128]{3,2,1,0:T(8,128)(2,1)S(1)}, bf16[8,3,64,128]{3,2,1,0:T(8,128)(2,1)S(1)}, u32[]{:S(2)}, u32[]{:S(2)}) collective-permute-start(bf16[8,3,64,128]{3,2,1,0:T(8,128)(2,1)S(1)} %collective-permute-done.2.refs_3_), channel_id=1, source_target_pairs={{0,12},{1,13},{2,14},{3,15},{4,0},{5,1},{6,2},{7,3},{8,4},{9,5},{1... | collective-permute-start | bytes 1179656 | tf_op jit(solution)/shard_map/ppermute | solution.py:221
  51.6 25.1 %collective-permute-start.6 = (bf16[8,3,64,128]{3,2,1,0:T(8,128)(2,1)S(1)}, bf16[8,3,64,128]{3,2,1,0:T(8,128)(2,1)S(1)}, u32[]{:S(2)}, u32[]{:S(2)}) collective-permute-start(bf16[8,3,64,128]{3,2,1,0:T(8,128)(2,1)S(1)} %collective-permute-done.2.refs_3_), channel_id=1, source_target_pairs={{0,4},{1,5},{2,6},{3,7},{4,8},{5,9},{6,10},{7,11},{8,12},{9,13},{1... | collective-permute-start | bytes 1179656 | tf_op jit(solution)/shard_map/ppermute | solution.py:220
  51.6 26.8 %collective-permute-start.9 = (bf16[8,3,64,128]{3,2,1,0:T(8,128)(2,1)S(1)}, bf16[8,3,64,128]{3,2,1,0:T(8,128)(2,1)S(1)}, u32[]{:S(2)}, u32[]{:S(2)}) collective-permute-start(bf16[8,3,64,128]{3,2,1,0:T(8,128)(2,1)S(1)} %collective-permute-done.1.refs_2_), channel_id=1, source_target_pairs={{0,12},{1,13},{2,14},{3,15},{4,0},{5,1},{6,2},{7,3},{8,4},{9,5},{1... | collective-permute-start | bytes 1179656 | tf_op jit(solution)/shard_map/ppermute | solution.py:221
  73.0 8.7 %collective-permute-start.5 = (bf16[8,3,64,128]{3,2,1,0:T(8,128)(2,1)S(1)}, bf16[8,3,64,128]{3,2,1,0:T(8,128)(2,1)S(1)}, u32[]{:S(2)}, u32[]{:S(2)}) collective-permute-start(bf16[8,3,64,128]{3,2,1,0:T(8,128)(2,1)S(1)} %collective-permute-done.1.refs_2_), channel_id=1, source_target_pairs={{0,4},{1,5},{2,6},{3,7},{4,8},{5,9},{6,10},{7,11},{8,12},{9,13},{1... | collective-permute-start | bytes 1179656 | tf_op jit(solution)/shard_map/ppermute | solution.py:220
  73.0 17.2 %collective-permute-start.4 = (bf16[8,3,64,128]{3,2,1,0:T(8,128)(2,1)S(1)}, bf16[8,3,64,128]{3,2,1,0:T(8,128)(2,1)S(1)}, u32[]{:S(2)}, u32[]{:S(2)}) collective-permute-start(bf16[8,3,64,128]{3,2,1,0:T(8,128)(2,1)S(1)} %collective-permute-done.refs_1_), channel_id=1, source_target_pairs={{0,4},{1,5},{2,6},{3,7},{4,8},{5,9},{6,10},{7,11},{8,12},{9,13},{1... | collective-permute-start | bytes 1179656 | tf_op jit(solution)/shard_map/ppermute | solution.py:220
  74.2 27.6 %collective-permute-start.19 = (bf16[8,3,96,128]{3,2,1,0:T(8,128)(2,1)S(1)}, bf16[8,3,96,128]{3,2,1,0:T(8,128)(2,1)S(1)}, u32[]{:S(2)}, u32[]{:S(2)}) collective-permute-start(bf16[8,3,96,128]{3,2,1,0:T(8,128)(2,1)S(1)} %collective-permute-done.15.refs_17_), channel_id=1, source_target_pairs={{0,192},{16,208},{32,224},{48,240},{64,0},{80,16},{96,32},{112,48}... | collective-permute-start | bytes 1769480 | tf_op jit(solution)/shard_map/ppermute | solution.py:231
  76.7 13.5 %collective-permute-start.14 = (bf16[8,3,64,128]{3,2,1,0:T(8,128)(2,1)S(1)}, bf16[8,3,64,128]{3,2,1,0:T(8,128)(2,1)S(1)}, u32[]{:S(2)}, u32[]{:S(2)}) collective-permute-start(bf16[8,3,64,128]{3,2,1,0:T(8,128)(2,1)S(1)} %collective-permute-done.refs_1_), channel_id=1, source_target_pairs={{0,12},{1,13},{2,14},{3,15},{4,0},{5,1},{6,2},{7,3},{8,4},{9,5},{1... | collective-permute-start | bytes 1179656 | tf_op jit(solution)/shard_map/ppermute | solution.py:221
  78.4 15.8 %collective-permute-start.12 = (bf16[8,3,64,128]{3,2,1,0:T(8,128)(2,1)S(1)}, bf16[8,3,64,128]{3,2,1,0:T(8,128)(2,1)S(1)}, u32[]{:S(2)}, u32[]{:S(2)}) collective-permute-start(bf16[8,3,64,128]{3,2,1,0:T(8,128)(2,1)S(1)} %collective-permute-done.11.refs_15_), channel_id=1, source_target_pairs={{0,12},{1,13},{2,14},{3,15},{4,0},{5,1},{6,2},{7,3},{8,4},{9,5},{1... | collective-permute-start | bytes 1179656 | tf_op jit(solution)/shard_map/ppermute | solution.py:226
  81.7 19.9 %collective-permute-start.10 = (bf16[8,3,64,128]{3,2,1,0:T(8,128)(2,1)S(1)}, bf16[8,3,64,128]{3,2,1,0:T(8,128)(2,1)S(1)}, u32[]{:S(2)}, u32[]{:S(2)}) collective-permute-start(bf16[8,3,64,128]{3,2,1,0:T(8,128)(2,1)S(1)} %collective-permute-done.9.refs_14_), channel_id=1, source_target_pairs={{0,12},{1,13},{2,14},{3,15},{4,0},{5,1},{6,2},{7,3},{8,4},{9,5},{1... | collective-permute-start | bytes 1179656 | tf_op jit(solution)/shard_map/ppermute | solution.py:226
  90.1 11.5 %collective-permute-start.8 = (bf16[8,3,64,128]{3,2,1,0:T(8,128)(2,1)S(1)}, bf16[8,3,64,128]{3,2,1,0:T(8,128)(2,1)S(1)}, u32[]{:S(2)}, u32[]{:S(2)}) collective-permute-start(bf16[8,3,64,128]{3,2,1,0:T(8,128)(2,1)S(1)} %collective-permute-done.4.refs_5_), channel_id=1, source_target_pairs={{0,4},{1,5},{2,6},{3,7},{4,8},{5,9},{6,10},{7,11},{8,12},{9,13},{1... | collective-permute-start | bytes 1179656 | tf_op jit(solution)/shard_map/ppermute | solution.py:224
  90.1 14.2 %collective-permute-start.28 = (bf16[8,3,96,128]{3,2,1,0:T(8,128)(2,1)S(1)}, bf16[8,3,96,128]{3,2,1,0:T(8,128)(2,1)S(1)}, u32[]{:S(2)}, u32[]{:S(2)}) collective-permute-start(bf16[8,3,96,128]{3,2,1,0:T(8,128)(2,1)S(1)} %collective-permute-done.21.refs_22_), channel_id=1, source_target_pairs={{0,16},{16,0},{32,48},{48,32},{64,80},{80,64},{96,112},{112,96},{1... | collective-permute-start | bytes 1769480 | tf_op jit(solution)/shard_map/ppermute | solution.py:236
  94.2 15.0 %collective-permute-start.24 = (bf16[8,3,96,128]{3,2,1,0:T(8,128)(2,1)S(1)}, bf16[8,3,96,128]{3,2,1,0:T(8,128)(2,1)S(1)}, u32[]{:S(2)}, u32[]{:S(2)}) collective-permute-start(bf16[8,3,96,128]{3,2,1,0:T(8,128)(2,1)S(1)} %collective-permute-done.16.refs_18_), channel_id=1, source_target_pairs={{0,16},{16,0},{32,48},{48,32},{64,80},{80,64},{96,112},{112,96},{1... | collective-permute-start | bytes 1769480 | tf_op jit(solution)/shard_map/ppermute | solution.py:236
  101.6 11.8 %collective-permute-start.18 = (bf16[8,3,96,128]{3,2,1,0:T(8,128)(2,1)S(1)}, bf16[8,3,96,128]{3,2,1,0:T(8,128)(2,1)S(1)}, u32[]{:S(2)}, u32[]{:S(2)}) collective-permute-start(bf16[8,3,96,128]{3,2,1,0:T(8,128)(2,1)S(1)} %collective-permute-done.16.refs_18_), channel_id=1, source_target_pairs={{0,64},{16,80},{32,96},{48,112},{64,128},{80,144},{96,160},{112,17... | collective-permute-start | bytes 1769480 | tf_op jit(solution)/shard_map/ppermute | solution.py:232
  101.6 24.5 %collective-permute-start.17 = (bf16[8,3,96,128]{3,2,1,0:T(8,128)(2,1)S(1)}, bf16[8,3,96,128]{3,2,1,0:T(8,128)(2,1)S(1)}, u32[]{:S(2)}, u32[]{:S(2)}) collective-permute-start(bf16[8,3,96,128]{3,2,1,0:T(8,128)(2,1)S(1)} %collective-permute-done.15.refs_17_), channel_id=1, source_target_pairs={{0,64},{16,80},{32,96},{48,112},{64,128},{80,144},{96,160},{112,17... | collective-permute-start | bytes 1769480 | tf_op jit(solution)/shard_map/ppermute | solution.py:230
  101.8 29.4 %collective-permute-start.20 = (bf16[8,3,96,128]{3,2,1,0:T(8,128)(2,1)S(1)}, bf16[8,3,96,128]{3,2,1,0:T(8,128)(2,1)S(1)}, u32[]{:S(2)}, u32[]{:S(2)}) collective-permute-start(bf16[8,3,96,128]{3,2,1,0:T(8,128)(2,1)S(1)} %collective-permute-done.19.refs_23_), channel_id=1, source_target_pairs={{0,192},{16,208},{32,224},{48,240},{64,0},{80,16},{96,32},{112,48}... | collective-permute-start | bytes 1769480 | tf_op jit(solution)/shard_map/ppermute | solution.py:233
  104.4 29.3 %copy-start.4 = (bf16[8,3,96,128]{3,2,1,0:T(8,128)(2,1)}, bf16[8,3,96,128]{3,2,1,0:T(8,128)(2,1)S(1)}, u32[]{:S(2)}) copy-start(bf16[8,3,96,128]{3,2,1,0:T(8,128)(2,1)S(1)} %collective-permute-done.28.refs_30_) | copy-start | bytes 1769476
  104.4 26.8 %collective-permute-start.23 = (bf16[8,3,96,128]{3,2,1,0:T(8,128)(2,1)S(1)}, bf16[8,3,96,128]{3,2,1,0:T(8,128)(2,1)S(1)}, u32[]{:S(2)}, u32[]{:S(2)}) collective-permute-start(bf16[8,3,96,128]{3,2,1,0:T(8,128)(2,1)S(1)} %collective-permute-done.15.refs_17_), channel_id=1, source_target_pairs={{0,16},{16,0},{32,48},{48,32},{64,80},{80,64},{96,112},{112,96},{1... | collective-permute-start | bytes 1769480 | tf_op jit(solution)/shard_map/ppermute | solution.py:236
  109.1 22.1 %collective-permute-start.29 = (bf16[8,3,96,128]{3,2,1,0:T(8,128)(2,1)S(1)}, bf16[8,3,96,128]{3,2,1,0:T(8,128)(2,1)S(1)}, u32[]{:S(2)}, u32[]{:S(2)}) collective-permute-start(bf16[8,3,96,128]{3,2,1,0:T(8,128)(2,1)S(1)} %collective-permute-done.19.refs_23_), channel_id=1, source_target_pairs={{0,16},{16,0},{32,48},{48,32},{64,80},{80,64},{96,112},{112,96},{1... | collective-permute-start | bytes 1769480 | tf_op jit(solution)/shard_map/ppermute | solution.py:236
  113.4 17.8 %collective-permute-start.26 = (bf16[8,3,96,128]{3,2,1,0:T(8,128)(2,1)S(1)}, bf16[8,3,96,128]{3,2,1,0:T(8,128)(2,1)S(1)}, u32[]{:S(2)}, u32[]{:S(2)}) collective-permute-start(bf16[8,3,96,128]{3,2,1,0:T(8,128)(2,1)S(1)} %collective-permute-done.18.refs_20_), channel_id=1, source_target_pairs={{0,16},{16,0},{32,48},{48,32},{64,80},{80,64},{96,112},{112,96},{1... | collective-permute-start | bytes 1769480 | tf_op jit(solution)/shard_map/ppermute | solution.py:236
  126.1 6.8 %collective-permute-start.25 = (bf16[8,3,96,128]{3,2,1,0:T(8,128)(2,1)S(1)}, bf16[8,3,96,128]{3,2,1,0:T(8,128)(2,1)S(1)}, u32[]{:S(2)}, u32[]{:S(2)}) collective-permute-start(bf16[8,3,96,128]{3,2,1,0:T(8,128)(2,1)S(1)} %collective-permute-done.17.refs_19_), channel_id=1, source_target_pairs={{0,16},{16,0},{32,48},{48,32},{64,80},{80,64},{96,112},{112,96},{1... | collective-permute-start | bytes 1769480 | tf_op jit(solution)/shard_map/ppermute | solution.py:236
  131.2 2.5 %collective-permute-start.27 = (bf16[8,3,96,128]{3,2,1,0:T(8,128)(2,1)S(1)}, bf16[8,3,96,128]{3,2,1,0:T(8,128)(2,1)S(1)}, u32[]{:S(2)}, u32[]{:S(2)}) collective-permute-start(bf16[8,3,96,128]{3,2,1,0:T(8,128)(2,1)S(1)} %collective-permute-done.20.refs_21_), channel_id=1, source_target_pairs={{0,16},{16,0},{32,48},{48,32},{64,80},{80,64},{96,112},{112,96},{1... | collective-permute-start | bytes 1769480 | tf_op jit(solution)/shard_map/ppermute | solution.py:236
  131.2 2.4 %copy-start.5 = (bf16[8,3,96,128]{3,2,1,0:T(8,128)(2,1)}, bf16[8,3,96,128]{3,2,1,0:T(8,128)(2,1)S(1)}, u32[]{:S(2)}) copy-start(bf16[8,3,96,128]{3,2,1,0:T(8,128)(2,1)S(1)} %collective-permute-done.29.refs_31_) | copy-start | bytes 1769476

commit v2 on v1

v2 whole, which is shorter than its diff:
```python
import jax
import jax.numpy as jnp
from jax import lax
from jax.experimental import pallas as pl
from jax.experimental.pallas import tpu as pltpu
from jax.sharding import PartitionSpec as P

NVI = 64
MESH_X, MESH_Y, MESH_ZH, MESH_ZL = 4, 4, 2, 4
CHUNKS = 16


def perm_pi(move):
    pairs = []
    for x in range(MESH_X):
        for zh in range(MESH_ZH):
            for c in range(2):
                x2, zh2, c2 = move(x, zh, c)
                pairs.append((x * 4 + zh * 2 + c, (x2 % 4) * 4 + zh2 * 2 + c2))
    return pairs


def perm_pj(move):
    pairs = []
    for y in range(MESH_Y):
        for zl in range(MESH_ZL):
            y2, zl2 = move(y, zl)
            pairs.append((y * 4 + zl, (y2 % 4) * 4 + zl2))
    return pairs


def shift_y(d):
    return perm_pj(lambda y, zl: (y + d, zl))


def shift_x(d):
    return perm_pi(lambda x, zh, c: (x + d, zh, c))


def swap_zl(d):
    return perm_pj(lambda y, zl: (y, zl ^ d))


SWAP_CORE = perm_pi(lambda x, zh, c: (x, zh, c ^ 1))
SWAP_ZH = perm_pi(lambda x, zh, c: (x, zh ^ 1, c))


def spread(half):
    row = lax.broadcasted_iota(jnp.int32, (512, 256), 0)
    col = lax.broadcasted_iota(jnp.int32, (512, 256), 1)
    want = ((row & 63) >> 1) * 8 + (row >> 6)
    return jnp.where((col == want) & ((row & 1) == half), 1.0, 0.0).astype(jnp.bfloat16)


def gather_back(half):
    row = lax.broadcasted_iota(jnp.int32, (256, 512), 0)
    col = lax.broadcasted_iota(jnp.int32, (256, 512), 1)
    want = ((col & 63) >> 1) * 8 + (col >> 6)
    return jnp.where((row == want) & ((col & 1) == half), 1.0, 0.0).astype(jnp.bfloat16)


def stacked(flat):
    return jnp.concatenate([flat[:, v * 128 : (v + 1) * 128] for v in range(32)], axis=0)


def prepare(labels, amp_in, coul_in, exch_in, amp_out, lad_out, amp, coul, exch, sems):
    loads = [
        pltpu.make_async_copy(source, target, sems.at[n])
        for n, (source, target) in enumerate(((amp_in, amp), (coul_in, coul), (exch_in, exch)))
    ]
    for load in loads:
        load.start()
    picks = [spread(0), spread(1)]

    def matrices(flats):
        rows = [stacked(flat).astype(jnp.bfloat16) for flat in flats]
        block = None
        for p in range(2):
            side = jnp.concatenate([r[:, p * 64 : p * 64 + 64] for r in rows], axis=1)
            part = jnp.dot(picks[p], side, preferred_element_type=jnp.float32)
            block = part if block is None else block + part
        return block

    loads[0].wait()
    base = lax.axis_index("pj") * 3
    for k in range(3):
        label = labels[base + k]
        block = matrices([amp[i, k].astype(jnp.float32) for i in range(2)]).astype(jnp.bfloat16)
        for h in range(8):
            amp_out[h ^ label, k] = block[h * 64 : h * 64 + 64]
    loads[1].wait()
    loads[2].wait()
    base = lax.axis_index("pi") * 3
    for k in range(3):
        label = labels[base + k]
        block = matrices(
            [2.0 * coul[k, j].astype(jnp.float32) - exch[k, j].astype(jnp.float32) for j in range(3)]
        )
        for h in range(8):
            part = block[h * 64 : h * 64 + 64]
            lad_out[h ^ label, k, 0:64] = part[:, 0:128].astype(jnp.bfloat16)
            third = jnp.concatenate([part[0:32, 128:192], part[32:64, 128:192]], axis=1)
            lad_out[h ^ label, k, 64:96] = third.astype(jnp.bfloat16)


def halves(x, y):
    late0, late1 = (x + 2) % 4, (y + 2) % 4
    late1 = jnp.where(late1 == late0, (late0 + 1) % 4, late1)
    early0 = jnp.where((late0 + 1) % 4 == late1, (late0 + 2) % 4, (late0 + 1) % 4)
    return (early0, 6 - late0 - late1 - early0), (late0, late1)


def products(labels, amp_in, lad_in, amp_parts, lad_parts, amp, lad, sems, late, one_block):
    pi, pj = lax.axis_index("pi"), lax.axis_index("pj")
    x, zh, core = pi // 4, (pi // 2) % 2, pi % 2
    y, zl = pj // 4, pj % 4
    columns = halves(x, y)[late]
    copies = []

    def bring(source, target, mx, group):
        copy = pltpu.make_async_copy(source, target, sems.at[len(copies)])
        copies.append((copy, (mx == columns[0]) | (mx == columns[1]), group))

    for name, first, (s, d), h, count in amp_parts:
        mx = (y + 4 - s) % 4
        slot = jnp.where(mx == columns[0], 0, 4) + (zl ^ d)
        bring(amp_in[name].at[pl.ds(first, count)], amp.at[slot, pl.ds(h, count)], mx, 0)
    for half in range(2):
        for name, first, (s, d, c) in lad_parts:
            mx = (x + 4 - s) % 4
            slot = jnp.where(mx == columns[0], 0, 4) + (zh ^ d) * 2 + (core ^ c)
            bring(
                lad_in[name].at[pl.ds(first + half * 4, 4)], lad.at[slot, pl.ds(half * 4, 4)], mx, half
            )
    for copy, wanted, _ in copies:
        pl.when(wanted)(copy.start)

    label_i = [labels[pi * 2 + i] for i in range(2)]

    def block(hb, carry):
        first = jnp.zeros((128, 256), jnp.float32)
        second = jnp.zeros((128, 256), jnp.float32)
        for g in range(2):
            weights, left, right = [], [], []
            for k in range(12):
                m, kk = g * 4 + k // 3, k % 3
                part = lad[m, hb, kk]
                low = part[64:96]
                turned = pltpu.roll(low.astype(jnp.float32), 64, 1).astype(jnp.bfloat16)
                weights.append(jnp.concatenate([part[0:64], jnp.concatenate([low, turned], axis=0)], axis=1))
                right.append(amp[m, hb, kk])
            for q in range(6):
                tops = []
                for i in range(2):
                    pair = []
                    for k in (2 * q, 2 * q + 1):
                        m, kk = g * 4 + k // 3, k % 3
                        label = labels[(columns[g] * 4 + k // 3) * 3 + kk]
                        pair.append(amp[m, hb ^ label_i[i] ^ label, kk][:, i * 64 : i * 64 + 64])
                    tops.append(jnp.concatenate(pair, axis=1))
                left.append(jnp.concatenate(tops, axis=0))
            weight = jnp.concatenate(weights, axis=0)
            first += jnp.dot(jnp.concatenate(left, axis=1), weight, preferred_element_type=jnp.float32)
            second += lax.dot_general(
                jnp.concatenate(right, axis=0), weight, (((0,), (0,)), ((), ())),
                preferred_element_type=jnp.float32,
            )
        one_block(hb, first, second)
        return carry

    for half in range(2):
        for copy, wanted, group in copies:
            if group == half:
                pl.when(wanted)(copy.wait)
        lax.fori_loop(half * 4, half * 4 + 4, block, 0)


def early_products(labels, *refs):
    amp_in = dict(zip(AMP_EARLY, refs))
    lad_in = dict(zip(LAD_EARLY, refs[len(AMP_EARLY) :]))
    first_out, second_out, amp, lad, sems = refs[len(AMP_EARLY) + len(LAD_EARLY) :]

    def keep(hb, first, second):
        first_out[hb] = first
        second_out[hb] = second

    amp_parts = [part for part in AMP_PARTS if part[2][0] != 2]
    lad_parts = [part for part in LAD_PARTS if part[2][0] != 2]
    products(labels, amp_in, lad_in, amp_parts, lad_parts, amp, lad, sems, 0, keep)


def late_products(labels, first_in, second_in, *refs):
    amp_in = dict(zip(AMP_NAMES, refs))
    lad_in = dict(zip(LAD_NAMES, refs[len(AMP_NAMES) :]))
    out_ref, amp, lad, diff, cross, sems = refs[len(AMP_NAMES) + len(LAD_NAMES) :]
    pi, pj = lax.axis_index("pi"), lax.axis_index("pj")

    def keep(hb, first, second):
        second = second + second_in[hb]
        diff[hb] = 2.0 * (first + first_in[hb]) - second
        cross[hb] = jnp.transpose(second)

    products(labels, amp_in, lad_in, AMP_PARTS, LAD_PARTS, amp, lad, sems, 1, keep)
    label_i = [labels[pi * 2 + i] for i in range(2)]
    label_j = [labels[pj * 3 + j] for j in range(3)]
    tall = []
    for h in range(8):
        row = []
        for i in range(2):
            for j in range(3):
                direct = diff[h ^ label_i[i], i * 64 : i * 64 + 64, j * 64 : j * 64 + 64]
                crossed = cross[h ^ label_j[j], j * 64 : j * 64 + 64, i * 64 : i * 64 + 64]
                row.append(direct - crossed)
        tall.append(jnp.concatenate(row, axis=1).astype(jnp.bfloat16))
    tall = jnp.concatenate(tall, axis=0)
    sides = [jnp.dot(gather_back(p), tall, preferred_element_type=jnp.float32) for p in range(2)]
    for i in range(2):
        for j in range(3):
            at = (i * 3 + j) * 64
            both = jnp.concatenate([s[:, at : at + 64] for s in sides], axis=1)
            for v in range(32):
                out_ref[i, j, :, v * 128 : v * 128 + 128] = both[v * 8 : v * 8 + 8].astype(jnp.bfloat16)


AMP_PARTS = [
    ("a", 0, (0, 0), 0, 8), ("z1", 0, (0, 1), 0, 8), ("z2", 0, (0, 2), 0, 8), ("z3", 0, (0, 3), 0, 8),
    ("yo+", 0, (1, 0), 0, 8), ("yo-", 0, (3, 0), 0, 8), ("fo", 0, (2, 0), 0, 8),
    ("yq+", 0, (1, 1), 0, 8), ("yq+", 8, (1, 2), 0, 8), ("yq-", 0, (3, 1), 0, 8), ("yq-", 8, (3, 2), 0, 8),
    ("f1", 0, (2, 1), 0, 8), ("f2", 0, (2, 2), 0, 8),
    ("y3+", 0, (1, 3), 0, 8), ("y3-", 0, (3, 3), 0, 8), ("f3a", 0, (2, 3), 0, 4), ("f3b", 0, (2, 3), 4, 4),
]
LAD_PARTS = [
    ("l", 0, (0, 0, 0)), ("xo+", 0, (1, 0, 0)), ("xo-", 0, (3, 0, 0)), ("fxo", 0, (2, 0, 0)),
    ("zh", 0, (0, 1, 0)), ("xz+", 0, (1, 1, 0)), ("xz-", 0, (3, 1, 0)), ("fxz", 0, (2, 1, 0)),
    ("c1", 0, (0, 0, 1)), ("c1", 8, (1, 0, 1)), ("c1", 16, (3, 0, 1)),
    ("c1", 24, (0, 1, 1)), ("c1", 32, (1, 1, 1)), ("c1", 40, (3, 1, 1)),
    ("c2", 0, (2, 0, 1)), ("c2", 8, (2, 1, 1)),
]
AMP_NAMES = list(dict.fromkeys(part[0] for part in AMP_PARTS))
LAD_NAMES = list(dict.fromkeys(part[0] for part in LAD_PARTS))
AMP_EARLY = list(dict.fromkeys(part[0] for part in AMP_PARTS if part[2][0] != 2))
LAD_EARLY = list(dict.fromkeys(part[0] for part in LAD_PARTS if part[2][0] != 2))
COPIES = len(AMP_PARTS) + 2 * len(LAD_PARTS)
X_UP, X_DOWN = ("pi", shift_x(1)), ("pi", shift_x(-1))
Y_UP, Y_DOWN, Y_FAR = ("pj", shift_y(1)), ("pj", shift_y(-1)), ("pj", shift_y(2))
Z_ONE, Z_TWO = ("pj", swap_zl(1)), ("pj", swap_zl(2))
Z_HALF, OTHER_CORE = ("pi", SWAP_ZH), ("pi", SWAP_CORE)
PLAN = [
    ("z1", "a", Z_ONE, 0, 1),
    ("z2", "a", Z_TWO, 0, 1),
    ("yo+", "a", Y_UP, 0, 1),
    ("yo-", "a", Y_DOWN, 0, 1),
    ("xo+", "l", X_UP, 0, 1),
    ("zh", "l", Z_HALF, 1, 2),
    ("yq+", ("z1", "z2"), Y_UP, 1, 2),
    ("yq-", ("z1", "z2"), Y_DOWN, 1, 2),
    ("fo", "yo+", Y_UP, 1, 2),
    ("xo-", "l", X_DOWN, 1, 2),
    ("z3", "z2", Z_ONE, 2, 3),
    ("f1", ("yq+", 0, 8), Y_UP, 2, 3),
    ("f2", ("yq-", 8, 16), Y_DOWN, 2, 3),
    ("xz+", "zh", X_UP, 2, 3),
    ("xz-", "zh", X_DOWN, 2, 3),
    ("y3+", "z3", Y_UP, 3, 4),
    ("y3-", "z3", Y_DOWN, 3, 4),
    ("fxo", "xo+", X_UP, 3, 4),
    ("fxz", "xz-", X_DOWN, 3, 4),
    ("c1", ("l", "xo+", "xo-", "zh", "xz+", "xz-"), OTHER_CORE, 3, 4),
    ("f3a", ("y3+", 0, 4), Y_UP, 4, 5),
    ("f3b", ("y3-", 4, 8), Y_DOWN, 4, 5),
    ("c2", ("fxo", "fxz"), OTHER_CORE, 4, 5),
]
JOINS = {}


def call(kernel, outs, labels, args, spaces, scratch, flops, nbytes, vmem):
    return pl.pallas_call(
        kernel,
        out_shape=outs,
        in_specs=[pl.BlockSpec(memory_space=pltpu.SMEM)] + [pl.BlockSpec(memory_space=s) for s in spaces],
        out_specs=[pl.BlockSpec(memory_space=pltpu.VMEM)] * len(outs),
        scratch_shapes=scratch,
        compiler_params=pltpu.CompilerParams(vmem_limit_bytes=vmem * 1024 * 1024),
        cost_estimate=pl.CostEstimate(flops=flops, bytes_accessed=nbytes, transcendentals=0),
    )(labels, *args)


def lay_out(labels, *args):
    scratch = [pltpu.VMEM(arg.shape, arg.dtype) for arg in args] + [pltpu.SemaphoreType.DMA((3,))]
    outs = [jax.ShapeDtypeStruct((8, 3, rows, 128), jnp.bfloat16) for rows in (64, 96)]
    return call(prepare, outs, labels, args, [pl.ANY] * 3, scratch, 2 * 10**9, 3 * 10**6, 60)


def slots():
    return [pltpu.VMEM((8, 8, 3, 64, 128), jnp.bfloat16), pltpu.VMEM((8, 8, 3, 96, 128), jnp.bfloat16)]


def begin(labels, got):
    args = [fetch(got, name) for name in AMP_EARLY + LAD_EARLY]
    outs = [jax.ShapeDtypeStruct((8, 128, 256), jnp.float32)] * 2
    scratch = slots() + [pltpu.SemaphoreType.DMA((COPIES,))]
    return call(early_products, outs, labels, args, [pl.ANY] * len(args), scratch, 5 * 10**9, 8 * 10**6, 18)


def finish(labels, got, sums):
    args = [fetch(got, name) for name in AMP_NAMES + LAD_NAMES]
    outs = [jax.ShapeDtypeStruct((2, 3, 8, NVI * NVI), jnp.bfloat16)]
    scratch = slots() + [
        pltpu.VMEM((8, 128, 256), jnp.float32),
        pltpu.VMEM((8, 256, 128), jnp.float32),
        pltpu.SemaphoreType.DMA((COPIES,)),
    ]
    spaces = [pltpu.VMEM] * 2 + [pl.ANY] * len(args)
    return call(late_products, outs, labels, [*sums, *args], spaces, scratch, 5 * 10**9, 8 * 10**6, 22)[0]


def fetch(got, source):
    if isinstance(source, str) and source in JOINS:
        source = JOINS[source]
    if isinstance(source, str):
        return got[source]
    if isinstance(source[1], int):
        return got[source[0]][source[1] : source[2]]
    return jnp.concatenate([fetch(got, part) for part in source], axis=0)


def on_device(amplitudes, coulomb, exchange, occ_irrep):
    got = dict(zip("al", lay_out(occ_irrep, amplitudes, coulomb, exchange)))
    ends = {name: end for name, _, _, _, end in PLAN}
    starts = {name: start for name, _, _, start, _ in PLAN}
    for name, source, (axis, pairs), start, _ in sorted(PLAN, key=lambda step: step[3]):
        before = [n for n in ends if ends[n] <= start]
        last = [n for n in before if not any(ends[n] <= starts[m] for m in before)]
        value = fetch(got, source)
        if last:
            value = lax.optimization_barrier((value, *[got[n] for n in last]))[0]
        got[name] = lax.ppermute(value, axis, pairs)
    return finish(occ_irrep, got, begin(occ_irrep, got))


def solution(mesh):
    placed = (P("pi", "pj", None, None), P("pi", "pj", None, None), P("pi", "pj", None, None), P())
    return jax.shard_map(
        on_device, mesh=mesh, in_specs=placed, out_specs=P("pi", "pj", None, None), check_vma=False
    )
```

time: 150 us -> 117 us (0.78)
  the two profiles are of different devices: /device:TPU:1 before, /device:TPU:97 now
where the time goes in v2:
time: 117 us
  waiting for transfers between devices  63.9 us (55%)
  starting transfers between devices  28 us (24%)
  Pallas kernels  23.2 us (20%)
  local copies, waits for them, and re-layouts  1.59 us (1%)
    ppermute x23, waiting for transfers between devices, on_device(): got[name] = lax.ppermute(value, axis, pairs)  63.9 us
    ppermute x23, starting transfers between devices, on_device(): got[name] = lax.ppermute(value, axis, pairs)  28 us
    pallas_call x3, Pallas kernels, call(): pl.pallas_call(kernel, out_shape=outs, in_specs=[pl.BlockSpec(memory_spac...  23.2 us
  transfers between devices with their start and end apart: 23, of which 6 were waited for; matrix products, arithmetic and copies ran while one was open for 1% of the time, Pallas kernels for 7%

profile of v2, /device:TPU:97, one launch (start us, length us, event | category | flops | bytes accessed | tf_op | source)
XLA Modules:
  0.0 117.2 jit_solution(13882983898185525325)
XLA Ops:
  0.0 4.2 %shard_map.46 = (bf16[8,3,64,128]{3,2,1,0:T(8,128)(2,1)}, bf16[8,3,96,128]{3,2,1,0:T(8,128)(2,1)}) custom-call(s32[48]{0:T(128)} %labels.5, bf16[2,3,8,4096]{3,2,1,0:T(8,128)(2,1)} %amp_in.1, bf16[3,3,8,4096]{3,2,1,0:T(8,128)(2,1)} %coul_in.1, bf16[3,3,8,4096]{3,2,1,0:T(8,128)(2,1)} %exch_in.1), custom_call_target="tpu_custom_call" | custom-call | flops 2000000000 | bytes 3000000 | tf_op jit(solution)/shard_map/pallas_call | solution.py:277
  4.2 1.3 %collective-permute-start.4 = (bf16[8,3,96,128]{3,2,1,0:T(8,128)(2,1)}, bf16[8,3,96,128]{3,2,1,0:T(8,128)(2,1)S(1)}, u32[]{:S(2)}, u32[]{:S(2)}) collective-permute-start(bf16[8,3,96,128]{3,2,1,0:T(8,128)(2,1)} %get-tuple-element.25.refs_10_.refs_15_), channel_id=1, source_target_pairs={{0,64},{16,80},{32,96},{48,112},{64,128},{80,144},{96,160},{112,17... | collective-permute-start | bytes 1769480 | tf_op jit(solution)/shard_map/ppermute | solution.py:337
  5.4 0.0 collective-permute-start.1
  5.5 0.0 collective-permute-start
  5.5 1.3 %collective-permute-start.2 = (bf16[8,3,64,128]{3,2,1,0:T(8,128)(2,1)}, bf16[8,3,64,128]{3,2,1,0:T(8,128)(2,1)S(1)}, u32[]{:S(2)}, u32[]{:S(2)}) collective-permute-start(bf16[8,3,64,128]{3,2,1,0:T(8,128)(2,1)} %get-tuple-element.23.refs_0_), channel_id=1, source_target_pairs={{0,4},{1,5},{2,6},{3,7},{4,8},{5,9},{6,10},{7,11},{8,12},{9,13},{1... | collective-permute-start | bytes 1179656 | tf_op jit(solution)/shard_map/ppermute | solution.py:337
  6.8 1.5 %collective-permute-start.3 = (bf16[8,3,64,128]{3,2,1,0:T(8,128)(2,1)}, bf16[8,3,64,128]{3,2,1,0:T(8,128)(2,1)S(1)}, u32[]{:S(2)}, u32[]{:S(2)}) collective-permute-start(bf16[8,3,64,128]{3,2,1,0:T(8,128)(2,1)} %get-tuple-element.23.refs_0_), channel_id=1, source_target_pairs={{0,12},{1,13},{2,14},{3,15},{4,0},{5,1},{6,2},{7,3},{8,4},{9,5},{1... | collective-permute-start | bytes 1179656 | tf_op jit(solution)/shard_map/ppermute | solution.py:337
  8.3 17.3 %collective-permute-done.1.refs_2_ = bf16[8,3,64,128]{3,2,1,0:T(8,128)(2,1)S(1)} collective-permute-done((bf16[8,3,64,128]{3,2,1,0:T(8,128)(2,1)}, bf16[8,3,64,128]{3,2,1,0:T(8,128)(2,1)S(1)}, u32[]{:S(2)}, u32[]{:S(2)}) %collective-permute-start.1) | collective-permute-done | bytes 393248 | tf_op jit(solution)/shard_map/ppermute | solution.py:337
  25.6 0.0 collective-permute-done.refs_1_
  25.6 0.1 pad_maximum_fusion.1
  25.6 0.0 collective-permute-done.2.refs_4_
  25.7 0.0 collective-permute-done.3.refs_5_
  25.7 0.0 collective-permute-done.4.refs_11_.refs_16_
  25.7 1.4 %collective-permute-start.6 = (bf16[16,3,64,128]{3,2,1,0:T(8,128)(2,1)S(1)}, bf16[16,3,64,128]{3,2,1,0:T(8,128)(2,1)S(1)}, u32[]{:S(2)}, u32[]{:S(2)}) collective-permute-start(bf16[16,3,64,128]{3,2,1,0:T(8,128)(2,1)S(1)} %pad_maximum_fusion.1), channel_id=1, source_target_pairs={{0,4},{1,5},{2,6},{3,7},{4,8},{5,9},{6,10},{7,11},{8,12},{9,13},{1... | collective-permute-start | bytes 2359304 | tf_op jit(solution)/shard_map/ppermute | solution.py:337
  27.1 1.5 %collective-permute-start.7 = (bf16[16,3,64,128]{3,2,1,0:T(8,128)(2,1)S(1)}, bf16[16,3,64,128]{3,2,1,0:T(8,128)(2,1)S(1)}, u32[]{:S(2)}, u32[]{:S(2)}) collective-permute-start(bf16[16,3,64,128]{3,2,1,0:T(8,128)(2,1)S(1)} %pad_maximum_fusion.1), channel_id=1, source_target_pairs={{0,12},{1,13},{2,14},{3,15},{4,0},{5,1},{6,2},{7,3},{8,4},{9,5},{1... | collective-permute-start | bytes 2359304 | tf_op jit(solution)/shard_map/ppermute | solution.py:337
  28.6 4.2 %collective-permute-start.5 = (bf16[8,3,96,128]{3,2,1,0:T(8,128)(2,1)}, bf16[8,3,96,128]{3,2,1,0:T(8,128)(2,1)S(1)}, u32[]{:S(2)}, u32[]{:S(2)}) collective-permute-start(bf16[8,3,96,128]{3,2,1,0:T(8,128)(2,1)} %get-tuple-element.25.refs_10_.refs_15_), channel_id=1, source_target_pairs={{0,32},{16,48},{32,0},{48,16},{64,96},{80,112},{96,64},{112,80},{1... | collective-permute-start | bytes 1769480 | tf_op jit(solution)/shard_map/ppermute | solution.py:337
  32.7 1.5 %collective-permute-start.9 = (bf16[8,3,96,128]{3,2,1,0:T(8,128)(2,1)}, bf16[8,3,96,128]{3,2,1,0:T(8,128)(2,1)S(1)}, u32[]{:S(2)}, u32[]{:S(2)}) collective-permute-start(bf16[8,3,96,128]{3,2,1,0:T(8,128)(2,1)} %get-tuple-element.25.refs_10_.refs_15_), channel_id=1, source_target_pairs={{0,192},{16,208},{32,224},{48,240},{64,0},{80,16},{96,32},{112,48}... | collective-permute-start | bytes 1769480 | tf_op jit(solution)/shard_map/ppermute | solution.py:337
  34.2 0.0 collective-permute-start.8
  34.2 19.9 %collective-permute-done.8.refs_6_ = bf16[8,3,64,128]{3,2,1,0:T(8,128)(2,1)S(1)} collective-permute-done((bf16[8,3,64,128]{3,2,1,0:T(8,128)(2,1)S(1)}, bf16[8,3,64,128]{3,2,1,0:T(8,128)(2,1)S(1)}, u32[]{:S(2)}, u32[]{:S(2)}) %collective-permute-start.8) | collective-permute-done | bytes 393248 | tf_op jit(solution)/shard_map/ppermute | solution.py:337
  54.1 5.2 %collective-permute-done.5.refs_13_.refs_19_ = bf16[8,3,96,128]{3,2,1,0:T(8,128)(2,1)S(1)} collective-permute-done((bf16[8,3,96,128]{3,2,1,0:T(8,128)(2,1)}, bf16[8,3,96,128]{3,2,1,0:T(8,128)(2,1)S(1)}, u32[]{:S(2)}, u32[]{:S(2)}) %collective-permute-start.5) | collective-permute-done | bytes 589856 | tf_op jit(solution)/shard_map/ppermute | solution.py:337
  59.3 0.0 collective-permute-done.9.refs_12_.refs_17_
  59.3 0.0 collective-permute-done.6.refs_6_.refs_7_
  59.3 0.0 collective-permute-done.7.refs_7_.refs_8_
  59.3 1.3 %collective-permute-start.13 = (bf16[8,3,96,128]{3,2,1,0:T(8,128)(2,1)S(1)}, bf16[8,3,96,128]{3,2,1,0:T(8,128)(2,1)S(1)}, u32[]{:S(2)}, u32[]{:S(2)}) collective-permute-start(bf16[8,3,96,128]{3,2,1,0:T(8,128)(2,1)S(1)} %collective-permute-done.5.refs_13_.refs_19_), channel_id=1, source_target_pairs={{0,64},{16,80},{32,96},{48,112},{64,128},{80,144},{96,160},{112,17... | collective-permute-start | bytes 1769480 | tf_op jit(solution)/shard_map/ppermute | solution.py:337
  60.6 1.4 %collective-permute-start.14 = (bf16[8,3,96,128]{3,2,1,0:T(8,128)(2,1)S(1)}, bf16[8,3,96,128]{3,2,1,0:T(8,128)(2,1)S(1)}, u32[]{:S(2)}, u32[]{:S(2)}) collective-permute-start(bf16[8,3,96,128]{3,2,1,0:T(8,128)(2,1)S(1)} %collective-permute-done.5.refs_13_.refs_19_), channel_id=1, source_target_pairs={{0,192},{16,208},{32,224},{48,240},{64,0},{80,16},{96,32},{112,48}... | collective-permute-start | bytes 1769480 | tf_op jit(solution)/shard_map/ppermute | solution.py:337
  62.1 1.1 constant_dynamic-update-slice_fusion.5
  63.2 0.1 constant_dynamic-update-slice_fusion.4
  63.3 1.3 %collective-permute-start.12 = (bf16[8,3,64,128]{3,2,1,0:T(8,128)(2,1)S(1)}, bf16[8,3,64,128]{3,2,1,0:T(8,128)(2,1)S(1)}, u32[]{:S(2)}, u32[]{:S(2)}) collective-permute-start(bf16[8,3,64,128]{3,2,1,0:T(8,128)(2,1)S(1)} %slice.17), channel_id=1, source_target_pairs={{0,12},{1,13},{2,14},{3,15},{4,0},{5,1},{6,2},{7,3},{8,4},{9,5},{1... | collective-permute-start | bytes 1179656 | tf_op jit(solution)/shard_map/ppermute | solution.py:337
  64.6 0.3 collective-permute-start.11
  65.0 0.0 collective-permute-start.10
  65.0 0.1 constant_dynamic-update-slice_fusion.3
  65.1 0.0 copy-start
  65.1 0.0 copy-start.1
  65.1 0.0 copy-start.2
  65.1 0.1 constant_dynamic-update-slice_fusion.2
  65.2 8.4 %collective-permute-done.13.refs_14_.refs_20_ = bf16[8,3,96,128]{3,2,1,0:T(8,128)(2,1)S(1)} collective-permute-done((bf16[8,3,96,128]{3,2,1,0:T(8,128)(2,1)S(1)}, bf16[8,3,96,128]{3,2,1,0:T(8,128)(2,1)S(1)}, u32[]{:S(2)}, u32[]{:S(2)}) %collective-permute-start.13) | collective-permute-done | bytes 589856 | tf_op jit(solution)/shard_map/ppermute | solution.py:337
  73.6 0.1 constant_dynamic-update-slice_fusion.1
  73.7 0.0 collective-permute-done.14.refs_15_.refs_21_
  73.7 0.1 constant_dynamic-update-slice_fusion
  73.8 0.0 collective-permute-done.12.refs_10_
  73.8 0.0 collective-permute-done.11.refs_9_
  73.8 0.0 collective-permute-done.10.refs_3_
  73.8 3.7 %collective-permute-start.17 = (bf16[48,3,96,128]{3,2,1,0:T(8,128)(2,1)S(1)}, bf16[48,3,96,128]{3,2,1,0:T(8,128)(2,1)S(1)}, u32[]{:S(2)}, u32[]{:S(2)}) collective-permute-start(bf16[48,3,96,128]{3,2,1,0:T(8,128)(2,1)S(1)} %constant_dynamic-update-slice_fusion), channel_id=1, source_target_pairs={{0,16},{16,0},{32,48},{48,32},{64,80},{80,64},{96,112},{112,96},{1... | collective-permute-start | bytes 10616840 | tf_op jit(solution)/shard_map/ppermute | solution.py:337
  77.5 1.8 %collective-permute-start.19 = (bf16[8,3,96,128]{3,2,1,0:T(8,128)(2,1)S(1)}, bf16[8,3,96,128]{3,2,1,0:T(8,128)(2,1)S(1)}, u32[]{:S(2)}, u32[]{:S(2)}) collective-permute-start(bf16[8,3,96,128]{3,2,1,0:T(8,128)(2,1)S(1)} %collective-permute-done.14.refs_15_.refs_21_), channel_id=1, source_target_pairs={{0,192},{16,208},{32,224},{48,240},{64,0},{80,16},{96,32},{112,48}... | collective-permute-start | bytes 1769480 | tf_op jit(solution)/shard_map/ppermute | solution.py:337
  79.3 0.0 collective-permute-start.18
  79.3 0.0 collective-permute-start.15
  79.3 2.7 %collective-permute-start.16 = (bf16[8,3,64,128]{3,2,1,0:T(8,128)(2,1)S(1)}, bf16[8,3,64,128]{3,2,1,0:T(8,128)(2,1)S(1)}, u32[]{:S(2)}, u32[]{:S(2)}) collective-permute-start(bf16[8,3,64,128]{3,2,1,0:T(8,128)(2,1)S(1)} %collective-permute-done.10.refs_3_), channel_id=1, source_target_pairs={{0,12},{1,13},{2,14},{3,15},{4,0},{5,1},{6,2},{7,3},{8,4},{9,5},{1... | collective-permute-start | bytes 1179656 | tf_op jit(solution)/shard_map/ppermute | solution.py:337
  81.9 10.5 %collective-permute-done.19.refs_22_ = bf16[8,3,96,128]{3,2,1,0:T(8,128)(2,1)S(1)} collective-permute-done((bf16[8,3,96,128]{3,2,1,0:T(8,128)(2,1)S(1)}, bf16[8,3,96,128]{3,2,1,0:T(8,128)(2,1)S(1)}, u32[]{:S(2)}, u32[]{:S(2)}) %collective-permute-start.19) | collective-permute-done | bytes 589856 | tf_op jit(solution)/shard_map/ppermute | solution.py:337
  92.4 2.6 %collective-permute-done.18.refs_18_ = bf16[8,3,96,128]{3,2,1,0:T(8,128)(2,1)S(1)} collective-permute-done((bf16[8,3,96,128]{3,2,1,0:T(8,128)(2,1)S(1)}, bf16[8,3,96,128]{3,2,1,0:T(8,128)(2,1)S(1)}, u32[]{:S(2)}, u32[]{:S(2)}) %collective-permute-start.18) | collective-permute-done | bytes 589856 | tf_op jit(solution)/shard_map/ppermute | solution.py:337
  95.0 0.1 pad_maximum_fusion
  95.1 0.0 collective-permute-done.15.refs_8_.refs_11_
  95.1 0.0 collective-permute-done.16.refs_9_.refs_12_
  95.2 0.0 collective-permute-done.17.refs_16_.refs_23_
  95.2 1.3 %collective-permute-start.22 = (bf16[16,3,96,128]{3,2,1,0:T(8,128)(2,1)S(1)}, bf16[16,3,96,128]{3,2,1,0:T(8,128)(2,1)S(1)}, u32[]{:S(2)}, u32[]{:S(2)}) collective-permute-start(bf16[16,3,96,128]{3,2,1,0:T(8,128)(2,1)S(1)} %pad_maximum_fusion), channel_id=1, source_target_pairs={{0,16},{16,0},{32,48},{48,32},{64,80},{80,64},{96,112},{112,96},{1... | collective-permute-start | bytes 3538952 | tf_op jit(solution)/shard_map/ppermute | solution.py:337
  96.5 1.3 %collective-permute-start.21 = (bf16[4,3,64,128]{3,2,1,0:T(8,128)(2,1)S(1)}, bf16[4,3,64,128]{3,2,1,0:T(8,128)(2,1)S(1)}, u32[]{:S(2)}, u32[]{:S(2)}) collective-permute-start(bf16[4,3,64,128]{3,2,1,0:T(8,128)(2,1)S(1)} %slice.19), channel_id=1, source_target_pairs={{0,12},{1,13},{2,14},{3,15},{4,0},{5,1},{6,2},{7,3},{8,4},{9,5},{1... | collective-permute-start | bytes 589832 | tf_op jit(solution)/shard_map/ppermute | solution.py:337
  97.8 0.2 collective-permute-start.20
  98.0 0.0 copy-done
  98.0 0.0 copy-done.1
  98.0 0.0 copy-done.2
  98.0 8.2 %shard_map.47 = (f32[8,128,256]{2,1,0:T(8,128)S(1)}, f32[8,128,256]{2,1,0:T(8,128)S(1)}) custom-call(s32[48]{0:T(128)S(1)} %copy-done.2, bf16[8,3,64,128]{3,2,1,0:T(8,128)(2,1)S(1)} %copy-done.1, bf16[8,3,64,128]{3,2,1,0:T(8,128)(2,1)S(1)} %collective-permute-done.refs_1_, bf16[8,3,64,128]{3,2,1,0:T(8,128)(2,1)S(1)} %collective-permute-done.1.refs_2_, ...), custom_call_target="tpu_custom_call" | custom-call | flops 5000000000 | bytes 8000000 | tf_op jit(solution)/shard_map/pallas_call | solution.py:277
  106.2 0.0 collective-permute-done.21.refs_14_
  106.2 0.0 collective-permute-done.20.refs_13_
  106.2 0.0 collective-permute-done.22.refs_24_
  106.2 10.8 %shard_map.48 = bf16[2,3,8,4096]{3,2,1,0:T(8,128)(2,1)} custom-call(s32[48]{0:T(128)S(1)} %copy-done.2, f32[8,128,256]{2,1,0:T(8,128)S(1)} %get-tuple-element.34.first_in, f32[8,128,256]{2,1,0:T(8,128)S(1)} %get-tuple-element.35.second_in, bf16[8,3,64,128]{3,2,1,0:T(8,128)(2,1)S(1)} %copy-done.1, bf16[8,3,64,128]{3,2,1,0:T(8,128)(2,1)S(1)} %collective-permute-done.refs_1_, ...), custom_call_target="tpu_custom_call" | custom-call | flops 5000000000 | bytes 8000000 | tf_op jit(solution)/shard_map/pallas_call | solution.py:277
  (4 shorter events, 0.1 us)
Async XLA Ops:
  4.2 21.5 %collective-permute-start.4 = (bf16[8,3,96,128]{3,2,1,0:T(8,128)(2,1)}, bf16[8,3,96,128]{3,2,1,0:T(8,128)(2,1)S(1)}, u32[]{:S(2)}, u32[]{:S(2)}) collective-permute-start(bf16[8,3,96,128]{3,2,1,0:T(8,128)(2,1)} %get-tuple-element.25.refs_10_.refs_15_), channel_id=1, source_target_pairs={{0,64},{16,80},{32,96},{48,112},{64,128},{80,144},{96,160},{112,17... | collective-permute-start | bytes 1769480 | tf_op jit(solution)/shard_map/ppermute | solution.py:337
  5.4 20.1 %collective-permute-start.1 = (bf16[8,3,64,128]{3,2,1,0:T(8,128)(2,1)}, bf16[8,3,64,128]{3,2,1,0:T(8,128)(2,1)S(1)}, u32[]{:S(2)}, u32[]{:S(2)}) collective-permute-start(bf16[8,3,64,128]{3,2,1,0:T(8,128)(2,1)} %get-tuple-element.23.refs_0_), channel_id=1, source_target_pairs={{0,2},{1,3},{2,0},{3,1},{4,6},{5,7},{6,4},{7,5},{8,10},{9,11},{10,... | collective-permute-start | bytes 1179656 | tf_op jit(solution)/shard_map/ppermute | solution.py:337
  5.5 20.1 %collective-permute-start = (bf16[8,3,64,128]{3,2,1,0:T(8,128)(2,1)}, bf16[8,3,64,128]{3,2,1,0:T(8,128)(2,1)S(1)}, u32[]{:S(2)}, u32[]{:S(2)}) collective-permute-start(bf16[8,3,64,128]{3,2,1,0:T(8,128)(2,1)} %get-tuple-element.23.refs_0_), channel_id=1, source_target_pairs={{0,1},{1,0},{2,3},{3,2},{4,5},{5,4},{6,7},{7,6},{8,9},{9,8},{10,11... | collective-permute-start | bytes 1179656 | tf_op jit(solution)/shard_map/ppermute | solution.py:337
  5.5 20.2 %collective-permute-start.2 = (bf16[8,3,64,128]{3,2,1,0:T(8,128)(2,1)}, bf16[8,3,64,128]{3,2,1,0:T(8,128)(2,1)S(1)}, u32[]{:S(2)}, u32[]{:S(2)}) collective-permute-start(bf16[8,3,64,128]{3,2,1,0:T(8,128)(2,1)} %get-tuple-element.23.refs_0_), channel_id=1, source_target_pairs={{0,4},{1,5},{2,6},{3,7},{4,8},{5,9},{6,10},{7,11},{8,12},{9,13},{1... | collective-permute-start | bytes 1179656 | tf_op jit(solution)/shard_map/ppermute | solution.py:337
  6.8 18.9 %collective-permute-start.3 = (bf16[8,3,64,128]{3,2,1,0:T(8,128)(2,1)}, bf16[8,3,64,128]{3,2,1,0:T(8,128)(2,1)S(1)}, u32[]{:S(2)}, u32[]{:S(2)}) collective-permute-start(bf16[8,3,64,128]{3,2,1,0:T(8,128)(2,1)} %get-tuple-element.23.refs_0_), channel_id=1, source_target_pairs={{0,12},{1,13},{2,14},{3,15},{4,0},{5,1},{6,2},{7,3},{8,4},{9,5},{1... | collective-permute-start | bytes 1179656 | tf_op jit(solution)/shard_map/ppermute | solution.py:337
  25.7 33.7 %collective-permute-start.6 = (bf16[16,3,64,128]{3,2,1,0:T(8,128)(2,1)S(1)}, bf16[16,3,64,128]{3,2,1,0:T(8,128)(2,1)S(1)}, u32[]{:S(2)}, u32[]{:S(2)}) collective-permute-start(bf16[16,3,64,128]{3,2,1,0:T(8,128)(2,1)S(1)} %pad_maximum_fusion.1), channel_id=1, source_target_pairs={{0,4},{1,5},{2,6},{3,7},{4,8},{5,9},{6,10},{7,11},{8,12},{9,13},{1... | collective-permute-start | bytes 2359304 | tf_op jit(solution)/shard_map/ppermute | solution.py:337
  27.1 32.3 %collective-permute-start.7 = (bf16[16,3,64,128]{3,2,1,0:T(8,128)(2,1)S(1)}, bf16[16,3,64,128]{3,2,1,0:T(8,128)(2,1)S(1)}, u32[]{:S(2)}, u32[]{:S(2)}) collective-permute-start(bf16[16,3,64,128]{3,2,1,0:T(8,128)(2,1)S(1)} %pad_maximum_fusion.1), channel_id=1, source_target_pairs={{0,12},{1,13},{2,14},{3,15},{4,0},{5,1},{6,2},{7,3},{8,4},{9,5},{1... | collective-permute-start | bytes 2359304 | tf_op jit(solution)/shard_map/ppermute | solution.py:337
  28.6 30.7 %collective-permute-start.5 = (bf16[8,3,96,128]{3,2,1,0:T(8,128)(2,1)}, bf16[8,3,96,128]{3,2,1,0:T(8,128)(2,1)S(1)}, u32[]{:S(2)}, u32[]{:S(2)}) collective-permute-start(bf16[8,3,96,128]{3,2,1,0:T(8,128)(2,1)} %get-tuple-element.25.refs_10_.refs_15_), channel_id=1, source_target_pairs={{0,32},{16,48},{32,0},{48,16},{64,96},{80,112},{96,64},{112,80},{1... | collective-permute-start | bytes 1769480 | tf_op jit(solution)/shard_map/ppermute | solution.py:337
  32.7 26.6 %collective-permute-start.9 = (bf16[8,3,96,128]{3,2,1,0:T(8,128)(2,1)}, bf16[8,3,96,128]{3,2,1,0:T(8,128)(2,1)S(1)}, u32[]{:S(2)}, u32[]{:S(2)}) collective-permute-start(bf16[8,3,96,128]{3,2,1,0:T(8,128)(2,1)} %get-tuple-element.25.refs_10_.refs_15_), channel_id=1, source_target_pairs={{0,192},{16,208},{32,224},{48,240},{64,0},{80,16},{96,32},{112,48}... | collective-permute-start | bytes 1769480 | tf_op jit(solution)/shard_map/ppermute | solution.py:337
  34.2 19.9 %collective-permute-start.8 = (bf16[8,3,64,128]{3,2,1,0:T(8,128)(2,1)S(1)}, bf16[8,3,64,128]{3,2,1,0:T(8,128)(2,1)S(1)}, u32[]{:S(2)}, u32[]{:S(2)}) collective-permute-start(bf16[8,3,64,128]{3,2,1,0:T(8,128)(2,1)S(1)} %collective-permute-done.2.refs_4_), channel_id=1, source_target_pairs={{0,4},{1,5},{2,6},{3,7},{4,8},{5,9},{6,10},{7,11},{8,12},{9,13},{1... | collective-permute-start | bytes 1179656 | tf_op jit(solution)/shard_map/ppermute | solution.py:337
  59.3 14.2 %collective-permute-start.13 = (bf16[8,3,96,128]{3,2,1,0:T(8,128)(2,1)S(1)}, bf16[8,3,96,128]{3,2,1,0:T(8,128)(2,1)S(1)}, u32[]{:S(2)}, u32[]{:S(2)}) collective-permute-start(bf16[8,3,96,128]{3,2,1,0:T(8,128)(2,1)S(1)} %collective-permute-done.5.refs_13_.refs_19_), channel_id=1, source_target_pairs={{0,64},{16,80},{32,96},{48,112},{64,128},{80,144},{96,160},{112,17... | collective-permute-start | bytes 1769480 | tf_op jit(solution)/shard_map/ppermute | solution.py:337
  60.6 13.0 %collective-permute-start.14 = (bf16[8,3,96,128]{3,2,1,0:T(8,128)(2,1)S(1)}, bf16[8,3,96,128]{3,2,1,0:T(8,128)(2,1)S(1)}, u32[]{:S(2)}, u32[]{:S(2)}) collective-permute-start(bf16[8,3,96,128]{3,2,1,0:T(8,128)(2,1)S(1)} %collective-permute-done.5.refs_13_.refs_19_), channel_id=1, source_target_pairs={{0,192},{16,208},{32,224},{48,240},{64,0},{80,16},{96,32},{112,48}... | collective-permute-start | bytes 1769480 | tf_op jit(solution)/shard_map/ppermute | solution.py:337
  63.3 10.4 %collective-permute-start.12 = (bf16[8,3,64,128]{3,2,1,0:T(8,128)(2,1)S(1)}, bf16[8,3,64,128]{3,2,1,0:T(8,128)(2,1)S(1)}, u32[]{:S(2)}, u32[]{:S(2)}) collective-permute-start(bf16[8,3,64,128]{3,2,1,0:T(8,128)(2,1)S(1)} %slice.17), channel_id=1, source_target_pairs={{0,12},{1,13},{2,14},{3,15},{4,0},{5,1},{6,2},{7,3},{8,4},{9,5},{1... | collective-permute-start | bytes 1179656 | tf_op jit(solution)/shard_map/ppermute | solution.py:337
  64.6 9.1 %collective-permute-start.11 = (bf16[8,3,64,128]{3,2,1,0:T(8,128)(2,1)S(1)}, bf16[8,3,64,128]{3,2,1,0:T(8,128)(2,1)S(1)}, u32[]{:S(2)}, u32[]{:S(2)}) collective-permute-start(bf16[8,3,64,128]{3,2,1,0:T(8,128)(2,1)S(1)} %slice.16), channel_id=1, source_target_pairs={{0,4},{1,5},{2,6},{3,7},{4,8},{5,9},{6,10},{7,11},{8,12},{9,13},{1... | collective-permute-start | bytes 1179656 | tf_op jit(solution)/shard_map/ppermute | solution.py:337
  65.0 8.8 %collective-permute-start.10 = (bf16[8,3,64,128]{3,2,1,0:T(8,128)(2,1)S(1)}, bf16[8,3,64,128]{3,2,1,0:T(8,128)(2,1)S(1)}, u32[]{:S(2)}, u32[]{:S(2)}) collective-permute-start(bf16[8,3,64,128]{3,2,1,0:T(8,128)(2,1)S(1)} %collective-permute-done.1.refs_2_), channel_id=1, source_target_pairs={{0,1},{1,0},{2,3},{3,2},{4,5},{5,4},{6,7},{7,6},{8,9},{9,8},{10,11... | collective-permute-start | bytes 1179656 | tf_op jit(solution)/shard_map/ppermute | solution.py:337
  65.1 32.9 %copy-start = (bf16[8,3,96,128]{3,2,1,0:T(8,128)(2,1)S(1)}, bf16[8,3,96,128]{3,2,1,0:T(8,128)(2,1)}, u32[]{:S(2)}) copy-start(bf16[8,3,96,128]{3,2,1,0:T(8,128)(2,1)} %get-tuple-element.25.refs_10_.refs_15_) | copy-start | bytes 1769476
  65.1 32.9 %copy-start.1 = (bf16[8,3,64,128]{3,2,1,0:T(8,128)(2,1)S(1)}, bf16[8,3,64,128]{3,2,1,0:T(8,128)(2,1)}, u32[]{:S(2)}) copy-start(bf16[8,3,64,128]{3,2,1,0:T(8,128)(2,1)} %get-tuple-element.23.refs_0_) | copy-start | bytes 1179652
  65.1 32.9 %copy-start.2 = (s32[48]{0:T(128)S(1)}, s32[48]{0:T(128)}, u32[]{:S(2)}) copy-start(s32[48]{0:T(128)} %labels.5) | copy-start | bytes 580
  73.8 21.4 %collective-permute-start.17 = (bf16[48,3,96,128]{3,2,1,0:T(8,128)(2,1)S(1)}, bf16[48,3,96,128]{3,2,1,0:T(8,128)(2,1)S(1)}, u32[]{:S(2)}, u32[]{:S(2)}) collective-permute-start(bf16[48,3,96,128]{3,2,1,0:T(8,128)(2,1)S(1)} %constant_dynamic-update-slice_fusion), channel_id=1, source_target_pairs={{0,16},{16,0},{32,48},{48,32},{64,80},{80,64},{96,112},{112,96},{1... | collective-permute-start | bytes 10616840 | tf_op jit(solution)/shard_map/ppermute | solution.py:337
  77.5 15.0 %collective-permute-start.19 = (bf16[8,3,96,128]{3,2,1,0:T(8,128)(2,1)S(1)}, bf16[8,3,96,128]{3,2,1,0:T(8,128)(2,1)S(1)}, u32[]{:S(2)}, u32[]{:S(2)}) collective-permute-start(bf16[8,3,96,128]{3,2,1,0:T(8,128)(2,1)S(1)} %collective-permute-done.14.refs_15_.refs_21_), channel_id=1, source_target_pairs={{0,192},{16,208},{32,224},{48,240},{64,0},{80,16},{96,32},{112,48}... | collective-permute-start | bytes 1769480 | tf_op jit(solution)/shard_map/ppermute | solution.py:337
  79.3 15.8 %collective-permute-start.18 = (bf16[8,3,96,128]{3,2,1,0:T(8,128)(2,1)S(1)}, bf16[8,3,96,128]{3,2,1,0:T(8,128)(2,1)S(1)}, u32[]{:S(2)}, u32[]{:S(2)}) collective-permute-start(bf16[8,3,96,128]{3,2,1,0:T(8,128)(2,1)S(1)} %collective-permute-done.4.refs_11_.refs_16_), channel_id=1, source_target_pairs={{0,64},{16,80},{32,96},{48,112},{64,128},{80,144},{96,160},{112,17... | collective-permute-start | bytes 1769480 | tf_op jit(solution)/shard_map/ppermute | solution.py:337
  79.3 15.9 %collective-permute-start.15 = (bf16[8,3,64,128]{3,2,1,0:T(8,128)(2,1)S(1)}, bf16[8,3,64,128]{3,2,1,0:T(8,128)(2,1)S(1)}, u32[]{:S(2)}, u32[]{:S(2)}) collective-permute-start(bf16[8,3,64,128]{3,2,1,0:T(8,128)(2,1)S(1)} %collective-permute-done.10.refs_3_), channel_id=1, source_target_pairs={{0,4},{1,5},{2,6},{3,7},{4,8},{5,9},{6,10},{7,11},{8,12},{9,13},{1... | collective-permute-start | bytes 1179656 | tf_op jit(solution)/shard_map/ppermute | solution.py:337
  79.3 15.9 %collective-permute-start.16 = (bf16[8,3,64,128]{3,2,1,0:T(8,128)(2,1)S(1)}, bf16[8,3,64,128]{3,2,1,0:T(8,128)(2,1)S(1)}, u32[]{:S(2)}, u32[]{:S(2)}) collective-permute-start(bf16[8,3,64,128]{3,2,1,0:T(8,128)(2,1)S(1)} %collective-permute-done.10.refs_3_), channel_id=1, source_target_pairs={{0,12},{1,13},{2,14},{3,15},{4,0},{5,1},{6,2},{7,3},{8,4},{9,5},{1... | collective-permute-start | bytes 1179656 | tf_op jit(solution)/shard_map/ppermute | solution.py:337
  95.2 11.1 %collective-permute-start.22 = (bf16[16,3,96,128]{3,2,1,0:T(8,128)(2,1)S(1)}, bf16[16,3,96,128]{3,2,1,0:T(8,128)(2,1)S(1)}, u32[]{:S(2)}, u32[]{:S(2)}) collective-permute-start(bf16[16,3,96,128]{3,2,1,0:T(8,128)(2,1)S(1)} %pad_maximum_fusion), channel_id=1, source_target_pairs={{0,16},{16,0},{32,48},{48,32},{64,80},{80,64},{96,112},{112,96},{1... | collective-permute-start | bytes 3538952 | tf_op jit(solution)/shard_map/ppermute | solution.py:337
  96.5 9.7 %collective-permute-start.21 = (bf16[4,3,64,128]{3,2,1,0:T(8,128)(2,1)S(1)}, bf16[4,3,64,128]{3,2,1,0:T(8,128)(2,1)S(1)}, u32[]{:S(2)}, u32[]{:S(2)}) collective-permute-start(bf16[4,3,64,128]{3,2,1,0:T(8,128)(2,1)S(1)} %slice.19), channel_id=1, source_target_pairs={{0,12},{1,13},{2,14},{3,15},{4,0},{5,1},{6,2},{7,3},{8,4},{9,5},{1... | collective-permute-start | bytes 589832 | tf_op jit(solution)/shard_map/ppermute | solution.py:337
  97.8 8.5 %collective-permute-start.20 = (bf16[4,3,64,128]{3,2,1,0:T(8,128)(2,1)S(1)}, bf16[4,3,64,128]{3,2,1,0:T(8,128)(2,1)S(1)}, u32[]{:S(2)}, u32[]{:S(2)}) collective-permute-start(bf16[4,3,64,128]{3,2,1,0:T(8,128)(2,1)S(1)} %slice.18), channel_id=1, source_target_pairs={{0,4},{1,5},{2,6},{3,7},{4,8},{5,9},{6,10},{7,11},{8,12},{9,13},{1... | collective-permute-start | bytes 589832 | tf_op jit(solution)/shard_map/ppermute | solution.py:337

commit v3 on v2

--- a/solution.py
+++ b/solution.py
@@ -6,6 +6,7 @@
 from jax.sharding import PartitionSpec as P
 
 NVI = 64
+UNROLL = 2
 MESH_X, MESH_Y, MESH_ZH, MESH_ZL = 4, 4, 2, 4
 CHUNKS = 16
 
@@ -46,17 +47,17 @@
 
 
 def spread(half):
-    row = lax.broadcasted_iota(jnp.int32, (512, 256), 0)
+    row = lax.broadcasted_iota(jnp.int32, (512, 1), 0)
+    want = jnp.where((row & 1) == half, ((row & 63) >> 1) * 8 + (row >> 6), -1)
     col = lax.broadcasted_iota(jnp.int32, (512, 256), 1)
-    want = ((row & 63) >> 1) * 8 + (row >> 6)
-    return jnp.where((col == want) & ((row & 1) == half), 1.0, 0.0).astype(jnp.bfloat16)
+    return jnp.where(col == want, 1.0, 0.0).astype(jnp.bfloat16)
 
 
 def gather_back(half):
+    col = lax.broadcasted_iota(jnp.int32, (1, 512), 1)
+    want = jnp.where((col & 1) == half, ((col & 63) >> 1) * 8 + (col >> 6), -1)
     row = lax.broadcasted_iota(jnp.int32, (256, 512), 0)
-    col = lax.broadcasted_iota(jnp.int32, (256, 512), 1)
-    want = ((col & 63) >> 1) * 8 + (col >> 6)
-    return jnp.where((row == want) & ((col & 1) == half), 1.0, 0.0).astype(jnp.bfloat16)
+    return jnp.where(row == want, 1.0, 0.0).astype(jnp.bfloat16)
 
 
 def stacked(flat):
@@ -126,12 +127,13 @@
         slot = jnp.where(mx == columns[0], 0, 4) + (zl ^ d)
         bring(amp_in[name].at[pl.ds(first, count)], amp.at[slot, pl.ds(h, count)], mx, 0)
     for half in range(2):
-        for name, first, (s, d, c) in lad_parts:
+        for name, first, (s, d, c), h, count in lad_parts:
+            if count == 4 and h != half * 4:
+                continue
             mx = (x + 4 - s) % 4
+            first = first + half * 4 - h
             slot = jnp.where(mx == columns[0], 0, 4) + (zh ^ d) * 2 + (core ^ c)
-            bring(
-                lad_in[name].at[pl.ds(first + half * 4, 4)], lad.at[slot, pl.ds(half * 4, 4)], mx, half
-            )
+            bring(lad_in[name].at[pl.ds(first, 4)], lad.at[slot, pl.ds(half * 4, 4)], mx, half)
     for copy, wanted, _ in copies:
         pl.when(wanted)(copy.start)
 
@@ -172,7 +174,7 @@
         for copy, wanted, group in copies:
             if group == half:
                 pl.when(wanted)(copy.wait)
-        lax.fori_loop(half * 4, half * 4 + 4, block, 0)
+        lax.fori_loop(half * 4, half * 4 + 4, block, 0, unroll=UNROLL)
 
 
 def early_products(labels, *refs):
@@ -227,14 +229,15 @@
     ("yo+", 0, (1, 0), 0, 8), ("yo-", 0, (3, 0), 0, 8), ("fo", 0, (2, 0), 0, 8),
     ("yq+", 0, (1, 1), 0, 8), ("yq+", 8, (1, 2), 0, 8), ("yq-", 0, (3, 1), 0, 8), ("yq-", 8, (3, 2), 0, 8),
     ("f1", 0, (2, 1), 0, 8), ("f2", 0, (2, 2), 0, 8),
-    ("y3+", 0, (1, 3), 0, 8), ("y3-", 0, (3, 3), 0, 8), ("f3a", 0, (2, 3), 0, 4), ("f3b", 0, (2, 3), 4, 4),
+    ("y3+", 0, (1, 3), 0, 8), ("y3-", 0, (3, 3), 0, 8), ("f3", 0, (2, 3), 0, 8),
 ]
 LAD_PARTS = [
-    ("l", 0, (0, 0, 0)), ("xo+", 0, (1, 0, 0)), ("xo-", 0, (3, 0, 0)), ("fxo", 0, (2, 0, 0)),
-    ("zh", 0, (0, 1, 0)), ("xz+", 0, (1, 1, 0)), ("xz-", 0, (3, 1, 0)), ("fxz", 0, (2, 1, 0)),
-    ("c1", 0, (0, 0, 1)), ("c1", 8, (1, 0, 1)), ("c1", 16, (3, 0, 1)),
-    ("c1", 24, (0, 1, 1)), ("c1", 32, (1, 1, 1)), ("c1", 40, (3, 1, 1)),
-    ("c2", 0, (2, 0, 1)), ("c2", 8, (2, 1, 1)),
+    ("l", 0, (0, 0, 0), 0, 8), ("xo+", 0, (1, 0, 0), 0, 8), ("xo-", 0, (3, 0, 0), 0, 8), ("fxo", 0, (2, 0, 0), 0, 8),
+    ("zh", 0, (0, 1, 0), 0, 8), ("xz+", 0, (1, 1, 0), 0, 8), ("xz-", 0, (3, 1, 0), 0, 8),
+    ("fxz+", 0, (2, 1, 0), 0, 4), ("fxz-", 0, (2, 1, 0), 4, 4),
+    ("c1", 0, (0, 0, 1), 0, 8), ("c1", 8, (1, 0, 1), 0, 8), ("c1", 16, (3, 0, 1), 0, 8),
+    ("c1", 24, (0, 1, 1), 0, 8), ("c1", 32, (1, 1, 1), 0, 8), ("c1", 40, (3, 1, 1), 0, 8),
+    ("c2", 0, (2, 0, 1), 0, 8), ("c2", 8, (2, 1, 1), 0, 8),
 ]
 AMP_NAMES = list(dict.fromkeys(part[0] for part in AMP_PARTS))
 LAD_NAMES = list(dict.fromkeys(part[0] for part in LAD_PARTS))
@@ -254,8 +257,8 @@
     ("zh", "l", Z_HALF, 1, 2),
     ("yq+", ("z1", "z2"), Y_UP, 1, 2),
     ("yq-", ("z1", "z2"), Y_DOWN, 1, 2),
-    ("fo", "yo+", Y_UP, 1, 2),
     ("xo-", "l", X_DOWN, 1, 2),
+    ("fxo", "xo+", X_UP, 1, 2),
     ("z3", "z2", Z_ONE, 2, 3),
     ("f1", ("yq+", 0, 8), Y_UP, 2, 3),
     ("f2", ("yq-", 8, 16), Y_DOWN, 2, 3),
@@ -263,12 +266,12 @@
     ("xz-", "zh", X_DOWN, 2, 3),
     ("y3+", "z3", Y_UP, 3, 4),
     ("y3-", "z3", Y_DOWN, 3, 4),
-    ("fxo", "xo+", X_UP, 3, 4),
-    ("fxz", "xz-", X_DOWN, 3, 4),
+    ("fxz+", ("xz+", 0, 4), X_UP, 3, 4),
+    ("fxz-", ("xz-", 4, 8), X_DOWN, 3, 4),
     ("c1", ("l", "xo+", "xo-", "zh", "xz+", "xz-"), OTHER_CORE, 3, 4),
-    ("f3a", ("y3+", 0, 4), Y_UP, 4, 5),
-    ("f3b", ("y3-", 4, 8), Y_DOWN, 4, 5),
-    ("c2", ("fxo", "fxz"), OTHER_CORE, 4, 5),
+    ("f3", "y3+", Y_UP, 4, 5),
+    ("fo", "yo-", Y_DOWN, 4, 5),
+    ("c2", ("fxo", "fxz+", "fxz-"), OTHER_CORE, 4, 5),
 ]
 JOINS = {}
 

time: 117 us -> 114 us (0.974)
  the two profiles are of different devices: /device:TPU:97 before, /device:TPU:102 now
where the time goes in v3:
time: 114 us
  waiting for transfers between devices  61.3 us (54%)
  starting transfers between devices  29.9 us (26%)
  Pallas kernels  20.7 us (18%)
  local copies, waits for them, and re-layouts  1.6 us (1%)
    ppermute x23, waiting for transfers between devices, on_device(): got[name] = lax.ppermute(value, axis, pairs)  61.3 us
    ppermute x23, starting transfers between devices, on_device(): got[name] = lax.ppermute(value, axis, pairs)  29.9 us
    pallas_call x3, Pallas kernels, call(): pl.pallas_call(kernel, out_shape=outs, in_specs=[pl.BlockSpec(memory_spac...  20.7 us
  transfers between devices with their start and end apart: 23, of which 7 were waited for; matrix products, arithmetic and copies ran while one was open for 2% of the time, Pallas kernels for 6%

profile of v3, /device:TPU:102, one launch (start us, length us, event | category | flops | bytes accessed | tf_op | source)
XLA Modules:
  0.0 114.1 jit_solution(6891876207498854332)
XLA Ops:
  0.0 4.2 %shard_map.46 = (bf16[8,3,64,128]{3,2,1,0:T(8,128)(2,1)}, bf16[8,3,96,128]{3,2,1,0:T(8,128)(2,1)}) custom-call(s32[48]{0:T(128)} %labels.5, bf16[2,3,8,4096]{3,2,1,0:T(8,128)(2,1)} %amp_in.1, bf16[3,3,8,4096]{3,2,1,0:T(8,128)(2,1)} %coul_in.1, bf16[3,3,8,4096]{3,2,1,0:T(8,128)(2,1)} %exch_in.1), custom_call_target="tpu_custom_call" | custom-call | flops 2000000000 | bytes 3000000 | tf_op jit(solution)/shard_map/pallas_call | solution.py:280
  4.2 0.6 collective-permute-start.4
  4.7 0.0 collective-permute-start.1
  4.7 1.5 %collective-permute-start = (bf16[8,3,64,128]{3,2,1,0:T(8,128)(2,1)}, bf16[8,3,64,128]{3,2,1,0:T(8,128)(2,1)S(1)}, u32[]{:S(2)}, u32[]{:S(2)}) collective-permute-start(bf16[8,3,64,128]{3,2,1,0:T(8,128)(2,1)} %get-tuple-element.23.refs_0_), channel_id=1, source_target_pairs={{0,1},{1,0},{2,3},{3,2},{4,5},{5,4},{6,7},{7,6},{8,9},{9,8},{10,11... | collective-permute-start | bytes 1179656 | tf_op jit(solution)/shard_map/ppermute | solution.py:340
  6.2 1.6 %collective-permute-start.3 = (bf16[8,3,64,128]{3,2,1,0:T(8,128)(2,1)}, bf16[8,3,64,128]{3,2,1,0:T(8,128)(2,1)S(1)}, u32[]{:S(2)}, u32[]{:S(2)}) collective-permute-start(bf16[8,3,64,128]{3,2,1,0:T(8,128)(2,1)} %get-tuple-element.23.refs_0_), channel_id=1, source_target_pairs={{0,12},{1,13},{2,14},{3,15},{4,0},{5,1},{6,2},{7,3},{8,4},{9,5},{1... | collective-permute-start | bytes 1179656 | tf_op jit(solution)/shard_map/ppermute | solution.py:340
  7.8 0.4 collective-permute-start.2
  8.2 16.1 %collective-permute-done.1.refs_2_ = bf16[8,3,64,128]{3,2,1,0:T(8,128)(2,1)S(1)} collective-permute-done((bf16[8,3,64,128]{3,2,1,0:T(8,128)(2,1)}, bf16[8,3,64,128]{3,2,1,0:T(8,128)(2,1)S(1)}, u32[]{:S(2)}, u32[]{:S(2)}) %collective-permute-start.1) | collective-permute-done | bytes 393248 | tf_op jit(solution)/shard_map/ppermute | solution.py:340
  24.4 0.0 collective-permute-done.refs_1_
  24.4 0.1 pad_maximum_fusion.1
  24.4 0.0 collective-permute-done.3.refs_5_
  24.5 0.0 collective-permute-done.2.refs_4_
  24.5 0.0 collective-permute-done.4.refs_11_.refs_15_
  24.5 1.7 %collective-permute-start.6 = (bf16[16,3,64,128]{3,2,1,0:T(8,128)(2,1)S(1)}, bf16[16,3,64,128]{3,2,1,0:T(8,128)(2,1)S(1)}, u32[]{:S(2)}, u32[]{:S(2)}) collective-permute-start(bf16[16,3,64,128]{3,2,1,0:T(8,128)(2,1)S(1)} %pad_maximum_fusion.1), channel_id=1, source_target_pairs={{0,4},{1,5},{2,6},{3,7},{4,8},{5,9},{6,10},{7,11},{8,12},{9,13},{1... | collective-permute-start | bytes 2359304 | tf_op jit(solution)/shard_map/ppermute | solution.py:340
  26.1 1.7 %collective-permute-start.7 = (bf16[16,3,64,128]{3,2,1,0:T(8,128)(2,1)S(1)}, bf16[16,3,64,128]{3,2,1,0:T(8,128)(2,1)S(1)}, u32[]{:S(2)}, u32[]{:S(2)}) collective-permute-start(bf16[16,3,64,128]{3,2,1,0:T(8,128)(2,1)S(1)} %pad_maximum_fusion.1), channel_id=1, source_target_pairs={{0,12},{1,13},{2,14},{3,15},{4,0},{5,1},{6,2},{7,3},{8,4},{9,5},{1... | collective-permute-start | bytes 2359304 | tf_op jit(solution)/shard_map/ppermute | solution.py:340
  27.8 4.9 %collective-permute-start.5 = (bf16[8,3,96,128]{3,2,1,0:T(8,128)(2,1)}, bf16[8,3,96,128]{3,2,1,0:T(8,128)(2,1)S(1)}, u32[]{:S(2)}, u32[]{:S(2)}) collective-permute-start(bf16[8,3,96,128]{3,2,1,0:T(8,128)(2,1)} %get-tuple-element.25.refs_10_.refs_14_), channel_id=1, source_target_pairs={{0,32},{16,48},{32,0},{48,16},{64,96},{80,112},{96,64},{112,80},{1... | collective-permute-start | bytes 1769480 | tf_op jit(solution)/shard_map/ppermute | solution.py:340
  32.7 1.5 %collective-permute-start.8 = (bf16[8,3,96,128]{3,2,1,0:T(8,128)(2,1)}, bf16[8,3,96,128]{3,2,1,0:T(8,128)(2,1)S(1)}, u32[]{:S(2)}, u32[]{:S(2)}) collective-permute-start(bf16[8,3,96,128]{3,2,1,0:T(8,128)(2,1)} %get-tuple-element.25.refs_10_.refs_14_), channel_id=1, source_target_pairs={{0,192},{16,208},{32,224},{48,240},{64,0},{80,16},{96,32},{112,48}... | collective-permute-start | bytes 1769480 | tf_op jit(solution)/shard_map/ppermute | solution.py:340
  34.3 1.7 %collective-permute-start.9 = (bf16[8,3,96,128]{3,2,1,0:T(8,128)(2,1)S(1)}, bf16[8,3,96,128]{3,2,1,0:T(8,128)(2,1)S(1)}, u32[]{:S(2)}, u32[]{:S(2)}) collective-permute-start(bf16[8,3,96,128]{3,2,1,0:T(8,128)(2,1)S(1)} %collective-permute-done.4.refs_11_.refs_15_), channel_id=1, source_target_pairs={{0,64},{16,80},{32,96},{48,112},{64,128},{80,144},{96,160},{112,17... | collective-permute-start | bytes 1769480 | tf_op jit(solution)/shard_map/ppermute | solution.py:340
  36.0 23.5 %collective-permute-done.5.refs_13_.refs_18_ = bf16[8,3,96,128]{3,2,1,0:T(8,128)(2,1)S(1)} collective-permute-done((bf16[8,3,96,128]{3,2,1,0:T(8,128)(2,1)}, bf16[8,3,96,128]{3,2,1,0:T(8,128)(2,1)S(1)}, u32[]{:S(2)}, u32[]{:S(2)}) %collective-permute-start.5) | collective-permute-done | bytes 589856 | tf_op jit(solution)/shard_map/ppermute | solution.py:340
  59.5 0.0 collective-permute-done.8.refs_12_.refs_16_
  59.5 0.0 collective-permute-done.9.refs_17_
  59.5 0.0 collective-permute-done.6.refs_6_.refs_7_
  59.5 0.0 collective-permute-done.7.refs_7_.refs_8_
  59.5 1.6 %collective-permute-start.13 = (bf16[8,3,96,128]{3,2,1,0:T(8,128)(2,1)S(1)}, bf16[8,3,96,128]{3,2,1,0:T(8,128)(2,1)S(1)}, u32[]{:S(2)}, u32[]{:S(2)}) collective-permute-start(bf16[8,3,96,128]{3,2,1,0:T(8,128)(2,1)S(1)} %collective-permute-done.5.refs_13_.refs_18_), channel_id=1, source_target_pairs={{0,64},{16,80},{32,96},{48,112},{64,128},{80,144},{96,160},{112,17... | collective-permute-start | bytes 1769480 | tf_op jit(solution)/shard_map/ppermute | solution.py:340
  61.1 0.5 collective-permute-start.14
  61.6 1.1 constant_dynamic-update-slice_fusion.5
  62.7 0.1 constant_dynamic-update-slice_fusion.4
  62.9 1.7 %collective-permute-start.12 = (bf16[8,3,64,128]{3,2,1,0:T(8,128)(2,1)S(1)}, bf16[8,3,64,128]{3,2,1,0:T(8,128)(2,1)S(1)}, u32[]{:S(2)}, u32[]{:S(2)}) collective-permute-start(bf16[8,3,64,128]{3,2,1,0:T(8,128)(2,1)S(1)} %slice.17), channel_id=1, source_target_pairs={{0,12},{1,13},{2,14},{3,15},{4,0},{5,1},{6,2},{7,3},{8,4},{9,5},{1... | collective-permute-start | bytes 1179656 | tf_op jit(solution)/shard_map/ppermute | solution.py:340
  64.6 0.5 collective-permute-start.11
  65.1 0.0 collective-permute-start.10
  65.1 0.1 constant_dynamic-update-slice_fusion.3
  65.2 0.0 copy-start
  65.2 0.0 copy-start.1
  65.2 0.0 copy-start.2
  65.2 0.1 constant_dynamic-update-slice_fusion.2
  65.3 8.2 %collective-permute-done.13.refs_14_.refs_19_ = bf16[8,3,96,128]{3,2,1,0:T(8,128)(2,1)S(1)} collective-permute-done((bf16[8,3,96,128]{3,2,1,0:T(8,128)(2,1)S(1)}, bf16[8,3,96,128]{3,2,1,0:T(8,128)(2,1)S(1)}, u32[]{:S(2)}, u32[]{:S(2)}) %collective-permute-start.13) | collective-permute-done | bytes 589856 | tf_op jit(solution)/shard_map/ppermute | solution.py:340
  73.5 0.1 constant_dynamic-update-slice_fusion.1
  73.6 2.3 %collective-permute-done.14.refs_15_.refs_20_ = bf16[8,3,96,128]{3,2,1,0:T(8,128)(2,1)S(1)} collective-permute-done((bf16[8,3,96,128]{3,2,1,0:T(8,128)(2,1)S(1)}, bf16[8,3,96,128]{3,2,1,0:T(8,128)(2,1)S(1)}, u32[]{:S(2)}, u32[]{:S(2)}) %collective-permute-start.14) | collective-permute-done | bytes 589856 | tf_op jit(solution)/shard_map/ppermute | solution.py:340
  75.9 0.1 constant_dynamic-update-slice_fusion
  76.0 0.0 collective-permute-done.12.refs_10_
  76.0 0.0 collective-permute-done.11.refs_9_
  76.0 0.0 collective-permute-done.10.refs_3_
  76.0 0.1 collective-permute-start.17
  76.1 0.1 collective-permute-start.19
  76.3 3.3 %collective-permute-start.18 = (bf16[4,3,96,128]{3,2,1,0:T(8,128)(2,1)S(1)}, bf16[4,3,96,128]{3,2,1,0:T(8,128)(2,1)S(1)}, u32[]{:S(2)}, u32[]{:S(2)}) collective-permute-start(bf16[4,3,96,128]{3,2,1,0:T(8,128)(2,1)S(1)} %slice.18), channel_id=1, source_target_pairs={{0,64},{16,80},{32,96},{48,112},{64,128},{80,144},{96,160},{112,17... | collective-permute-start | bytes 884744 | tf_op jit(solution)/shard_map/ppermute | solution.py:340
  79.6 0.1 collective-permute-start.15
  79.6 3.2 %collective-permute-start.16 = (bf16[8,3,64,128]{3,2,1,0:T(8,128)(2,1)S(1)}, bf16[8,3,64,128]{3,2,1,0:T(8,128)(2,1)S(1)}, u32[]{:S(2)}, u32[]{:S(2)}) collective-permute-start(bf16[8,3,64,128]{3,2,1,0:T(8,128)(2,1)S(1)} %collective-permute-done.10.refs_3_), channel_id=1, source_target_pairs={{0,12},{1,13},{2,14},{3,15},{4,0},{5,1},{6,2},{7,3},{8,4},{9,5},{1... | collective-permute-start | bytes 1179656 | tf_op jit(solution)/shard_map/ppermute | solution.py:340
  82.8 4.0 %collective-permute-done.19.refs_22_ = bf16[4,3,96,128]{3,2,1,0:T(8,128)(2,1)S(1)} collective-permute-done((bf16[4,3,96,128]{3,2,1,0:T(8,128)(2,1)S(1)}, bf16[4,3,96,128]{3,2,1,0:T(8,128)(2,1)S(1)}, u32[]{:S(2)}, u32[]{:S(2)}) %collective-permute-start.19) | collective-permute-done | bytes 294944 | tf_op jit(solution)/shard_map/ppermute | solution.py:340
  86.8 0.0 collective-permute-done.18.refs_21_
  86.8 0.1 pad_maximum_fusion
  87.0 4.7 %collective-permute-done.15.refs_8_.refs_11_ = bf16[8,3,64,128]{3,2,1,0:T(8,128)(2,1)S(1)} collective-permute-done((bf16[8,3,64,128]{3,2,1,0:T(8,128)(2,1)S(1)}, bf16[8,3,64,128]{3,2,1,0:T(8,128)(2,1)S(1)}, u32[]{:S(2)}, u32[]{:S(2)}) %collective-permute-start.15) | collective-permute-done | bytes 393248 | tf_op jit(solution)/shard_map/ppermute | solution.py:340
  91.7 0.0 collective-permute-done.16.refs_9_.refs_12_
  91.7 0.0 collective-permute-done.17.refs_16_.refs_23_
  91.7 0.0 collective-permute-start.22
  91.7 0.1 collective-permute-start.21
  91.9 3.2 %collective-permute-start.20 = (bf16[8,3,64,128]{3,2,1,0:T(8,128)(2,1)S(1)}, bf16[8,3,64,128]{3,2,1,0:T(8,128)(2,1)S(1)}, u32[]{:S(2)}, u32[]{:S(2)}) collective-permute-start(bf16[8,3,64,128]{3,2,1,0:T(8,128)(2,1)S(1)} %collective-permute-done.3.refs_5_), channel_id=1, source_target_pairs={{0,12},{1,13},{2,14},{3,15},{4,0},{5,1},{6,2},{7,3},{8,4},{9,5},{1... | collective-permute-start | bytes 1179656 | tf_op jit(solution)/shard_map/ppermute | solution.py:340
  95.0 0.0 copy-done
  95.1 0.0 copy-done.1
  95.1 0.0 copy-done.2
  95.1 7.2 %shard_map.47 = (f32[8,128,256]{2,1,0:T(8,128)S(1)}, f32[8,128,256]{2,1,0:T(8,128)S(1)}) custom-call(s32[48]{0:T(128)S(1)} %copy-done.2, bf16[8,3,64,128]{3,2,1,0:T(8,128)(2,1)S(1)} %copy-done.1, bf16[8,3,64,128]{3,2,1,0:T(8,128)(2,1)S(1)} %collective-permute-done.refs_1_, bf16[8,3,64,128]{3,2,1,0:T(8,128)(2,1)S(1)} %collective-permute-done.1.refs_2_, ...), custom_call_target="tpu_custom_call" | custom-call | flops 5000000000 | bytes 8000000 | tf_op jit(solution)/shard_map/pallas_call | solution.py:280
  102.2 2.2 %collective-permute-done.21.refs_13_ = bf16[8,3,64,128]{3,2,1,0:T(8,128)(2,1)S(1)} collective-permute-done((bf16[8,3,64,128]{3,2,1,0:T(8,128)(2,1)S(1)}, bf16[8,3,64,128]{3,2,1,0:T(8,128)(2,1)S(1)}, u32[]{:S(2)}, u32[]{:S(2)}) %collective-permute-start.21) | collective-permute-done | bytes 393248 | tf_op jit(solution)/shard_map/ppermute | solution.py:340
  104.5 0.0 collective-permute-done.20.refs_6_
  104.5 0.0 collective-permute-done.22.refs_24_
  104.5 9.4 %shard_map.48 = bf16[2,3,8,4096]{3,2,1,0:T(8,128)(2,1)} custom-call(s32[48]{0:T(128)S(1)} %copy-done.2, f32[8,128,256]{2,1,0:T(8,128)S(1)} %get-tuple-element.34.first_in, f32[8,128,256]{2,1,0:T(8,128)S(1)} %get-tuple-element.35.second_in, bf16[8,3,64,128]{3,2,1,0:T(8,128)(2,1)S(1)} %copy-done.1, bf16[8,3,64,128]{3,2,1,0:T(8,128)(2,1)S(1)} %collective-permute-done.refs_1_, ...), custom_call_target="tpu_custom_call" | custom-call | flops 5000000000 | bytes 8000000 | tf_op jit(solution)/shard_map/pallas_call | solution.py:280
  (4 shorter events, 0.1 us)
Async XLA Ops:
  4.2 20.3 %collective-permute-start.4 = (bf16[8,3,96,128]{3,2,1,0:T(8,128)(2,1)}, bf16[8,3,96,128]{3,2,1,0:T(8,128)(2,1)S(1)}, u32[]{:S(2)}, u32[]{:S(2)}) collective-permute-start(bf16[8,3,96,128]{3,2,1,0:T(8,128)(2,1)} %get-tuple-element.25.refs_10_.refs_14_), channel_id=1, source_target_pairs={{0,64},{16,80},{32,96},{48,112},{64,128},{80,144},{96,160},{112,17... | collective-permute-start | bytes 1769480 | tf_op jit(solution)/shard_map/ppermute | solution.py:340
  4.7 19.7 %collective-permute-start.1 = (bf16[8,3,64,128]{3,2,1,0:T(8,128)(2,1)}, bf16[8,3,64,128]{3,2,1,0:T(8,128)(2,1)S(1)}, u32[]{:S(2)}, u32[]{:S(2)}) collective-permute-start(bf16[8,3,64,128]{3,2,1,0:T(8,128)(2,1)} %get-tuple-element.23.refs_0_), channel_id=1, source_target_pairs={{0,2},{1,3},{2,0},{3,1},{4,6},{5,7},{6,4},{7,5},{8,10},{9,11},{10,... | collective-permute-start | bytes 1179656 | tf_op jit(solution)/shard_map/ppermute | solution.py:340
  4.7 19.7 %collective-permute-start = (bf16[8,3,64,128]{3,2,1,0:T(8,128)(2,1)}, bf16[8,3,64,128]{3,2,1,0:T(8,128)(2,1)S(1)}, u32[]{:S(2)}, u32[]{:S(2)}) collective-permute-start(bf16[8,3,64,128]{3,2,1,0:T(8,128)(2,1)} %get-tuple-element.23.refs_0_), channel_id=1, source_target_pairs={{0,1},{1,0},{2,3},{3,2},{4,5},{5,4},{6,7},{7,6},{8,9},{9,8},{10,11... | collective-permute-start | bytes 1179656 | tf_op jit(solution)/shard_map/ppermute | solution.py:340
  6.2 18.2 %collective-permute-start.3 = (bf16[8,3,64,128]{3,2,1,0:T(8,128)(2,1)}, bf16[8,3,64,128]{3,2,1,0:T(8,128)(2,1)S(1)}, u32[]{:S(2)}, u32[]{:S(2)}) collective-permute-start(bf16[8,3,64,128]{3,2,1,0:T(8,128)(2,1)} %get-tuple-element.23.refs_0_), channel_id=1, source_target_pairs={{0,12},{1,13},{2,14},{3,15},{4,0},{5,1},{6,2},{7,3},{8,4},{9,5},{1... | collective-permute-start | bytes 1179656 | tf_op jit(solution)/shard_map/ppermute | solution.py:340
  7.8 16.6 %collective-permute-start.2 = (bf16[8,3,64,128]{3,2,1,0:T(8,128)(2,1)}, bf16[8,3,64,128]{3,2,1,0:T(8,128)(2,1)S(1)}, u32[]{:S(2)}, u32[]{:S(2)}) collective-permute-start(bf16[8,3,64,128]{3,2,1,0:T(8,128)(2,1)} %get-tuple-element.23.refs_0_), channel_id=1, source_target_pairs={{0,4},{1,5},{2,6},{3,7},{4,8},{5,9},{6,10},{7,11},{8,12},{9,13},{1... | collective-permute-start | bytes 1179656 | tf_op jit(solution)/shard_map/ppermute | solution.py:340
  24.5 35.0 %collective-permute-start.6 = (bf16[16,3,64,128]{3,2,1,0:T(8,128)(2,1)S(1)}, bf16[16,3,64,128]{3,2,1,0:T(8,128)(2,1)S(1)}, u32[]{:S(2)}, u32[]{:S(2)}) collective-permute-start(bf16[16,3,64,128]{3,2,1,0:T(8,128)(2,1)S(1)} %pad_maximum_fusion.1), channel_id=1, source_target_pairs={{0,4},{1,5},{2,6},{3,7},{4,8},{5,9},{6,10},{7,11},{8,12},{9,13},{1... | collective-permute-start | bytes 2359304 | tf_op jit(solution)/shard_map/ppermute | solution.py:340
  26.1 33.4 %collective-permute-start.7 = (bf16[16,3,64,128]{3,2,1,0:T(8,128)(2,1)S(1)}, bf16[16,3,64,128]{3,2,1,0:T(8,128)(2,1)S(1)}, u32[]{:S(2)}, u32[]{:S(2)}) collective-permute-start(bf16[16,3,64,128]{3,2,1,0:T(8,128)(2,1)S(1)} %pad_maximum_fusion.1), channel_id=1, source_target_pairs={{0,12},{1,13},{2,14},{3,15},{4,0},{5,1},{6,2},{7,3},{8,4},{9,5},{1... | collective-permute-start | bytes 2359304 | tf_op jit(solution)/shard_map/ppermute | solution.py:340
  27.8 31.7 %collective-permute-start.5 = (bf16[8,3,96,128]{3,2,1,0:T(8,128)(2,1)}, bf16[8,3,96,128]{3,2,1,0:T(8,128)(2,1)S(1)}, u32[]{:S(2)}, u32[]{:S(2)}) collective-permute-start(bf16[8,3,96,128]{3,2,1,0:T(8,128)(2,1)} %get-tuple-element.25.refs_10_.refs_14_), channel_id=1, source_target_pairs={{0,32},{16,48},{32,0},{48,16},{64,96},{80,112},{96,64},{112,80},{1... | collective-permute-start | bytes 1769480 | tf_op jit(solution)/shard_map/ppermute | solution.py:340
  32.7 26.8 %collective-permute-start.8 = (bf16[8,3,96,128]{3,2,1,0:T(8,128)(2,1)}, bf16[8,3,96,128]{3,2,1,0:T(8,128)(2,1)S(1)}, u32[]{:S(2)}, u32[]{:S(2)}) collective-permute-start(bf16[8,3,96,128]{3,2,1,0:T(8,128)(2,1)} %get-tuple-element.25.refs_10_.refs_14_), channel_id=1, source_target_pairs={{0,192},{16,208},{32,224},{48,240},{64,0},{80,16},{96,32},{112,48}... | collective-permute-start | bytes 1769480 | tf_op jit(solution)/shard_map/ppermute | solution.py:340
  34.3 25.2 %collective-permute-start.9 = (bf16[8,3,96,128]{3,2,1,0:T(8,128)(2,1)S(1)}, bf16[8,3,96,128]{3,2,1,0:T(8,128)(2,1)S(1)}, u32[]{:S(2)}, u32[]{:S(2)}) collective-permute-start(bf16[8,3,96,128]{3,2,1,0:T(8,128)(2,1)S(1)} %collective-permute-done.4.refs_11_.refs_15_), channel_id=1, source_target_pairs={{0,64},{16,80},{32,96},{48,112},{64,128},{80,144},{96,160},{112,17... | collective-permute-start | bytes 1769480 | tf_op jit(solution)/shard_map/ppermute | solution.py:340
  59.5 13.9 %collective-permute-start.13 = (bf16[8,3,96,128]{3,2,1,0:T(8,128)(2,1)S(1)}, bf16[8,3,96,128]{3,2,1,0:T(8,128)(2,1)S(1)}, u32[]{:S(2)}, u32[]{:S(2)}) collective-permute-start(bf16[8,3,96,128]{3,2,1,0:T(8,128)(2,1)S(1)} %collective-permute-done.5.refs_13_.refs_18_), channel_id=1, source_target_pairs={{0,64},{16,80},{32,96},{48,112},{64,128},{80,144},{96,160},{112,17... | collective-permute-start | bytes 1769480 | tf_op jit(solution)/shard_map/ppermute | solution.py:340
  61.1 14.8 %collective-permute-start.14 = (bf16[8,3,96,128]{3,2,1,0:T(8,128)(2,1)S(1)}, bf16[8,3,96,128]{3,2,1,0:T(8,128)(2,1)S(1)}, u32[]{:S(2)}, u32[]{:S(2)}) collective-permute-start(bf16[8,3,96,128]{3,2,1,0:T(8,128)(2,1)S(1)} %collective-permute-done.5.refs_13_.refs_18_), channel_id=1, source_target_pairs={{0,192},{16,208},{32,224},{48,240},{64,0},{80,16},{96,32},{112,48}... | collective-permute-start | bytes 1769480 | tf_op jit(solution)/shard_map/ppermute | solution.py:340
  62.9 13.1 %collective-permute-start.12 = (bf16[8,3,64,128]{3,2,1,0:T(8,128)(2,1)S(1)}, bf16[8,3,64,128]{3,2,1,0:T(8,128)(2,1)S(1)}, u32[]{:S(2)}, u32[]{:S(2)}) collective-permute-start(bf16[8,3,64,128]{3,2,1,0:T(8,128)(2,1)S(1)} %slice.17), channel_id=1, source_target_pairs={{0,12},{1,13},{2,14},{3,15},{4,0},{5,1},{6,2},{7,3},{8,4},{9,5},{1... | collective-permute-start | bytes 1179656 | tf_op jit(solution)/shard_map/ppermute | solution.py:340
  64.6 11.4 %collective-permute-start.11 = (bf16[8,3,64,128]{3,2,1,0:T(8,128)(2,1)S(1)}, bf16[8,3,64,128]{3,2,1,0:T(8,128)(2,1)S(1)}, u32[]{:S(2)}, u32[]{:S(2)}) collective-permute-start(bf16[8,3,64,128]{3,2,1,0:T(8,128)(2,1)S(1)} %slice.16), channel_id=1, source_target_pairs={{0,4},{1,5},{2,6},{3,7},{4,8},{5,9},{6,10},{7,11},{8,12},{9,13},{1... | collective-permute-start | bytes 1179656 | tf_op jit(solution)/shard_map/ppermute | solution.py:340
  65.1 10.9 %collective-permute-start.10 = (bf16[8,3,64,128]{3,2,1,0:T(8,128)(2,1)S(1)}, bf16[8,3,64,128]{3,2,1,0:T(8,128)(2,1)S(1)}, u32[]{:S(2)}, u32[]{:S(2)}) collective-permute-start(bf16[8,3,64,128]{3,2,1,0:T(8,128)(2,1)S(1)} %collective-permute-done.1.refs_2_), channel_id=1, source_target_pairs={{0,1},{1,0},{2,3},{3,2},{4,5},{5,4},{6,7},{7,6},{8,9},{9,8},{10,11... | collective-permute-start | bytes 1179656 | tf_op jit(solution)/shard_map/ppermute | solution.py:340
  65.2 29.9 %copy-start = (bf16[8,3,96,128]{3,2,1,0:T(8,128)(2,1)S(1)}, bf16[8,3,96,128]{3,2,1,0:T(8,128)(2,1)}, u32[]{:S(2)}) copy-start(bf16[8,3,96,128]{3,2,1,0:T(8,128)(2,1)} %get-tuple-element.25.refs_10_.refs_14_) | copy-start | bytes 1769476
  65.2 29.9 %copy-start.1 = (bf16[8,3,64,128]{3,2,1,0:T(8,128)(2,1)S(1)}, bf16[8,3,64,128]{3,2,1,0:T(8,128)(2,1)}, u32[]{:S(2)}) copy-start(bf16[8,3,64,128]{3,2,1,0:T(8,128)(2,1)} %get-tuple-element.23.refs_0_) | copy-start | bytes 1179652
  65.2 29.9 %copy-start.2 = (s32[48]{0:T(128)S(1)}, s32[48]{0:T(128)}, u32[]{:S(2)}) copy-start(s32[48]{0:T(128)} %labels.5) | copy-start | bytes 580
  76.0 15.7 %collective-permute-start.17 = (bf16[48,3,96,128]{3,2,1,0:T(8,128)(2,1)S(1)}, bf16[48,3,96,128]{3,2,1,0:T(8,128)(2,1)S(1)}, u32[]{:S(2)}, u32[]{:S(2)}) collective-permute-start(bf16[48,3,96,128]{3,2,1,0:T(8,128)(2,1)S(1)} %constant_dynamic-update-slice_fusion), channel_id=1, source_target_pairs={{0,16},{16,0},{32,48},{48,32},{64,80},{80,64},{96,112},{112,96},{1... | collective-permute-start | bytes 10616840 | tf_op jit(solution)/shard_map/ppermute | solution.py:340
  76.1 10.7 %collective-permute-start.19 = (bf16[4,3,96,128]{3,2,1,0:T(8,128)(2,1)S(1)}, bf16[4,3,96,128]{3,2,1,0:T(8,128)(2,1)S(1)}, u32[]{:S(2)}, u32[]{:S(2)}) collective-permute-start(bf16[4,3,96,128]{3,2,1,0:T(8,128)(2,1)S(1)} %slice.19), channel_id=1, source_target_pairs={{0,192},{16,208},{32,224},{48,240},{64,0},{80,16},{96,32},{112,48}... | collective-permute-start | bytes 884744 | tf_op jit(solution)/shard_map/ppermute | solution.py:340
  76.3 10.6 %collective-permute-start.18 = (bf16[4,3,96,128]{3,2,1,0:T(8,128)(2,1)S(1)}, bf16[4,3,96,128]{3,2,1,0:T(8,128)(2,1)S(1)}, u32[]{:S(2)}, u32[]{:S(2)}) collective-permute-start(bf16[4,3,96,128]{3,2,1,0:T(8,128)(2,1)S(1)} %slice.18), channel_id=1, source_target_pairs={{0,64},{16,80},{32,96},{48,112},{64,128},{80,144},{96,160},{112,17... | collective-permute-start | bytes 884744 | tf_op jit(solution)/shard_map/ppermute | solution.py:340
  79.6 12.2 %collective-permute-start.15 = (bf16[8,3,64,128]{3,2,1,0:T(8,128)(2,1)S(1)}, bf16[8,3,64,128]{3,2,1,0:T(8,128)(2,1)S(1)}, u32[]{:S(2)}, u32[]{:S(2)}) collective-permute-start(bf16[8,3,64,128]{3,2,1,0:T(8,128)(2,1)S(1)} %collective-permute-done.10.refs_3_), channel_id=1, source_target_pairs={{0,4},{1,5},{2,6},{3,7},{4,8},{5,9},{6,10},{7,11},{8,12},{9,13},{1... | collective-permute-start | bytes 1179656 | tf_op jit(solution)/shard_map/ppermute | solution.py:340
  79.6 12.1 %collective-permute-start.16 = (bf16[8,3,64,128]{3,2,1,0:T(8,128)(2,1)S(1)}, bf16[8,3,64,128]{3,2,1,0:T(8,128)(2,1)S(1)}, u32[]{:S(2)}, u32[]{:S(2)}) collective-permute-start(bf16[8,3,64,128]{3,2,1,0:T(8,128)(2,1)S(1)} %collective-permute-done.10.refs_3_), channel_id=1, source_target_pairs={{0,12},{1,13},{2,14},{3,15},{4,0},{5,1},{6,2},{7,3},{8,4},{9,5},{1... | collective-permute-start | bytes 1179656 | tf_op jit(solution)/shard_map/ppermute | solution.py:340
  91.7 12.8 %collective-permute-start.22 = (bf16[16,3,96,128]{3,2,1,0:T(8,128)(2,1)S(1)}, bf16[16,3,96,128]{3,2,1,0:T(8,128)(2,1)S(1)}, u32[]{:S(2)}, u32[]{:S(2)}) collective-permute-start(bf16[16,3,96,128]{3,2,1,0:T(8,128)(2,1)S(1)} %pad_maximum_fusion), channel_id=1, source_target_pairs={{0,16},{16,0},{32,48},{48,32},{64,80},{80,64},{96,112},{112,96},{1... | collective-permute-start | bytes 3538952 | tf_op jit(solution)/shard_map/ppermute | solution.py:340
  91.7 12.7 %collective-permute-start.21 = (bf16[8,3,64,128]{3,2,1,0:T(8,128)(2,1)S(1)}, bf16[8,3,64,128]{3,2,1,0:T(8,128)(2,1)S(1)}, u32[]{:S(2)}, u32[]{:S(2)}) collective-permute-start(bf16[8,3,64,128]{3,2,1,0:T(8,128)(2,1)S(1)} %collective-permute-done.15.refs_8_.refs_11_), channel_id=1, source_target_pairs={{0,4},{1,5},{2,6},{3,7},{4,8},{5,9},{6,10},{7,11},{8,12},{9,13},{1... | collective-permute-start | bytes 1179656 | tf_op jit(solution)/shard_map/ppermute | solution.py:340
  91.9 12.6 %collective-permute-start.20 = (bf16[8,3,64,128]{3,2,1,0:T(8,128)(2,1)S(1)}, bf16[8,3,64,128]{3,2,1,0:T(8,128)(2,1)S(1)}, u32[]{:S(2)}, u32[]{:S(2)}) collective-permute-start(bf16[8,3,64,128]{3,2,1,0:T(8,128)(2,1)S(1)} %collective-permute-done.3.refs_5_), channel_id=1, source_target_pairs={{0,12},{1,13},{2,14},{3,15},{4,0},{5,1},{6,2},{7,3},{8,4},{9,5},{1... | collective-permute-start | bytes 1179656 | tf_op jit(solution)/shard_map/ppermute | solution.py:340

commit v4 on v3

--- a/solution.py
+++ b/solution.py
@@ -6,7 +6,6 @@
 from jax.sharding import PartitionSpec as P
 
 NVI = 64
-UNROLL = 2
 MESH_X, MESH_Y, MESH_ZH, MESH_ZL = 4, 4, 2, 4
 CHUNKS = 16
 
@@ -104,45 +103,77 @@
             lad_out[h ^ label, k, 64:96] = third.astype(jnp.bfloat16)
 
 
-def halves(x, y):
-    late0, late1 = (x + 2) % 4, (y + 2) % 4
-    late1 = jnp.where(late1 == late0, (late0 + 1) % 4, late1)
-    early0 = jnp.where((late0 + 1) % 4 == late1, (late0 + 2) % 4, (late0 + 1) % 4)
-    return (early0, 6 - late0 - late1 - early0), (late0, late1)
-
-
-def products(labels, amp_in, lad_in, amp_parts, lad_parts, amp, lad, sems, late, one_block):
+def where_am_i():
     pi, pj = lax.axis_index("pi"), lax.axis_index("pj")
-    x, zh, core = pi // 4, (pi // 2) % 2, pi % 2
-    y, zl = pj // 4, pj % 4
-    columns = halves(x, y)[late]
+    return pi // 4, (pi // 2) % 2, pi % 2, pj // 4, pj % 4
+
+
+def columns(x, y):
+    far_x, far_y = (x + 2) % 4, (y + 2) % 4
+    third = jnp.where(far_y == far_x, (far_x + 1) % 4, far_y)
+    first = jnp.where((far_x + 1) % 4 == third, (far_x + 2) % 4, (far_x + 1) % 4)
+    return first, 6 - far_x - third - first, third, far_x
+
+
+def slot_of(mx, mz):
+    x, _, core, y, zl = where_am_i()
+    first, second, third, last = columns(x, y)
+    d = mz ^ zl
+    by_d = jnp.where(d == 1, 8, jnp.where(d == 2, 9, jnp.where(d == 0, 12, 13)))
+    by_core = jnp.where(mz % 2 == core, 10, 14) + mz // 2
+    in_third = jnp.where(x == y, 8 + mz, by_d)
+    in_last = jnp.where(x == y, 12 + mz, by_core)
+    rest = jnp.where(mx == third, in_third, in_last)
+    return jnp.where(mx == first, mz, jnp.where(mx == second, 4 + mz, rest))
+
+
+def source_of(slot):
+    x, _, core, y, zl = where_am_i()
+    first, second, third, last = columns(x, y)
+    if slot < 8:
+        return (first, second)[slot // 4] * 4 + slot % 4
+    if slot < 10:
+        return third * 4 + jnp.where(x == y, slot - 8, zl ^ (slot - 7))
+    if slot < 12:
+        apart = last * 4 + 2 * (slot - 10) + core
+        return jnp.where(x == y, third * 4 + slot - 8, apart)
+    if slot < 14:
+        apart = third * 4 + (zl ^ (0, 3)[slot - 12])
+        return jnp.where(x == y, last * 4 + slot - 12, apart)
+    return last * 4 + jnp.where(x == y, slot - 12, 2 * (slot - 14) + 1 - core)
+
+
+def products(labels, amp_in, lad_in, amp_parts, lad_parts, amp, lad, sems, low, groups, unroll, one_block):
+    pi = lax.axis_index("pi")
+    x, zh, core, y, zl = where_am_i()
     copies = []
 
-    def bring(source, target, mx, group):
-        copy = pltpu.make_async_copy(source, target, sems.at[len(copies)])
-        copies.append((copy, (mx == columns[0]) | (mx == columns[1]), group))
+    def bring(source, target, h, slot, group):
+        wanted = (slot >= low) & (slot < low + 4 * groups)
+        at = jnp.where(wanted, slot - low, 0)
+        copy = pltpu.make_async_copy(source, target.at[at, h], sems.at[len(copies)])
+        copies.append((copy, wanted, group))
 
     for name, first, (s, d), h, count in amp_parts:
-        mx = (y + 4 - s) % 4
-        slot = jnp.where(mx == columns[0], 0, 4) + (zl ^ d)
-        bring(amp_in[name].at[pl.ds(first, count)], amp.at[slot, pl.ds(h, count)], mx, 0)
+        slot = slot_of((y + 4 - s) % 4, zl ^ d)
+        bring(amp_in[name].at[pl.ds(first, count)], amp, pl.ds(h, count), slot, 0)
     for half in range(2):
         for name, first, (s, d, c), h, count in lad_parts:
             if count == 4 and h != half * 4:
                 continue
-            mx = (x + 4 - s) % 4
-            first = first + half * 4 - h
-            slot = jnp.where(mx == columns[0], 0, 4) + (zh ^ d) * 2 + (core ^ c)
-            bring(lad_in[name].at[pl.ds(first, 4)], lad.at[slot, pl.ds(half * 4, 4)], mx, half)
+            slot = slot_of((x + 4 - s) % 4, (zh ^ d) * 2 + (core ^ c))
+            source = lad_in[name].at[pl.ds(first + half * 4 - h, 4)]
+            bring(source, lad, pl.ds(half * 4, 4), slot, half)
     for copy, wanted, _ in copies:
         pl.when(wanted)(copy.start)
+    sources = [source_of(low + n) for n in range(4 * groups)]
 
     label_i = [labels[pi * 2 + i] for i in range(2)]
 
     def block(hb, carry):
         first = jnp.zeros((128, 256), jnp.float32)
         second = jnp.zeros((128, 256), jnp.float32)
-        for g in range(2):
+        for g in range(groups):
             weights, left, right = [], [], []
             for k in range(12):
                 m, kk = g * 4 + k // 3, k % 3
@@ -157,7 +188,7 @@
                     pair = []
                     for k in (2 * q, 2 * q + 1):
                         m, kk = g * 4 + k // 3, k % 3
-                        label = labels[(columns[g] * 4 + k // 3) * 3 + kk]
+                        label = labels[sources[m] * 3 + kk]
                         pair.append(amp[m, hb ^ label_i[i] ^ label, kk][:, i * 64 : i * 64 + 64])
                     tops.append(jnp.concatenate(pair, axis=1))
                 left.append(jnp.concatenate(tops, axis=0))
@@ -174,7 +205,7 @@
         for copy, wanted, group in copies:
             if group == half:
                 pl.when(wanted)(copy.wait)
-        lax.fori_loop(half * 4, half * 4 + 4, block, 0, unroll=UNROLL)
+        lax.fori_loop(half * 4, half * 4 + 4, block, 0, unroll=unroll)
 
 
 def early_products(labels, *refs):
@@ -186,9 +217,9 @@
         first_out[hb] = first
         second_out[hb] = second
 
-    amp_parts = [part for part in AMP_PARTS if part[2][0] != 2]
-    lad_parts = [part for part in LAD_PARTS if part[2][0] != 2]
-    products(labels, amp_in, lad_in, amp_parts, lad_parts, amp, lad, sems, 0, keep)
+    amp_parts = [part for part in AMP_PARTS if part[0] in AMP_EARLY]
+    lad_parts = [part for part in LAD_PARTS if part[0] in LAD_EARLY]
+    products(labels, amp_in, lad_in, amp_parts, lad_parts, amp, lad, sems, 0, 3, 4, keep)
 
 
 def late_products(labels, first_in, second_in, *refs):
@@ -202,7 +233,7 @@
         diff[hb] = 2.0 * (first + first_in[hb]) - second
         cross[hb] = jnp.transpose(second)
 
-    products(labels, amp_in, lad_in, AMP_PARTS, LAD_PARTS, amp, lad, sems, 1, keep)
+    products(labels, amp_in, lad_in, AMP_PARTS, LAD_PARTS, amp, lad, sems, 12, 1, 2, keep)
     label_i = [labels[pi * 2 + i] for i in range(2)]
     label_j = [labels[pj * 3 + j] for j in range(3)]
     tall = []
@@ -241,13 +272,14 @@
 ]
 AMP_NAMES = list(dict.fromkeys(part[0] for part in AMP_PARTS))
 LAD_NAMES = list(dict.fromkeys(part[0] for part in LAD_PARTS))
-AMP_EARLY = list(dict.fromkeys(part[0] for part in AMP_PARTS if part[2][0] != 2))
-LAD_EARLY = list(dict.fromkeys(part[0] for part in LAD_PARTS if part[2][0] != 2))
+AMP_EARLY = [name for name in AMP_NAMES if name not in ("fo", "f3")]
+LAD_EARLY = [name for name in LAD_NAMES if name != "c2"]
 COPIES = len(AMP_PARTS) + 2 * len(LAD_PARTS)
 X_UP, X_DOWN = ("pi", shift_x(1)), ("pi", shift_x(-1))
 Y_UP, Y_DOWN, Y_FAR = ("pj", shift_y(1)), ("pj", shift_y(-1)), ("pj", shift_y(2))
 Z_ONE, Z_TWO = ("pj", swap_zl(1)), ("pj", swap_zl(2))
 Z_HALF, OTHER_CORE = ("pi", SWAP_ZH), ("pi", SWAP_CORE)
+SOONER = {"zh": ("z1", "z2")}
 PLAN = [
     ("z1", "a", Z_ONE, 0, 1),
     ("z2", "a", Z_TWO, 0, 1),
@@ -294,27 +326,27 @@
     return call(prepare, outs, labels, args, [pl.ANY] * 3, scratch, 2 * 10**9, 3 * 10**6, 60)
 
 
-def slots():
-    return [pltpu.VMEM((8, 8, 3, 64, 128), jnp.bfloat16), pltpu.VMEM((8, 8, 3, 96, 128), jnp.bfloat16)]
+def slots(count):
+    return [pltpu.VMEM((count, 8, 3, rows, 128), jnp.bfloat16) for rows in (64, 96)]
 
 
 def begin(labels, got):
     args = [fetch(got, name) for name in AMP_EARLY + LAD_EARLY]
     outs = [jax.ShapeDtypeStruct((8, 128, 256), jnp.float32)] * 2
-    scratch = slots() + [pltpu.SemaphoreType.DMA((COPIES,))]
-    return call(early_products, outs, labels, args, [pl.ANY] * len(args), scratch, 5 * 10**9, 8 * 10**6, 18)
+    scratch = slots(12) + [pltpu.SemaphoreType.DMA((COPIES,))]
+    return call(early_products, outs, labels, args, [pl.ANY] * len(args), scratch, 7 * 10**9, 12 * 10**6, 22)
 
 
 def finish(labels, got, sums):
     args = [fetch(got, name) for name in AMP_NAMES + LAD_NAMES]
     outs = [jax.ShapeDtypeStruct((2, 3, 8, NVI * NVI), jnp.bfloat16)]
-    scratch = slots() + [
+    scratch = slots(4) + [
         pltpu.VMEM((8, 128, 256), jnp.float32),
         pltpu.VMEM((8, 256, 128), jnp.float32),
         pltpu.SemaphoreType.DMA((COPIES,)),
     ]
     spaces = [pltpu.VMEM] * 2 + [pl.ANY] * len(args)
-    return call(late_products, outs, labels, [*sums, *args], spaces, scratch, 5 * 10**9, 8 * 10**6, 22)[0]
+    return call(late_products, outs, labels, [*sums, *args], spaces, scratch, 2 * 10**9, 4 * 10**6, 20)[0]
 
 
 def fetch(got, source):
@@ -333,7 +365,7 @@
     starts = {name: start for name, _, _, start, _ in PLAN}
     for name, source, (axis, pairs), start, _ in sorted(PLAN, key=lambda step: step[3]):
         before = [n for n in ends if ends[n] <= start]
-        last = [n for n in before if not any(ends[n] <= starts[m] for m in before)]
+        last = SOONER.get(name) or [n for n in before if not any(ends[n] <= starts[m] for m in before)]
         value = fetch(got, source)
         if last:
             value = lax.optimization_barrier((value, *[got[n] for n in last]))[0]

time: 114 us -> 112 us (0.982)
  the two profiles are of different devices: /device:TPU:102 before, /device:TPU:1 now
where the time goes in v4:
time: 112 us; the launch traced here: 110 us
  waiting for transfers between devices  46.8 us (42%)
  starting transfers between devices  40.1 us (36%)
  Pallas kernels  21.1 us (19%)
  local copies, waits for them, and re-layouts  1.61 us (1%)
    ppermute x23, waiting for transfers between devices, on_device(): got[name] = lax.ppermute(value, axis, pairs)  46.8 us
    ppermute x23, starting transfers between devices, on_device(): got[name] = lax.ppermute(value, axis, pairs)  40.1 us
    pallas_call x3, Pallas kernels, call(): pl.pallas_call(kernel, out_shape=outs, in_specs=[pl.BlockSpec(memory_spac...  21.1 us
  transfers between devices with their start and end apart: 23, of which 7 were waited for; matrix products, arithmetic and copies ran while one was open for 2% of the time, Pallas kernels for 9%

profile of v4, /device:TPU:1, one launch (start us, length us, event | category | flops | bytes accessed | tf_op | source)
XLA Modules:
  0.0 110.3 jit_solution(15961407922602390578)
XLA Ops:
  0.0 4.2 %shard_map.46 = (bf16[8,3,64,128]{3,2,1,0:T(8,128)(2,1)}, bf16[8,3,96,128]{3,2,1,0:T(8,128)(2,1)}) custom-call(s32[48]{0:T(128)} %labels.5, bf16[2,3,8,4096]{3,2,1,0:T(8,128)(2,1)} %amp_in.1, bf16[3,3,8,4096]{3,2,1,0:T(8,128)(2,1)} %coul_in.1, bf16[3,3,8,4096]{3,2,1,0:T(8,128)(2,1)} %exch_in.1), custom_call_target="tpu_custom_call" | custom-call | flops 2000000000 | bytes 3000000 | tf_op jit(solution)/shard_map/pallas_call | solution.py:312
  4.2 2.1 %collective-permute-start.5 = (bf16[8,3,96,128]{3,2,1,0:T(8,128)(2,1)}, bf16[8,3,96,128]{3,2,1,0:T(8,128)(2,1)S(1)}, u32[]{:S(2)}, u32[]{:S(2)}) collective-permute-start(bf16[8,3,96,128]{3,2,1,0:T(8,128)(2,1)} %get-tuple-element.28.refs_12_.refs_14_), channel_id=1, source_target_pairs={{0,64},{16,80},{32,96},{48,112},{64,128},{80,144},{96,160},{112,17... | collective-permute-start | bytes 1769480 | tf_op jit(solution)/shard_map/ppermute | solution.py:372
  6.3 3.0 %collective-permute-start.1 = (bf16[8,3,64,128]{3,2,1,0:T(8,128)(2,1)}, bf16[8,3,64,128]{3,2,1,0:T(8,128)(2,1)S(1)}, u32[]{:S(2)}, u32[]{:S(2)}) collective-permute-start(bf16[8,3,64,128]{3,2,1,0:T(8,128)(2,1)} %get-tuple-element.24.refs_0_), channel_id=1, source_target_pairs={{0,2},{1,3},{2,0},{3,1},{4,6},{5,7},{6,4},{7,5},{8,10},{9,11},{10,... | collective-permute-start | bytes 1179656 | tf_op jit(solution)/shard_map/ppermute | solution.py:372
  9.3 1.6 %collective-permute-start = (bf16[8,3,64,128]{3,2,1,0:T(8,128)(2,1)}, bf16[8,3,64,128]{3,2,1,0:T(8,128)(2,1)S(1)}, u32[]{:S(2)}, u32[]{:S(2)}) collective-permute-start(bf16[8,3,64,128]{3,2,1,0:T(8,128)(2,1)} %get-tuple-element.24.refs_0_), channel_id=1, source_target_pairs={{0,1},{1,0},{2,3},{3,2},{4,5},{5,4},{6,7},{7,6},{8,9},{9,8},{10,11... | collective-permute-start | bytes 1179656 | tf_op jit(solution)/shard_map/ppermute | solution.py:372
  10.9 2.7 %collective-permute-start.4 = (bf16[8,3,64,128]{3,2,1,0:T(8,128)(2,1)}, bf16[8,3,64,128]{3,2,1,0:T(8,128)(2,1)S(1)}, u32[]{:S(2)}, u32[]{:S(2)}) collective-permute-start(bf16[8,3,64,128]{3,2,1,0:T(8,128)(2,1)} %get-tuple-element.24.refs_0_), channel_id=1, source_target_pairs={{0,12},{1,13},{2,14},{3,15},{4,0},{5,1},{6,2},{7,3},{8,4},{9,5},{1... | collective-permute-start | bytes 1179656 | tf_op jit(solution)/shard_map/ppermute | solution.py:372
  13.6 0.0 collective-permute-start.3
  13.6 12.8 %collective-permute-done.1.refs_2_ = bf16[8,3,64,128]{3,2,1,0:T(8,128)(2,1)S(1)} collective-permute-done((bf16[8,3,64,128]{3,2,1,0:T(8,128)(2,1)}, bf16[8,3,64,128]{3,2,1,0:T(8,128)(2,1)S(1)}, u32[]{:S(2)}, u32[]{:S(2)}) %collective-permute-start.1) | collective-permute-done | bytes 393248 | tf_op jit(solution)/shard_map/ppermute | solution.py:372
  26.5 0.0 collective-permute-done.refs_1_
  26.5 0.1 pad_maximum_fusion.1
  26.6 0.0 collective-permute-done.4.refs_5_
  26.6 0.0 collective-permute-done.3.refs_4_
  26.6 0.0 collective-permute-done.5.refs_13_.refs_15_
  26.6 1.4 %collective-permute-start.6 = (bf16[16,3,64,128]{3,2,1,0:T(8,128)(2,1)S(1)}, bf16[16,3,64,128]{3,2,1,0:T(8,128)(2,1)S(1)}, u32[]{:S(2)}, u32[]{:S(2)}) collective-permute-start(bf16[16,3,64,128]{3,2,1,0:T(8,128)(2,1)S(1)} %pad_maximum_fusion.1), channel_id=1, source_target_pairs={{0,4},{1,5},{2,6},{3,7},{4,8},{5,9},{6,10},{7,11},{8,12},{9,13},{1... | collective-permute-start | bytes 2359304 | tf_op jit(solution)/shard_map/ppermute | solution.py:372
  28.0 1.5 %collective-permute-start.7 = (bf16[16,3,64,128]{3,2,1,0:T(8,128)(2,1)S(1)}, bf16[16,3,64,128]{3,2,1,0:T(8,128)(2,1)S(1)}, u32[]{:S(2)}, u32[]{:S(2)}) collective-permute-start(bf16[16,3,64,128]{3,2,1,0:T(8,128)(2,1)S(1)} %pad_maximum_fusion.1), channel_id=1, source_target_pairs={{0,12},{1,13},{2,14},{3,15},{4,0},{5,1},{6,2},{7,3},{8,4},{9,5},{1... | collective-permute-start | bytes 2359304 | tf_op jit(solution)/shard_map/ppermute | solution.py:372
  29.5 6.8 %collective-permute-start.2 = (bf16[8,3,96,128]{3,2,1,0:T(8,128)(2,1)}, bf16[8,3,96,128]{3,2,1,0:T(8,128)(2,1)S(1)}, u32[]{:S(2)}, u32[]{:S(2)}) collective-permute-start(bf16[8,3,96,128]{3,2,1,0:T(8,128)(2,1)} %get-tuple-element.28.refs_12_.refs_14_), channel_id=1, source_target_pairs={{0,32},{16,48},{32,0},{48,16},{64,96},{80,112},{96,64},{112,80},{1... | collective-permute-start | bytes 1769480 | tf_op jit(solution)/shard_map/ppermute | solution.py:372
  36.3 1.5 %collective-permute-start.8 = (bf16[8,3,96,128]{3,2,1,0:T(8,128)(2,1)}, bf16[8,3,96,128]{3,2,1,0:T(8,128)(2,1)S(1)}, u32[]{:S(2)}, u32[]{:S(2)}) collective-permute-start(bf16[8,3,96,128]{3,2,1,0:T(8,128)(2,1)} %get-tuple-element.28.refs_12_.refs_14_), channel_id=1, source_target_pairs={{0,192},{16,208},{32,224},{48,240},{64,0},{80,16},{96,32},{112,48}... | collective-permute-start | bytes 1769480 | tf_op jit(solution)/shard_map/ppermute | solution.py:372
  37.7 0.0 collective-permute-start.9
  37.7 18.0 %collective-permute-done.2.refs_16_.refs_18_ = bf16[8,3,96,128]{3,2,1,0:T(8,128)(2,1)S(1)} collective-permute-done((bf16[8,3,96,128]{3,2,1,0:T(8,128)(2,1)}, bf16[8,3,96,128]{3,2,1,0:T(8,128)(2,1)S(1)}, u32[]{:S(2)}, u32[]{:S(2)}) %collective-permute-start.2) | collective-permute-done | bytes 589856 | tf_op jit(solution)/shard_map/ppermute | solution.py:372
  55.8 0.0 collective-permute-done.8.refs_14_.refs_16_
  55.8 0.0 collective-permute-done.9.refs_15_.refs_17_
  55.8 0.0 collective-permute-done.6.refs_6_.refs_7_
  55.8 0.0 collective-permute-done.7.refs_7_.refs_8_
  55.8 1.3 %collective-permute-start.13 = (bf16[8,3,96,128]{3,2,1,0:T(8,128)(2,1)S(1)}, bf16[8,3,96,128]{3,2,1,0:T(8,128)(2,1)S(1)}, u32[]{:S(2)}, u32[]{:S(2)}) collective-permute-start(bf16[8,3,96,128]{3,2,1,0:T(8,128)(2,1)S(1)} %collective-permute-done.2.refs_16_.refs_18_), channel_id=1, source_target_pairs={{0,64},{16,80},{32,96},{48,112},{64,128},{80,144},{96,160},{112,17... | collective-permute-start | bytes 1769480 | tf_op jit(solution)/shard_map/ppermute | solution.py:372
  57.1 1.5 %collective-permute-start.14 = (bf16[8,3,96,128]{3,2,1,0:T(8,128)(2,1)S(1)}, bf16[8,3,96,128]{3,2,1,0:T(8,128)(2,1)S(1)}, u32[]{:S(2)}, u32[]{:S(2)}) collective-permute-start(bf16[8,3,96,128]{3,2,1,0:T(8,128)(2,1)S(1)} %collective-permute-done.2.refs_16_.refs_18_), channel_id=1, source_target_pairs={{0,192},{16,208},{32,224},{48,240},{64,0},{80,16},{96,32},{112,48}... | collective-permute-start | bytes 1769480 | tf_op jit(solution)/shard_map/ppermute | solution.py:372
  58.5 1.1 constant_dynamic-update-slice_fusion.5
  59.7 0.1 constant_dynamic-update-slice_fusion.4
  59.8 1.3 %collective-permute-start.12 = (bf16[8,3,64,128]{3,2,1,0:T(8,128)(2,1)S(1)}, bf16[8,3,64,128]{3,2,1,0:T(8,128)(2,1)S(1)}, u32[]{:S(2)}, u32[]{:S(2)}) collective-permute-start(bf16[8,3,64,128]{3,2,1,0:T(8,128)(2,1)S(1)} %slice.17), channel_id=1, source_target_pairs={{0,12},{1,13},{2,14},{3,15},{4,0},{5,1},{6,2},{7,3},{8,4},{9,5},{1... | collective-permute-start | bytes 1179656 | tf_op jit(solution)/shard_map/ppermute | solution.py:372
  61.1 0.4 collective-permute-start.11
  61.4 0.0 collective-permute-start.10
  61.4 0.1 constant_dynamic-update-slice_fusion.3
  61.5 0.0 copy-start
  61.5 0.0 copy-start.1
  61.5 0.0 copy-start.2
  61.6 0.1 constant_dynamic-update-slice_fusion.2
  61.6 5.4 %collective-permute-done.13.refs_17_.refs_19_ = bf16[8,3,96,128]{3,2,1,0:T(8,128)(2,1)S(1)} collective-permute-done((bf16[8,3,96,128]{3,2,1,0:T(8,128)(2,1)S(1)}, bf16[8,3,96,128]{3,2,1,0:T(8,128)(2,1)S(1)}, u32[]{:S(2)}, u32[]{:S(2)}) %collective-permute-start.13) | collective-permute-done | bytes 589856 | tf_op jit(solution)/shard_map/ppermute | solution.py:372
  67.1 0.1 constant_dynamic-update-slice_fusion.1
  67.1 0.0 collective-permute-done.14.refs_18_.refs_20_
  67.2 0.1 constant_dynamic-update-slice_fusion
  67.2 0.0 collective-permute-done.12.refs_9_.refs_10_
  67.2 2.0 %collective-permute-done.11.refs_8_.refs_9_ = bf16[8,3,64,128]{3,2,1,0:T(8,128)(2,1)S(1)} collective-permute-done((bf16[8,3,64,128]{3,2,1,0:T(8,128)(2,1)S(1)}, bf16[8,3,64,128]{3,2,1,0:T(8,128)(2,1)S(1)}, u32[]{:S(2)}, u32[]{:S(2)}) %collective-permute-start.11) | collective-permute-done | bytes 393248 | tf_op jit(solution)/shard_map/ppermute | solution.py:372
  69.3 0.0 collective-permute-done.10.refs_3_
  69.3 6.7 %collective-permute-start.19 = (bf16[48,3,96,128]{3,2,1,0:T(8,128)(2,1)S(1)}, bf16[48,3,96,128]{3,2,1,0:T(8,128)(2,1)S(1)}, u32[]{:S(2)}, u32[]{:S(2)}) collective-permute-start(bf16[48,3,96,128]{3,2,1,0:T(8,128)(2,1)S(1)} %constant_dynamic-update-slice_fusion), channel_id=1, source_target_pairs={{0,16},{16,0},{32,48},{48,32},{64,80},{80,64},{96,112},{112,96},{1... | collective-permute-start | bytes 10616840 | tf_op jit(solution)/shard_map/ppermute | solution.py:372
  76.0 0.3 collective-permute-start.18
  76.4 1.3 %collective-permute-start.17 = (bf16[4,3,96,128]{3,2,1,0:T(8,128)(2,1)S(1)}, bf16[4,3,96,128]{3,2,1,0:T(8,128)(2,1)S(1)}, u32[]{:S(2)}, u32[]{:S(2)}) collective-permute-start(bf16[4,3,96,128]{3,2,1,0:T(8,128)(2,1)S(1)} %slice.18), channel_id=1, source_target_pairs={{0,64},{16,80},{32,96},{48,112},{64,128},{80,144},{96,160},{112,17... | collective-permute-start | bytes 884744 | tf_op jit(solution)/shard_map/ppermute | solution.py:372
  77.7 0.0 collective-permute-start.15
  77.7 2.7 %collective-permute-start.16 = (bf16[8,3,64,128]{3,2,1,0:T(8,128)(2,1)S(1)}, bf16[8,3,64,128]{3,2,1,0:T(8,128)(2,1)S(1)}, u32[]{:S(2)}, u32[]{:S(2)}) collective-permute-start(bf16[8,3,64,128]{3,2,1,0:T(8,128)(2,1)S(1)} %collective-permute-done.10.refs_3_), channel_id=1, source_target_pairs={{0,12},{1,13},{2,14},{3,15},{4,0},{5,1},{6,2},{7,3},{8,4},{9,5},{1... | collective-permute-start | bytes 1179656 | tf_op jit(solution)/shard_map/ppermute | solution.py:372
  80.4 4.4 %collective-permute-done.18.refs_20_.refs_22_ = bf16[4,3,96,128]{3,2,1,0:T(8,128)(2,1)S(1)} collective-permute-done((bf16[4,3,96,128]{3,2,1,0:T(8,128)(2,1)S(1)}, bf16[4,3,96,128]{3,2,1,0:T(8,128)(2,1)S(1)}, u32[]{:S(2)}, u32[]{:S(2)}) %collective-permute-start.18) | collective-permute-done | bytes 294944 | tf_op jit(solution)/shard_map/ppermute | solution.py:372
  84.7 1.3 %collective-permute-done.17.refs_19_.refs_21_ = bf16[4,3,96,128]{3,2,1,0:T(8,128)(2,1)S(1)} collective-permute-done((bf16[4,3,96,128]{3,2,1,0:T(8,128)(2,1)S(1)}, bf16[4,3,96,128]{3,2,1,0:T(8,128)(2,1)S(1)}, u32[]{:S(2)}, u32[]{:S(2)}) %collective-permute-start.17) | collective-permute-done | bytes 294944 | tf_op jit(solution)/shard_map/ppermute | solution.py:372
  86.0 0.1 pad_maximum_fusion
  86.2 2.8 %collective-permute-done.15.refs_10_.refs_11_ = bf16[8,3,64,128]{3,2,1,0:T(8,128)(2,1)S(1)} collective-permute-done((bf16[8,3,64,128]{3,2,1,0:T(8,128)(2,1)S(1)}, bf16[8,3,64,128]{3,2,1,0:T(8,128)(2,1)S(1)}, u32[]{:S(2)}, u32[]{:S(2)}) %collective-permute-start.15) | collective-permute-done | bytes 393248 | tf_op jit(solution)/shard_map/ppermute | solution.py:372
  89.0 0.0 collective-permute-done.16.refs_11_.refs_12_
  89.0 0.0 collective-permute-done.19.refs_21_.refs_23_
  89.0 1.4 %collective-permute-start.22 = (bf16[16,3,96,128]{3,2,1,0:T(8,128)(2,1)S(1)}, bf16[16,3,96,128]{3,2,1,0:T(8,128)(2,1)S(1)}, u32[]{:S(2)}, u32[]{:S(2)}) collective-permute-start(bf16[16,3,96,128]{3,2,1,0:T(8,128)(2,1)S(1)} %pad_maximum_fusion), channel_id=1, source_target_pairs={{0,16},{16,0},{32,48},{48,32},{64,80},{80,64},{96,112},{112,96},{1... | collective-permute-start | bytes 3538952 | tf_op jit(solution)/shard_map/ppermute | solution.py:372
  90.4 0.0 collective-permute-start.21
  90.4 2.7 %collective-permute-start.20 = (bf16[8,3,64,128]{3,2,1,0:T(8,128)(2,1)S(1)}, bf16[8,3,64,128]{3,2,1,0:T(8,128)(2,1)S(1)}, u32[]{:S(2)}, u32[]{:S(2)}) collective-permute-start(bf16[8,3,64,128]{3,2,1,0:T(8,128)(2,1)S(1)} %collective-permute-done.4.refs_5_), channel_id=1, source_target_pairs={{0,12},{1,13},{2,14},{3,15},{4,0},{5,1},{6,2},{7,3},{8,4},{9,5},{1... | collective-permute-start | bytes 1179656 | tf_op jit(solution)/shard_map/ppermute | solution.py:372
  93.1 0.0 copy-done
  93.1 0.0 copy-done.1
  93.1 0.0 copy-done.2
  93.1 9.6 %shard_map.47 = (f32[8,128,256]{2,1,0:T(8,128)S(1)}, f32[8,128,256]{2,1,0:T(8,128)S(1)}) custom-call(s32[48]{0:T(128)S(1)} %copy-done.2, bf16[8,3,64,128]{3,2,1,0:T(8,128)(2,1)S(1)} %copy-done.1, bf16[8,3,64,128]{3,2,1,0:T(8,128)(2,1)S(1)} %collective-permute-done.refs_1_, bf16[8,3,64,128]{3,2,1,0:T(8,128)(2,1)S(1)} %collective-permute-done.1.refs_2_, ...), custom_call_target="tpu_custom_call" | custom-call | flops 7000000000 | bytes 12000000 | tf_op jit(solution)/shard_map/pallas_call | solution.py:312
  102.7 0.0 collective-permute-done.21.refs_13_
  102.8 0.0 collective-permute-done.20.refs_6_
  102.8 0.0 collective-permute-done.22.refs_24_
  102.8 7.3 %shard_map.48 = bf16[2,3,8,4096]{3,2,1,0:T(8,128)(2,1)} custom-call(s32[48]{0:T(128)S(1)} %copy-done.2, f32[8,128,256]{2,1,0:T(8,128)S(1)} %get-tuple-element.38.first_in, f32[8,128,256]{2,1,0:T(8,128)S(1)} %get-tuple-element.39.second_in, bf16[8,3,64,128]{3,2,1,0:T(8,128)(2,1)S(1)} %copy-done.1, bf16[8,3,64,128]{3,2,1,0:T(8,128)(2,1)S(1)} %collective-permute-done.refs_1_, ...), custom_call_target="tpu_custom_call" | custom-call | flops 2000000000 | bytes 4000000 | tf_op jit(solution)/shard_map/pallas_call | solution.py:312
  (4 shorter events, 0.1 us)
Async XLA Ops:
  4.2 22.4 %collective-permute-start.5 = (bf16[8,3,96,128]{3,2,1,0:T(8,128)(2,1)}, bf16[8,3,96,128]{3,2,1,0:T(8,128)(2,1)S(1)}, u32[]{:S(2)}, u32[]{:S(2)}) collective-permute-start(bf16[8,3,96,128]{3,2,1,0:T(8,128)(2,1)} %get-tuple-element.28.refs_12_.refs_14_), channel_id=1, source_target_pairs={{0,64},{16,80},{32,96},{48,112},{64,128},{80,144},{96,160},{112,17... | collective-permute-start | bytes 1769480 | tf_op jit(solution)/shard_map/ppermute | solution.py:372
  6.3 20.2 %collective-permute-start.1 = (bf16[8,3,64,128]{3,2,1,0:T(8,128)(2,1)}, bf16[8,3,64,128]{3,2,1,0:T(8,128)(2,1)S(1)}, u32[]{:S(2)}, u32[]{:S(2)}) collective-permute-start(bf16[8,3,64,128]{3,2,1,0:T(8,128)(2,1)} %get-tuple-element.24.refs_0_), channel_id=1, source_target_pairs={{0,2},{1,3},{2,0},{3,1},{4,6},{5,7},{6,4},{7,5},{8,10},{9,11},{10,... | collective-permute-start | bytes 1179656 | tf_op jit(solution)/shard_map/ppermute | solution.py:372
  9.3 17.2 %collective-permute-start = (bf16[8,3,64,128]{3,2,1,0:T(8,128)(2,1)}, bf16[8,3,64,128]{3,2,1,0:T(8,128)(2,1)S(1)}, u32[]{:S(2)}, u32[]{:S(2)}) collective-permute-start(bf16[8,3,64,128]{3,2,1,0:T(8,128)(2,1)} %get-tuple-element.24.refs_0_), channel_id=1, source_target_pairs={{0,1},{1,0},{2,3},{3,2},{4,5},{5,4},{6,7},{7,6},{8,9},{9,8},{10,11... | collective-permute-start | bytes 1179656 | tf_op jit(solution)/shard_map/ppermute | solution.py:372
  10.9 15.6 %collective-permute-start.4 = (bf16[8,3,64,128]{3,2,1,0:T(8,128)(2,1)}, bf16[8,3,64,128]{3,2,1,0:T(8,128)(2,1)S(1)}, u32[]{:S(2)}, u32[]{:S(2)}) collective-permute-start(bf16[8,3,64,128]{3,2,1,0:T(8,128)(2,1)} %get-tuple-element.24.refs_0_), channel_id=1, source_target_pairs={{0,12},{1,13},{2,14},{3,15},{4,0},{5,1},{6,2},{7,3},{8,4},{9,5},{1... | collective-permute-start | bytes 1179656 | tf_op jit(solution)/shard_map/ppermute | solution.py:372
  13.6 12.9 %collective-permute-start.3 = (bf16[8,3,64,128]{3,2,1,0:T(8,128)(2,1)}, bf16[8,3,64,128]{3,2,1,0:T(8,128)(2,1)S(1)}, u32[]{:S(2)}, u32[]{:S(2)}) collective-permute-start(bf16[8,3,64,128]{3,2,1,0:T(8,128)(2,1)} %get-tuple-element.24.refs_0_), channel_id=1, source_target_pairs={{0,4},{1,5},{2,6},{3,7},{4,8},{5,9},{6,10},{7,11},{8,12},{9,13},{1... | collective-permute-start | bytes 1179656 | tf_op jit(solution)/shard_map/ppermute | solution.py:372
  26.6 29.2 %collective-permute-start.6 = (bf16[16,3,64,128]{3,2,1,0:T(8,128)(2,1)S(1)}, bf16[16,3,64,128]{3,2,1,0:T(8,128)(2,1)S(1)}, u32[]{:S(2)}, u32[]{:S(2)}) collective-permute-start(bf16[16,3,64,128]{3,2,1,0:T(8,128)(2,1)S(1)} %pad_maximum_fusion.1), channel_id=1, source_target_pairs={{0,4},{1,5},{2,6},{3,7},{4,8},{5,9},{6,10},{7,11},{8,12},{9,13},{1... | collective-permute-start | bytes 2359304 | tf_op jit(solution)/shard_map/ppermute | solution.py:372
  28.0 27.8 %collective-permute-start.7 = (bf16[16,3,64,128]{3,2,1,0:T(8,128)(2,1)S(1)}, bf16[16,3,64,128]{3,2,1,0:T(8,128)(2,1)S(1)}, u32[]{:S(2)}, u32[]{:S(2)}) collective-permute-start(bf16[16,3,64,128]{3,2,1,0:T(8,128)(2,1)S(1)} %pad_maximum_fusion.1), channel_id=1, source_target_pairs={{0,12},{1,13},{2,14},{3,15},{4,0},{5,1},{6,2},{7,3},{8,4},{9,5},{1... | collective-permute-start | bytes 2359304 | tf_op jit(solution)/shard_map/ppermute | solution.py:372
  29.5 26.3 %collective-permute-start.2 = (bf16[8,3,96,128]{3,2,1,0:T(8,128)(2,1)}, bf16[8,3,96,128]{3,2,1,0:T(8,128)(2,1)S(1)}, u32[]{:S(2)}, u32[]{:S(2)}) collective-permute-start(bf16[8,3,96,128]{3,2,1,0:T(8,128)(2,1)} %get-tuple-element.28.refs_12_.refs_14_), channel_id=1, source_target_pairs={{0,32},{16,48},{32,0},{48,16},{64,96},{80,112},{96,64},{112,80},{1... | collective-permute-start | bytes 1769480 | tf_op jit(solution)/shard_map/ppermute | solution.py:372
  36.3 19.5 %collective-permute-start.8 = (bf16[8,3,96,128]{3,2,1,0:T(8,128)(2,1)}, bf16[8,3,96,128]{3,2,1,0:T(8,128)(2,1)S(1)}, u32[]{:S(2)}, u32[]{:S(2)}) collective-permute-start(bf16[8,3,96,128]{3,2,1,0:T(8,128)(2,1)} %get-tuple-element.28.refs_12_.refs_14_), channel_id=1, source_target_pairs={{0,192},{16,208},{32,224},{48,240},{64,0},{80,16},{96,32},{112,48}... | collective-permute-start | bytes 1769480 | tf_op jit(solution)/shard_map/ppermute | solution.py:372
  37.7 18.0 %collective-permute-start.9 = (bf16[8,3,96,128]{3,2,1,0:T(8,128)(2,1)S(1)}, bf16[8,3,96,128]{3,2,1,0:T(8,128)(2,1)S(1)}, u32[]{:S(2)}, u32[]{:S(2)}) collective-permute-start(bf16[8,3,96,128]{3,2,1,0:T(8,128)(2,1)S(1)} %collective-permute-done.5.refs_13_.refs_15_), channel_id=1, source_target_pairs={{0,64},{16,80},{32,96},{48,112},{64,128},{80,144},{96,160},{112,17... | collective-permute-start | bytes 1769480 | tf_op jit(solution)/shard_map/ppermute | solution.py:372
  55.8 11.3 %collective-permute-start.13 = (bf16[8,3,96,128]{3,2,1,0:T(8,128)(2,1)S(1)}, bf16[8,3,96,128]{3,2,1,0:T(8,128)(2,1)S(1)}, u32[]{:S(2)}, u32[]{:S(2)}) collective-permute-start(bf16[8,3,96,128]{3,2,1,0:T(8,128)(2,1)S(1)} %collective-permute-done.2.refs_16_.refs_18_), channel_id=1, source_target_pairs={{0,64},{16,80},{32,96},{48,112},{64,128},{80,144},{96,160},{112,17... | collective-permute-start | bytes 1769480 | tf_op jit(solution)/shard_map/ppermute | solution.py:372
  57.1 10.1 %collective-permute-start.14 = (bf16[8,3,96,128]{3,2,1,0:T(8,128)(2,1)S(1)}, bf16[8,3,96,128]{3,2,1,0:T(8,128)(2,1)S(1)}, u32[]{:S(2)}, u32[]{:S(2)}) collective-permute-start(bf16[8,3,96,128]{3,2,1,0:T(8,128)(2,1)S(1)} %collective-permute-done.2.refs_16_.refs_18_), channel_id=1, source_target_pairs={{0,192},{16,208},{32,224},{48,240},{64,0},{80,16},{96,32},{112,48}... | collective-permute-start | bytes 1769480 | tf_op jit(solution)/shard_map/ppermute | solution.py:372
  59.8 7.5 %collective-permute-start.12 = (bf16[8,3,64,128]{3,2,1,0:T(8,128)(2,1)S(1)}, bf16[8,3,64,128]{3,2,1,0:T(8,128)(2,1)S(1)}, u32[]{:S(2)}, u32[]{:S(2)}) collective-permute-start(bf16[8,3,64,128]{3,2,1,0:T(8,128)(2,1)S(1)} %slice.17), channel_id=1, source_target_pairs={{0,12},{1,13},{2,14},{3,15},{4,0},{5,1},{6,2},{7,3},{8,4},{9,5},{1... | collective-permute-start | bytes 1179656 | tf_op jit(solution)/shard_map/ppermute | solution.py:372
  61.1 8.2 %collective-permute-start.11 = (bf16[8,3,64,128]{3,2,1,0:T(8,128)(2,1)S(1)}, bf16[8,3,64,128]{3,2,1,0:T(8,128)(2,1)S(1)}, u32[]{:S(2)}, u32[]{:S(2)}) collective-permute-start(bf16[8,3,64,128]{3,2,1,0:T(8,128)(2,1)S(1)} %slice.16), channel_id=1, source_target_pairs={{0,4},{1,5},{2,6},{3,7},{4,8},{5,9},{6,10},{7,11},{8,12},{9,13},{1... | collective-permute-start | bytes 1179656 | tf_op jit(solution)/shard_map/ppermute | solution.py:372
  61.4 7.9 %collective-permute-start.10 = (bf16[8,3,64,128]{3,2,1,0:T(8,128)(2,1)S(1)}, bf16[8,3,64,128]{3,2,1,0:T(8,128)(2,1)S(1)}, u32[]{:S(2)}, u32[]{:S(2)}) collective-permute-start(bf16[8,3,64,128]{3,2,1,0:T(8,128)(2,1)S(1)} %collective-permute-done.1.refs_2_), channel_id=1, source_target_pairs={{0,1},{1,0},{2,3},{3,2},{4,5},{5,4},{6,7},{7,6},{8,9},{9,8},{10,11... | collective-permute-start | bytes 1179656 | tf_op jit(solution)/shard_map/ppermute | solution.py:372
  61.5 31.6 %copy-start = (bf16[8,3,96,128]{3,2,1,0:T(8,128)(2,1)S(1)}, bf16[8,3,96,128]{3,2,1,0:T(8,128)(2,1)}, u32[]{:S(2)}) copy-start(bf16[8,3,96,128]{3,2,1,0:T(8,128)(2,1)} %get-tuple-element.28.refs_12_.refs_14_) | copy-start | bytes 1769476
  61.5 31.6 %copy-start.1 = (bf16[8,3,64,128]{3,2,1,0:T(8,128)(2,1)S(1)}, bf16[8,3,64,128]{3,2,1,0:T(8,128)(2,1)}, u32[]{:S(2)}) copy-start(bf16[8,3,64,128]{3,2,1,0:T(8,128)(2,1)} %get-tuple-element.24.refs_0_) | copy-start | bytes 1179652
  61.5 31.6 %copy-start.2 = (s32[48]{0:T(128)S(1)}, s32[48]{0:T(128)}, u32[]{:S(2)}) copy-start(s32[48]{0:T(128)} %labels.5) | copy-start | bytes 580
  69.3 19.7 %collective-permute-start.19 = (bf16[48,3,96,128]{3,2,1,0:T(8,128)(2,1)S(1)}, bf16[48,3,96,128]{3,2,1,0:T(8,128)(2,1)S(1)}, u32[]{:S(2)}, u32[]{:S(2)}) collective-permute-start(bf16[48,3,96,128]{3,2,1,0:T(8,128)(2,1)S(1)} %constant_dynamic-update-slice_fusion), channel_id=1, source_target_pairs={{0,16},{16,0},{32,48},{48,32},{64,80},{80,64},{96,112},{112,96},{1... | collective-permute-start | bytes 10616840 | tf_op jit(solution)/shard_map/ppermute | solution.py:372
  76.0 8.7 %collective-permute-start.18 = (bf16[4,3,96,128]{3,2,1,0:T(8,128)(2,1)S(1)}, bf16[4,3,96,128]{3,2,1,0:T(8,128)(2,1)S(1)}, u32[]{:S(2)}, u32[]{:S(2)}) collective-permute-start(bf16[4,3,96,128]{3,2,1,0:T(8,128)(2,1)S(1)} %slice.19), channel_id=1, source_target_pairs={{0,192},{16,208},{32,224},{48,240},{64,0},{80,16},{96,32},{112,48}... | collective-permute-start | bytes 884744 | tf_op jit(solution)/shard_map/ppermute | solution.py:372
  76.4 9.6 %collective-permute-start.17 = (bf16[4,3,96,128]{3,2,1,0:T(8,128)(2,1)S(1)}, bf16[4,3,96,128]{3,2,1,0:T(8,128)(2,1)S(1)}, u32[]{:S(2)}, u32[]{:S(2)}) collective-permute-start(bf16[4,3,96,128]{3,2,1,0:T(8,128)(2,1)S(1)} %slice.18), channel_id=1, source_target_pairs={{0,64},{16,80},{32,96},{48,112},{64,128},{80,144},{96,160},{112,17... | collective-permute-start | bytes 884744 | tf_op jit(solution)/shard_map/ppermute | solution.py:372
  77.7 11.3 %collective-permute-start.15 = (bf16[8,3,64,128]{3,2,1,0:T(8,128)(2,1)S(1)}, bf16[8,3,64,128]{3,2,1,0:T(8,128)(2,1)S(1)}, u32[]{:S(2)}, u32[]{:S(2)}) collective-permute-start(bf16[8,3,64,128]{3,2,1,0:T(8,128)(2,1)S(1)} %collective-permute-done.10.refs_3_), channel_id=1, source_target_pairs={{0,4},{1,5},{2,6},{3,7},{4,8},{5,9},{6,10},{7,11},{8,12},{9,13},{1... | collective-permute-start | bytes 1179656 | tf_op jit(solution)/shard_map/ppermute | solution.py:372
  77.7 11.3 %collective-permute-start.16 = (bf16[8,3,64,128]{3,2,1,0:T(8,128)(2,1)S(1)}, bf16[8,3,64,128]{3,2,1,0:T(8,128)(2,1)S(1)}, u32[]{:S(2)}, u32[]{:S(2)}) collective-permute-start(bf16[8,3,64,128]{3,2,1,0:T(8,128)(2,1)S(1)} %collective-permute-done.10.refs_3_), channel_id=1, source_target_pairs={{0,12},{1,13},{2,14},{3,15},{4,0},{5,1},{6,2},{7,3},{8,4},{9,5},{1... | collective-permute-start | bytes 1179656 | tf_op jit(solution)/shard_map/ppermute | solution.py:372
  89.0 13.8 %collective-permute-start.22 = (bf16[16,3,96,128]{3,2,1,0:T(8,128)(2,1)S(1)}, bf16[16,3,96,128]{3,2,1,0:T(8,128)(2,1)S(1)}, u32[]{:S(2)}, u32[]{:S(2)}) collective-permute-start(bf16[16,3,96,128]{3,2,1,0:T(8,128)(2,1)S(1)} %pad_maximum_fusion), channel_id=1, source_target_pairs={{0,16},{16,0},{32,48},{48,32},{64,80},{80,64},{96,112},{112,96},{1... | collective-permute-start | bytes 3538952 | tf_op jit(solution)/shard_map/ppermute | solution.py:372
  90.4 12.3 %collective-permute-start.21 = (bf16[8,3,64,128]{3,2,1,0:T(8,128)(2,1)S(1)}, bf16[8,3,64,128]{3,2,1,0:T(8,128)(2,1)S(1)}, u32[]{:S(2)}, u32[]{:S(2)}) collective-permute-start(bf16[8,3,64,128]{3,2,1,0:T(8,128)(2,1)S(1)} %collective-permute-done.15.refs_10_.refs_11_), channel_id=1, source_target_pairs={{0,4},{1,5},{2,6},{3,7},{4,8},{5,9},{6,10},{7,11},{8,12},{9,13},{1... | collective-permute-start | bytes 1179656 | tf_op jit(solution)/shard_map/ppermute | solution.py:372
  90.4 12.3 %collective-permute-start.20 = (bf16[8,3,64,128]{3,2,1,0:T(8,128)(2,1)S(1)}, bf16[8,3,64,128]{3,2,1,0:T(8,128)(2,1)S(1)}, u32[]{:S(2)}, u32[]{:S(2)}) collective-permute-start(bf16[8,3,64,128]{3,2,1,0:T(8,128)(2,1)S(1)} %collective-permute-done.4.refs_5_), channel_id=1, source_target_pairs={{0,12},{1,13},{2,14},{3,15},{4,0},{5,1},{6,2},{7,3},{8,4},{9,5},{1... | collective-permute-start | bytes 1179656 | tf_op jit(solution)/shard_map/ppermute | solution.py:372
